TPU v7x, 32 devices: a whole 2x2x4 slice. The times are simulated.
32 devices in a mesh: dp: 4 (over y, core), tile: 8 (over z, x).
Axes of the slice: x: 2, y: 2, z: 4, core: 2. Of those that a mesh axis runs over, the one named last changes fastest.
Arguments:
- inputs: bfloat16 [8, 64, 128, 256], P('dp', None, 'tile'), may hold values from -6 to 6
- cotangent: bfloat16 [8, 64, 128, 256], P('dp', None, 'tile'), may hold values from -6 to 6
- mode_weight: bfloat16 [64, 64, 64, 128], P('tile'), may hold values from -0.5 to 0.5
- local_weight: bfloat16 [64, 64], replicated, may hold values from -0.75 to 0.75
Outputs:
- input_grad: bfloat16 [8, 64, 128, 256], P('dp', None, 'tile')
- mode_grad: float32 [64, 64, 64, 128], P('tile')
- local_grad: float32 [64, 64], replicated
All inputs are finite; a program needn't handle non-finite values.
Results may differ from a plain program's by a relative error of at most 0.015.
Values may be sent and summed in bfloat16 or wider, within the bound.
No kernel may reach another device: no remote copies, remote signals or barrier semaphores. Data moves between devices by JAX's collectives and lax.ppermute only.
A program may use at most 128 MiB of HBM per device.

v0:
```python
import functools
import math

import jax
import jax.numpy as jnp
import numpy as np
from jax import lax
from jax.experimental import pallas as pl
from jax.experimental.pallas import tpu as pltpu
from jax.sharding import PartitionSpec as P

F32 = jnp.float32
BF16 = jnp.bfloat16
LIMIT = 56 * 1024 * 1024
SMALL = 24 * 1024 * 1024
ROWS = 8
PACK = 16
GROUP = 8
SPLIT = 4
AHEAD = 3


def row_tables(height, modes):
    index = np.arange(modes)
    signed = np.where(index < modes // 2, index, index - modes)
    phases = np.mod(np.arange(height)[:, None] * signed[None, :], height)
    angles = phases * (2.0 * math.pi / height)
    return np.cos(angles), np.sin(angles)


def column_tables(width, modes):
    phases = np.mod(np.arange(modes)[:, None] * np.arange(width)[None, :], width)
    angles = phases * (2.0 * math.pi / width)
    return np.stack([np.cos(angles), -np.sin(angles)])


def constant(table):
    return jnp.asarray(np.asarray(table, np.float32)).astype(BF16)


def tables(tiles, owned, th, width, modes):
    cols = column_tables(width, tiles * owned)
    split = cols.reshape(2, tiles, owned, width)
    send_cols = split.transpose(1, 0, 2, 3).reshape(tiles, 2 * owned, width)
    send_cols = np.pad(send_cols, ((0, 0), (0, padded(2 * owned) - 2 * owned), (0, 0))).reshape(-1, width)
    back_cols = split.transpose(2, 1, 0, 3).reshape(-1, width)
    cosine, sine = row_tables(th * tiles, modes)
    real = np.concatenate([cosine, -sine], axis=1)
    imag = np.concatenate([sine, cosine], axis=1)
    pair = np.stack([real, imag]).reshape(2, tiles, th, 2 * modes)
    rows = pair.transpose(2, 1, 0, 3).reshape(-1, 2 * modes)
    back_rows = pair.transpose(1, 0, 2, 3).reshape(-1, 2 * modes)
    return constant(send_cols), constant(rows), constant(back_rows), constant(back_cols)


def padded(rows):
    return -(-rows // PACK) * PACK


def order(outer, inner):
    take = np.arange(outer * inner).reshape(outer, inner).T.reshape(-1)
    return constant(np.eye(outer * inner)[take])


def mode_order(tiles, owned):
    rows = np.arange(tiles * padded(2 * owned)).reshape(tiles, -1)
    take = rows[:, : 2 * owned].reshape(tiles, 2, owned).transpose(2, 0, 1).reshape(-1)
    return constant(np.eye(rows.size)[take])


def dot(left, right, dims):
    return lax.dot_general(left, right, (dims, ((), ())), preferred_element_type=F32)


def low_half(shape, half):
    return lax.broadcasted_iota(jnp.int32, shape, 1) < half


def gelu_slope(values):
    size = jnp.abs(values)
    expo = jnp.exp(-0.5 * values * values)
    t = 1.0 / (1.0 + (0.3275911 / math.sqrt(2.0)) * size)
    poly = 0.5 * 1.061405429
    for factor in (-1.453152027, 1.421413741, -0.284496736, 0.254829592):
        poly = poly * t + 0.5 * factor
    tail = poly * t * expo
    cumulative = jnp.where(values < 0.0, tail, 1.0 - tail)
    return cumulative + values * expo * (1.0 / math.sqrt(2.0 * math.pi))


def shuffle(order_ref, value):
    return dot(order_ref[...], value, ((1,), (0,))).astype(BF16)


def by_rows(order_ref, field_refs, rows_ref):
    heights, lanes, _ = rows_ref.shape
    block = PACK * heights
    quarter = lanes // len(field_refs)
    for first in range(0, lanes, PACK):
        start = first % quarter * heights
        moved = shuffle(order_ref, field_refs[first // quarter][start : start + block, :])
        for h in range(heights):
            rows_ref[h, first : first + PACK, :] = moved[h * PACK : (h + 1) * PACK]


def columns_kernel(order_ref, table_ref, *rest):
    field_refs, (rows_ref, send_ref) = rest[:SPLIT], rest[SPLIT:]
    heights, lanes, _ = rows_ref.shape
    by_rows(order_ref, field_refs, rows_ref)
    for h in range(heights):
        send_ref[:, h * lanes : (h + 1) * lanes] = dot(table_ref[...], rows_ref[h], ((1,), (1,))).astype(BF16)


def relayout_kernel(order_ref, *rest):
    by_rows(order_ref, rest[:SPLIT], rest[SPLIT])


def shuffle_groups(order_ref, recv_ref, width):
    size = order_ref.shape[0]
    return [shuffle(order_ref, recv_ref[n : n + size, :width]) for n in range(0, recv_ref.shape[0], size)]


def stack(groups, index, count, lanes):
    return jnp.concatenate(
        [
            group[index * count : (index + 1) * count, n : n + lanes]
            for n in range(0, groups[0].shape[1], lanes)
            for group in groups
        ],
        axis=0,
    )


def spectra_into(scale, owned, lanes, recv_ref, order_ref, rows_ref, spec_ref):
    count = order_ref.shape[0] // owned
    fields = rows_ref.shape[0] // count * lanes
    ordered = [shuffle(order_ref, recv_ref[:, :fields])]
    for q in range(owned):
        stacked = stack(ordered, q, count, lanes)
        spec_ref[q * lanes : (q + 1) * lanes, :] = (
            scale * dot(stacked, rows_ref[...], ((0,), (0,)))
        ).astype(BF16)


def to_piece(value, rows):
    return jnp.concatenate([value[n : n + rows] for n in range(0, value.shape[0], rows)], axis=1)


def from_piece(value, extent):
    return jnp.concatenate([value[:, n : n + extent] for n in range(0, value.shape[1], extent)], axis=0)


def spectra_kernel(scale, owned, lanes, recv_ref, order_ref, rows_ref, spec_ref):
    spectra_into(scale, owned, lanes, recv_ref, order_ref, rows_ref, spec_ref)


def running(pairs):
    waiting = []
    for left, right in pairs:
        value, level = left * right, 0
        while waiting and waiting[-1][1] == level:
            value, level = waiting.pop()[0] + value, level + 1
        waiting.append((value, level))
    return sum((value for value, _ in reversed(waiting[:-1])), waiting[-1][0])


def rows_of(store, block, extent):
    return store.at[pl.ds(pl.multiple_of(block * extent, extent), extent), :]


def packed_row(view, index):
    row = view[index : index + 1, :]
    return jnp.broadcast_to(row, (PACK, row.shape[1])).astype(BF16)


def duplicates(spec, half):
    value = spec.astype(F32)
    other = pltpu.roll(value, half, 1)
    low = low_half(value.shape, half)
    return jnp.where(low, value, other), jnp.where(low, other, value)


def finish(back_ref, sums, send_ref, stage, sems, mix):
    @pl.when(pl.program_id(0) == pl.num_programs(0) - 1)
    def _():
        moves = []
        for q in range(sums.shape[0]):
            mixed = mix(sums.at[q]).astype(BF16)
            column = pl.ds(q * mixed.shape[0], mixed.shape[0])
            stage[:, column] = dot(back_ref[...], mixed, ((1,), (1,))).astype(BF16)
            moves.append(pltpu.make_async_copy(stage.at[:, column], send_ref.at[:, column], sems.at[q]))
            moves[-1].start()
        for move in moves:
            move.wait()


def fetch(sources, targets, sems):
    moves = [
        pltpu.make_async_copy(source, target, sems.at[n]) for n, (source, target) in enumerate(zip(sources, targets))
    ]

    @pl.when(pl.program_id(0) == 0)
    def _():
        for move in moves:
            move.start()

    return moves


def fetch_weights(moves, source_ref, weights, sems):
    q = pl.program_id(0)
    owned = sems.shape[0]
    size = weights.shape[0] // owned

    def move(mode):
        part = pl.ds(pl.multiple_of(mode * size, size), size)
        return pltpu.make_async_copy(source_ref.at[part, :], weights.at[part, :], sems.at[mode])

    @pl.when(q == 0)
    def _():
        move(0).start()
        for early in moves:
            early.wait()
        for mode in range(1, min(AHEAD, owned)):
            move(mode).start()

    @pl.when(q + AHEAD < owned)
    def _():
        move(q + AHEAD).start()

    return move(q), weights.at[pl.ds(pl.multiple_of(q * size, size), size), :]


def forward_kernel(scale, samples, owned, *rest):
    sources, source_ref, spec_ref, send_ref, real, imag, sums, weights, sems = rest[:4], *rest[4:12]
    targets, early, stage, late = rest[12:16], *rest[16:19]
    recv_ref, order_ref, rows_ref, back_ref = targets
    _, _, outs, both = sums.shape
    channels = weights.shape[0] // outs // owned
    half = both // 2
    lanes = samples * channels
    q = pl.program_id(0)
    moves = fetch(sources, targets, early)
    coming, weight_ref = fetch_weights(moves, source_ref, weights, sems)

    @pl.when(q == 0)
    def _():
        spectra_into(scale, owned, lanes, recv_ref, order_ref, rows_ref, spec_ref)
        real[...], imag[...] = duplicates(spec_ref[...], half)
        sums[...] = jnp.zeros_like(sums)

    coming.wait()

    def body(block, carry):
        view = rows_of(weight_ref, block, GROUP * outs)
        into = sums.at[q]
        for s in range(samples):
            rows = []
            for store in (real, imag):
                part = rows_of(store, (q * lanes + s * channels) // GROUP + block, GROUP)
                rows.append([packed_row(part, step) for step in range(GROUP)])
            for o in range(0, outs, PACK):
                column = [view[step * outs + o : step * outs + o + PACK, :] for step in range(GROUP)]
                for n, row in enumerate(rows):
                    into[2 * s + n, o : o + PACK, :] += running([(w, r) for w, r in zip(column, row)]).astype(F32)
        return carry

    lax.fori_loop(0, channels // GROUP, body, 0)

    def mix(parts):
        low = low_half((outs, both), half)
        result = []
        for s in range(samples):
            crossed = pltpu.roll(parts[2 * s + 1], half, 1)
            result.append(parts[2 * s] + jnp.where(low, -crossed, crossed))
        return jnp.concatenate(result, axis=0)

    finish(back_ref, sums, send_ref, stage, late, mix)


def backward_kernel(samples, tiles, *rest):
    sources, source_ref, send_ref, real, imag, sums, weights, sems = rest[:3], *rest[3:10]
    targets, early, stage, late = rest[10:13], *rest[13:16]
    spec_ref, back_ref, local_ref = targets

    def carried():
        column = pl.ds(sums.shape[0] * lanes, stage.shape[1] - sums.shape[0] * lanes)
        return pltpu.make_async_copy(stage.at[:, column], send_ref.at[:, column], late.at[0])

    channels, both = sums.shape[2] // ROWS, sums.shape[3]
    outs = weights.shape[0] // channels // sums.shape[0]
    half = both // 2
    lanes = samples * outs
    q = pl.program_id(0)
    moves = fetch(sources, targets, early)
    coming, weight_ref = fetch_weights(moves, source_ref, weights, sems)

    @pl.when(q == 0)
    def _():
        first, second = duplicates(spec_ref[...], half)
        real[...], imag[...] = first.astype(BF16), second.astype(BF16)
        extent = stage.shape[0] // tiles
        partial = to_piece(local_ref[...].astype(BF16), extent)
        for n in range(0, stage.shape[0], extent):
            stage[n : n + extent, sums.shape[0] * lanes :] = partial
        move = carried()
        move.start()
        move.wait()

    coming.wait()
    grads = [
        [store[pl.ds(pl.multiple_of(q * lanes + s * outs + o, PACK), PACK), :] for o in range(0, outs, PACK)]
        for s in range(samples)
        for store in (real, imag)
    ]

    def body(block, carry):
        view = rows_of(weight_ref, block, GROUP * outs)
        into = [rows_of(sums.at[q, n], block, GROUP * ROWS) for n in range(len(grads))]
        for first in range(0, GROUP, 4):
            totals = []
            for step in range(first, first + 4):
                column = [view[step * outs + o : step * outs + o + PACK, :] for o in range(0, outs, PACK)]
                for n, grad in enumerate(grads):
                    total = running([(w, g) for w, g in zip(column, grad)]).astype(F32)
                    totals.append((n, step, total[:ROWS] + total[ROWS:]))
            for n, step, total in totals:
                into[n][step * ROWS : (step + 1) * ROWS, :] = total
        return carry

    lax.fori_loop(0, channels // GROUP, body, 0)

    def mix(parts):
        low = low_half((channels, both), half)
        result = []
        for s in range(samples):
            straight, crossed = (
                sum(parts[n, pl.ds(row, channels, stride=ROWS), :] for row in range(ROWS)) for n in (2 * s, 2 * s + 1)
            )
            result.append(jnp.where(low, straight, -straight) + pltpu.roll(crossed, half, 1))
        return jnp.concatenate(result, axis=0)

    finish(back_ref, sums, send_ref, stage, late, mix)


def pixels_kernel(scale, heights, recv_ref, order_ref, back_ref, local_ref, field_ref, cot_ref, table_ref, *rest):
    grad_ref, send_ref, sum_ref, ordered, total = rest
    steps, lanes, _ = field_ref.shape
    count = order_ref.shape[0] // heights
    size = order_ref.shape[0]
    group = pl.program_id(0)

    @pl.when(group == 0)
    def _():
        for n in range(0, recv_ref.shape[0], size):
            ordered[n : n + size, :] = shuffle(order_ref, recv_ref[n : n + size, :])
        total[...] = jnp.zeros_like(total)

    local = jnp.zeros(total.shape, F32)
    for step in range(steps):
        parts = []
        for n in range(0, recv_ref.shape[0], size):
            first = pl.multiple_of(n + (group * steps + step) * count, count)
            parts.append(ordered[pl.ds(first, count), :])
        inner = stack(parts, 0, count, lanes)
        pre = scale * dot(inner, back_ref[...], ((0,), (0,)))
        pre = pre + dot(local_ref[...], field_ref[step], ((1,), (0,)))
        grad = (cot_ref[step].astype(F32) * gelu_slope(pre)).astype(BF16)
        grad_ref[step] = grad
        send_ref[:, step * lanes : (step + 1) * lanes] = dot(table_ref[...], grad, ((1,), (1,))).astype(BF16)
        local = local + dot(field_ref[step], grad, ((1,), (1,)))
    total[...] += local

    @pl.when(group == pl.num_programs(0) - 1)
    def _():
        extent = sum_ref.shape[0]
        sum_ref[...] = sum(total[n : n + extent, n : n + extent] for n in range(0, lanes, extent))


def final_kernel(scale, tiles, recv_ref, order_ref, back_ref, local_ref, grad_ref, restore_ref, *rest):
    out_ref, sum_ref, result = rest
    heights, lanes, _ = grad_ref.shape
    extent = recv_ref.shape[0] // tiles
    first = back_ref.shape[0] // (2 * tiles) * lanes
    partials = sum(recv_ref[n : n + extent, first:].astype(F32) for n in range(0, recv_ref.shape[0], extent))
    sum_ref[...] = from_piece(partials, sum_ref.shape[1])
    count = order_ref.shape[0] // heights
    ordered = shuffle_groups(order_ref, recv_ref, first)
    for h in range(heights):
        inner = stack(ordered, h, count, lanes)
        value = scale * dot(inner, back_ref[...], ((0,), (0,)))
        result[h] = (value + dot(local_ref[...], grad_ref[h], ((1,), (0,)))).astype(BF16)
    block = PACK * heights
    for first in range(0, lanes, PACK):
        part = jnp.concatenate([result[h, first : first + PACK, :] for h in range(heights)], axis=0)
        out_ref[first * heights : first * heights + block, :] = shuffle(restore_ref, part)


def outer_kernel(samples, groups, *refs):
    specs, grads = refs[:groups], refs[groups : 2 * groups]
    out_ref, real, imag, crossed = refs[2 * groups :]
    total, channels, both = real.shape
    outs = crossed.shape[1]
    half = both // 2
    low = low_half((channels, both), half)

    for g in range(groups):
        for s in range(samples):
            n = g * samples + s
            spec = specs[g][s * channels : (s + 1) * channels, :].astype(F32)
            other = pltpu.roll(spec, half, 1)
            real[n] = jnp.where(low, spec, other)
            imag[n] = jnp.where(low, other, -spec)
            grad = grads[g][s * outs : (s + 1) * outs, :]
            crossed[n] = pltpu.roll(grad.astype(F32), half, 1).astype(BF16)

    def body(block, carry):
        into = rows_of(out_ref, block, GROUP * outs)
        views = [rows_of(store.at[n], block, GROUP) for n in range(total) for store in (real, imag)]
        for first in range(0, GROUP, 2):
            pair = range(first, first + 2)
            lefts = [[packed_row(view, c) for view in views] for c in pair]
            for o in range(0, outs, PACK):
                right = []
                for n in range(total):
                    at = n % samples * outs + o
                    right += [grads[n // samples][at : at + PACK, :], crossed[n, o : o + PACK, :]]
                results = [running(list(zip(left, right))) for left in lefts]
                for c, result in zip(pair, results):
                    into[c * outs + o : c * outs + o + PACK, :] = result.astype(F32)
        return carry

    lax.fori_loop(0, channels // GROUP, body, 0)


def whole(extent):
    return pl.BlockSpec(extent, lambda *_: (0,) * len(extent))


def call(kernel, name, operands, outs, scratch=(), grid=(1,), blocks=None, out_blocks=None, limit=LIMIT):
    blocks, out_blocks = blocks or {}, out_blocks or {}
    in_specs = [blocks.get(n) or whole(operand.shape) for n, operand in enumerate(operands)]
    out_specs = [out_blocks.get(n, whole(out.shape)) for n, out in enumerate(outs)]
    return pl.pallas_call(
        kernel,
        out_shape=tuple(outs),
        grid=grid,
        in_specs=in_specs,
        out_specs=tuple(out_specs),
        scratch_shapes=list(scratch),
        compiler_params=pltpu.CompilerParams(vmem_limit_bytes=limit),
        name=name,
    )(*operands)


def swap(values, axis, step):
    return lax.ppermute(values, axis, [(i, i ^ step) for i in range(lax.axis_size(axis))])


def gather_near(values, axis):
    size = lax.axis_size(axis)
    return {0: values} | {1 << bit: swap(values, axis, 1 << bit) for bit in range(size.bit_length() - 1)}


def gather_far(near, axis):
    whole_set = dict(near)
    for step in range(1, lax.axis_size(axis)):
        if step not in whole_set:
            whole_set[step] = swap(whole_set[step & (step - 1)], axis, step & -step)
    return [whole_set[step] for step in sorted(whole_set)]


def sum_over(values, axis):
    step = 1
    while step < lax.axis_size(axis):
        values = values + swap(values, axis, step)
        step *= 2
    return values


def block_diagonal(matrix, copies):
    zero = jnp.zeros_like(matrix)
    return jnp.concatenate(
        [
            jnp.concatenate([matrix if i == j else zero for j in range(copies)], axis=1)
            for i in range(copies)
        ],
        axis=0,
    )


def shape(extent, kind=BF16):
    return jax.ShapeDtypeStruct(extent, kind)


def local(inputs, cotangent, mode_weight, local_weight):
    tiles = lax.axis_size("tile")
    samples, channels, th, width = inputs.shape
    owned, _, _, both = mode_weight.shape
    modes = both // 2
    lanes = samples * channels
    parts = width // 128
    spec_scale = 1.0 / math.sqrt(tiles * th * width)
    mode_scale = 1.0 / math.sqrt(modes * tiles * owned)
    send_cols, rows, back_rows, back_cols = tables(tiles, owned, th, width, modes)
    pixel_rows = samples * channels * th
    halves = tiles * padded(2 * owned)
    inverse = 2 * tiles * th

    def exchange(values):
        split = values.reshape(tiles, values.shape[0] // tiles, values.shape[1])
        moved = lax.all_to_all(split, "tile", split_axis=0, concat_axis=0, tiled=False)
        return moved.reshape(values.shape)

    forward_mix = block_diagonal(local_weight.T, samples)
    backward_mix = block_diagonal(local_weight, samples)
    by_row = order(PACK, th)
    by_channel = order(th, PACK)
    by_mode = mode_order(tiles, owned)
    by_height = order(2 * min(tiles, 8), th)
    flat_weight = mode_weight.reshape(-1, both)
    weight_block = pl.BlockSpec((flat_weight.shape[0] // owned, both), lambda q: (q, 0))
    weight_scratch = [pltpu.VMEM(flat_weight.shape, BF16), pltpu.SemaphoreType.DMA((owned,))]
    in_place = pl.BlockSpec(memory_space=pl.ANY)
    to_modes = shape((halves, th * lanes))
    to_pixels = shape((inverse, owned * lanes))
    field_shape = shape((th, lanes, width))

    def kept(*operands):
        return [pltpu.VMEM(operand.shape, operand.dtype) for operand in operands]

    def early(*operands):
        return kept(*operands) + [pltpu.SemaphoreType.DMA((len(operands),))]

    def field_blocks(first):
        return {first + n: pl.BlockSpec((pixel_rows // SPLIT, width), lambda _, n=n: (n, 0)) for n in range(SPLIT)}

    field_rows, send = call(
        columns_kernel,
        "columns",
        (by_row, send_cols, *[inputs.reshape(pixel_rows, width)] * SPLIT),
        (field_shape, to_modes),
        blocks=field_blocks(2),
    )
    arrived = exchange(send)
    (cot_rows,) = call(
        relayout_kernel,
        "relayout",
        (by_row, *[cotangent.reshape(pixel_rows, width)] * SPLIT),
        (field_shape,),
        blocks=field_blocks(1),
    )
    spectra, send = call(
        functools.partial(forward_kernel, spec_scale, samples, owned),
        "mix_forward",
        (arrived, by_mode, rows, back_rows, flat_weight),
        (shape((owned * lanes, both)), to_pixels),
        [
            pltpu.VMEM((owned * lanes, both), F32),
            pltpu.VMEM((owned * lanes, both), F32),
            pltpu.VMEM((owned, 2 * samples, channels, both), F32),
            *weight_scratch,
            *early(arrived, by_mode, rows, back_rows),
            pltpu.VMEM((inverse, owned * lanes), BF16),
            pltpu.SemaphoreType.DMA((owned,)),
        ],
        grid=(owned,),
        blocks={n: in_place for n in range(5)},
        out_blocks={1: in_place},
    )
    all_spectra = gather_far(gather_near(spectra, "dp"), "dp")
    arrived = exchange(send)
    steps = 4
    row_block = pl.BlockSpec((steps, lanes, width), lambda n: (n, 0, 0))
    gate_rows, send, local_sum = call(
        functools.partial(pixels_kernel, mode_scale, th),
        "pixels",
        (arrived, by_height, back_cols, forward_mix, field_rows, cot_rows, send_cols),
        (field_shape, to_modes, shape((channels, channels), F32)),
        [pltpu.VMEM((inverse, owned * lanes), BF16), pltpu.VMEM((lanes, lanes), F32)],
        grid=(th // steps,),
        blocks={4: row_block, 5: row_block},
        out_blocks={0: row_block, 1: pl.BlockSpec((halves, steps * lanes), lambda n: (0, n))},
        limit=SMALL,
    )
    send, *all_spectra = lax.optimization_barrier((send, *all_spectra))
    arrived, local_sum = lax.optimization_barrier((exchange(send), sum_over(local_sum, "dp")))
    (grad_spectra,) = call(
        functools.partial(spectra_kernel, mode_scale, owned, lanes),
        "grad_spectra",
        (arrived, by_mode, rows),
        (shape((owned * lanes, both)),),
        limit=SMALL,
    )
    near = gather_near(grad_spectra, "dp")
    carried = channels * channels * tiles // inverse
    (send,) = call(
        functools.partial(backward_kernel, samples, tiles),
        "mix_backward",
        (grad_spectra, back_rows, local_sum, flat_weight),
        (shape((inverse, owned * lanes + carried)),),
        [
            pltpu.VMEM((owned * lanes, both), BF16),
            pltpu.VMEM((owned * lanes, both), BF16),
            pltpu.VMEM((owned, 2 * samples, channels * ROWS, both), F32),
            *weight_scratch,
            *early(grad_spectra, back_rows, local_sum),
            pltpu.VMEM((inverse, owned * lanes + carried), BF16),
            pltpu.SemaphoreType.DMA((owned,)),
        ],
        grid=(owned,),
        blocks={n: in_place for n in range(4)},
        out_blocks={0: in_place},
    )
    send, near = lax.optimization_barrier((send, near))
    all_grads = gather_far(near, "dp")
    arrived = exchange(send)

    groups = lax.axis_size("dp")
    total = groups * samples
    per_mode = pl.BlockSpec((lanes, both), lambda q: (q, 0))
    (mode_grad,) = call(
        functools.partial(outer_kernel, samples, groups),
        "mode_grad",
        (*all_spectra, *all_grads),
        (shape(flat_weight.shape, F32),),
        [pltpu.VMEM((total, channels, both), F32)] * 2 + [pltpu.VMEM((total, channels, both), BF16)],
        grid=(owned,),
        blocks={n: per_mode for n in range(2 * groups)},
        out_blocks={0: weight_block},
    )
    arrived, mode_grad = lax.optimization_barrier((arrived, mode_grad))

    input_grad, local_grad = call(
        functools.partial(final_kernel, spec_scale, tiles),
        "final",
        (arrived, by_height, back_cols, backward_mix, gate_rows, by_channel),
        (shape((pixel_rows, width)), shape((channels, channels), F32)),
        [pltpu.VMEM((th, lanes, width), BF16)],
        limit=SMALL,
    )
    return (input_grad.reshape(inputs.shape), mode_grad.reshape(mode_weight.shape), local_grad)


def solution(mesh):
    return jax.shard_map(
        local,
        mesh=mesh,
        in_specs=(
            P("dp", None, "tile", None),
            P("dp", None, "tile", None),
            P("tile", None, None, None),
            P(),
        ),
        out_specs=(P("dp", None, "tile", None), P("tile", None, None, None), P()),
        check_vma=False,
    )
```

profile of v0, /device:TPU:0, one launch (start us, length us, event | category | flops | bytes accessed | tf_op | source)
XLA Modules:
  0.0 115.8 jit_solution(12176827076554264)
XLA Ops:
  0.6 0.0 copy-start.1
  0.6 0.0 copy-start.5
  0.7 0.0 copy-start.7
  0.7 0.0 copy-start.4
  0.7 0.0 copy-start.6
  0.7 3.0 %columns.1 = (bf16[16,128,256]{2,1,0:T(8,128)(2,1)}, bf16[128,2048]{1,0:T(8,128)(2,1)}) custom-call(bf16[256,256]{1,0:T(8,128)(2,1)} %constant.30.order_ref.restore_ref, bf16[128,256]{1,0:T(8,128)(2,1)} %constant.31.table_ref, bf16[2048,256]{1,0:T(8,128)(2,1)} %bitcast.20, bf16[2048,256]{1,0:T(8,128)(2,1)} %bitcast.21, bf16[2048,256]{1,0:T(8,128)(2,1)} %bitcast.22, ...), custom_call_target="tpu_custom_call" | custom-call | tf_op jit(solution)/shard_map/columns/pallas_call | solution.py:444
  3.7 22.0 %all_to_all.20 = bf16[8,16,2048]{2,1,0:T(8,128)(2,1)} all-to-all(bf16[8,16,2048]{2,1,0:T(8,128)(2,1)} %bitcast.31), channel_id=1, replica_groups=mesh['dp'=4,'tile'=8] {'tile'}, dimensions={0} | all-to-all | bytes 1048576 | tf_op jit(solution)/shard_map/all_to_all | solution.py:512
  25.7 9.8 %mix_forward.1 = (bf16[1024,128]{1,0:T(8,128)(2,1)}, bf16[256,1024]{1,0:T(8,128)(2,1)}) custom-call(bf16[128,2048]{1,0:T(8,128)(2,1)} %bitcast.29, bf16[128,128]{1,0:T(8,128)(2,1)} %constant.32.rest_1_.order_ref, bf16[256,128]{1,0:T(8,128)(2,1)} %constant.33.rest_2_.rows_ref, bf16[256,128]{1,0:T(8,128)(2,1)} %constant.34.rest_3_.rest_1_, ...), custom_call_target="tpu_custom_call" | custom-call | tf_op jit(solution)/shard_map/mix_forward/pallas_call | solution.py:444
  35.5 3.6 %all-to-all-start.1 = ((bf16[8,32,1024]{2,1,0:T(8,128)(2,1)}), bf16[8,32,1024]{2,1,0:T(8,128)(2,1)S(1)}, u32[]{:S(2)}, u32[]{:S(2)}) async-start(bf16[8,32,1024]{2,1,0:T(8,128)(2,1)} %bitcast.30), calls=%async_computation.1 | async-start | bytes 1048576 | tf_op jit(solution)/shard_map/all_to_all | solution.py:512
  39.1 1.5 %collective-permute-start.1 = (bf16[1024,128]{1,0:T(8,128)(2,1)}, bf16[1024,128]{1,0:T(8,128)(2,1)S(1)}, u32[]{:S(2)}, u32[]{:S(2)}) collective-permute-start(bf16[1024,128]{1,0:T(8,128)(2,1)} %get-tuple-element.35.refs_0_), channel_id=1, source_target_pairs={{0,16},{8,24},{16,0},{24,8},{1,17},{9,25},{17,1},{25,9},{2,18},{10... | collective-permute-start | bytes 786440 | tf_op jit(solution)/shard_map/ppermute | solution.py:457
  40.7 0.0 collective-permute-start
  40.7 6.1 %collective-permute-done.1.refs_2_ = bf16[1024,128]{1,0:T(8,128)(2,1)S(1)} collective-permute-done((bf16[1024,128]{1,0:T(8,128)(2,1)}, bf16[1024,128]{1,0:T(8,128)(2,1)S(1)}, u32[]{:S(2)}, u32[]{:S(2)}) %collective-permute-start.1) | collective-permute-done | bytes 262176 | tf_op jit(solution)/shard_map/ppermute | solution.py:457
  46.8 0.0 collective-permute-start.2
  46.8 0.8 copy.15
  47.6 2.6 %relayout.1.cot_ref = bf16[16,128,256]{2,1,0:T(8,128)(2,1)} custom-call(bf16[256,256]{1,0:T(8,128)(2,1)} %constant.30.order_ref.restore_ref, bf16[2048,256]{1,0:T(8,128)(2,1)} %bitcast.24, bf16[2048,256]{1,0:T(8,128)(2,1)} %bitcast.25, bf16[2048,256]{1,0:T(8,128)(2,1)} %bitcast.26, bf16[2048,256]{1,0:T(8,128)(2,1)} %bitcast.27), custom_call_target="tpu_custom_call" | custom-call | tf_op jit(solution)/shard_map/relayout/pallas_call | solution.py:444
  50.2 0.1 fusion.4.local_ref
  50.3 3.0 %all-to-all-done.1 = bf16[8,32,1024]{2,1,0:T(8,128)(2,1)S(1)} async-done(((bf16[8,32,1024]{2,1,0:T(8,128)(2,1)}), bf16[8,32,1024]{2,1,0:T(8,128)(2,1)S(1)}, u32[]{:S(2)}, u32[]{:S(2)}) %all-to-all-start.1) | async-done | bytes 524320 | tf_op jit(solution)/shard_map/all_to_all | solution.py:512
  53.3 0.0 copy-done.1
  53.3 0.0 copy-start
  53.3 1.2 %copy-done = bf16[16,128,256]{2,1,0:T(8,128)(2,1)S(1)} copy-done((bf16[16,128,256]{2,1,0:T(8,128)(2,1)S(1)}, bf16[16,128,256]{2,1,0:T(8,128)(2,1)}, u32[]{:S(2)}) %copy-start) | copy-done | bytes 1048600
  54.6 6.6 %pixels.1 = (bf16[16,128,256]{2,1,0:T(8,128)(2,1)S(1)}, bf16[128,2048]{1,0:T(8,128)(2,1)}, f32[64,64]{1,0:T(8,128)S(1)}) custom-call(bf16[256,1024]{1,0:T(8,128)(2,1)S(1)} %bitcast.16, bf16[256,256]{1,0:T(8,128)(2,1)S(1)} %copy-done.1, bf16[128,256]{1,0:T(8,128)(2,1)S(1)} %copy-done.6, bf16[128,128]{1,0:T(8,128)(2,1)S(1)} %fusion.4.local_ref, ...), custom_call_target="tpu_custom_call" | custom-call | tf_op jit(solution)/shard_map/pixels/pallas_call | solution.py:444
  61.2 0.0 collective-permute-done.refs_1_
  61.2 0.0 collective-permute-done.2.refs_3_
  61.2 3.6 %all-to-all-start.2 = ((bf16[8,16,2048]{2,1,0:T(8,128)(2,1)}), bf16[8,16,2048]{2,1,0:T(8,128)(2,1)S(1)}, u32[]{:S(2)}, u32[]{:S(2)}) async-start(bf16[8,16,2048]{2,1,0:T(8,128)(2,1)} %bitcast.8), calls=%async_computation.2 | async-start | bytes 1048576 | tf_op jit(solution)/shard_map/all_to_all | solution.py:512
  64.9 0.0 collective-permute-start.3
  64.9 1.2 %collective-permute-done.3 = f32[64,64]{1,0:T(8,128)S(1)} collective-permute-done((f32[64,64]{1,0:T(8,128)S(1)}, f32[64,64]{1,0:T(8,128)S(1)}, u32[]{:S(2)}, u32[]{:S(2)}) %collective-permute-start.3) | collective-permute-done | bytes 16416 | tf_op jit(solution)/shard_map/ppermute | solution.py:457
  66.1 1.5 %collective-permute-start.4 = (f32[64,64]{1,0:T(8,128)S(1)}, f32[64,64]{1,0:T(8,128)S(1)}, u32[]{:S(2)}, u32[]{:S(2)}) collective-permute-start(f32[64,64]{1,0:T(8,128)S(1)} %add.14), channel_id=1, source_target_pairs={{0,16},{8,24},{16,0},{24,8},{1,17},{9,25},{17,1},{25,9},{2,18},{10... | collective-permute-start | bytes 49160 | tf_op jit(solution)/shard_map/ppermute | solution.py:457
  67.6 2.4 %collective-permute-done.4 = f32[64,64]{1,0:T(8,128)S(1)} collective-permute-done((f32[64,64]{1,0:T(8,128)S(1)}, f32[64,64]{1,0:T(8,128)S(1)}, u32[]{:S(2)}, u32[]{:S(2)}) %collective-permute-start.4) | collective-permute-done | bytes 16416 | tf_op jit(solution)/shard_map/ppermute | solution.py:457
  70.0 0.6 add.15.rest_2_
  70.6 8.7 %all-to-all-done.2 = bf16[8,16,2048]{2,1,0:T(8,128)(2,1)S(1)} async-done(((bf16[8,16,2048]{2,1,0:T(8,128)(2,1)}), bf16[8,16,2048]{2,1,0:T(8,128)(2,1)S(1)}, u32[]{:S(2)}, u32[]{:S(2)}) %all-to-all-start.2) | async-done | bytes 524320 | tf_op jit(solution)/shard_map/all_to_all | solution.py:512
  79.3 0.0 copy-done.7
  79.3 0.6 grad_spectra.1.rest_0_.refs_4_
  79.9 0.0 copy-start.2
  79.9 0.1 collective-permute-start.5
  80.0 1.6 %collective-permute-start.6 = (bf16[1024,128]{1,0:T(8,128)(2,1)S(1)}, bf16[1024,128]{1,0:T(8,128)(2,1)S(1)}, u32[]{:S(2)}, u32[]{:S(2)}) collective-permute-start(bf16[1024,128]{1,0:T(8,128)(2,1)S(1)} %grad_spectra.1.rest_0_.refs_4_), channel_id=1, source_target_pairs={{0,16},{8,24},{16,0},{24,8},{1,17},{9,25},{17,1},{25,9},{2,18},{10... | collective-permute-start | bytes 786440 | tf_op jit(solution)/shard_map/ppermute | solution.py:457
  81.6 9.2 %mix_backward.1 = bf16[256,1152]{1,0:T(8,128)(2,1)} custom-call(bf16[1024,128]{1,0:T(8,128)(2,1)} %copy-done.2, bf16[256,128]{1,0:T(8,128)(2,1)} %constant.34.rest_3_.rest_1_, f32[64,64]{1,0:T(8,128)} %add.15.rest_2_, bf16[32768,128]{1,0:T(8,128)(2,1)} %bitcast.18), custom_call_target="tpu_custom_call" | custom-call | tf_op jit(solution)/shard_map/mix_backward/pallas_call | solution.py:444
  90.8 0.0 collective-permute-done.5.refs_5_
  90.8 0.0 collective-permute-done.6.refs_6_
  90.8 0.0 copy-start.10
  90.8 3.6 %all-to-all-start.3 = ((bf16[8,32,1152]{2,1,0:T(8,128)(2,1)}), bf16[8,32,1152]{2,1,0:T(8,128)(2,1)S(1)}, u32[]{:S(2)}, u32[]{:S(2)}) async-start(bf16[8,32,1152]{2,1,0:T(8,128)(2,1)} %bitcast.28), calls=%async_computation.3 | async-start | bytes 1179648 | tf_op jit(solution)/shard_map/all_to_all | solution.py:512
  94.5 0.1 collective-permute-start.7
  94.6 0.1 fusion.5.local_ref
  94.7 1.3 %collective-permute-done.7.refs_7_ = bf16[1024,128]{1,0:T(8,128)(2,1)S(1)} collective-permute-done((bf16[1024,128]{1,0:T(8,128)(2,1)S(1)}, bf16[1024,128]{1,0:T(8,128)(2,1)S(1)}, u32[]{:S(2)}, u32[]{:S(2)}) %collective-permute-start.7) | collective-permute-done | bytes 262176 | tf_op jit(solution)/shard_map/ppermute | solution.py:457
  96.0 0.0 copy-start.11
  96.0 0.7 copy-done.11
  96.7 16.7 %mode_grad.1 = f32[32768,128]{1,0:T(8,128)} custom-call(bf16[1024,128]{1,0:T(8,128)(2,1)} %get-tuple-element.35.refs_0_, bf16[1024,128]{1,0:T(8,128)(2,1)} %collective-permute-done.refs_1_, bf16[1024,128]{1,0:T(8,128)(2,1)} %copy-done.8, bf16[1024,128]{1,0:T(8,128)(2,1)} %collective-permute-done.2.refs_3_, bf16[1024,128]{1,0:T(8,128)(2,1)} %copy-done.2, ...), custom_call_target="tpu_custom_call" | custom-call | tf_op jit(solution)/shard_map/mode_grad/pallas_call | solution.py:444
  113.5 0.0 all-to-all-done.3
  113.5 2.3 %final.1 = (bf16[2048,256]{1,0:T(8,128)(2,1)}, f32[64,64]{1,0:T(8,128)}) custom-call(bf16[256,1152]{1,0:T(8,128)(2,1)S(1)} %bitcast.14, bf16[256,256]{1,0:T(8,128)(2,1)S(1)} %copy-done.1, bf16[128,256]{1,0:T(8,128)(2,1)S(1)} %copy-done.6, bf16[128,128]{1,0:T(8,128)(2,1)S(1)} %fusion.5.local_ref, bf16[16,128,256]{2,1,0:T(8,128)(2,1)S(1)} %get-tuple-element.43.grad_ref, ...), custom_call_target="tpu_custom_call" | custom-call | tf_op jit(solution)/shard_map/final/pallas_call | solution.py:444
  (14 shorter events, 0.0 us)
Async XLA Ops:
  0.6 52.7 %copy-start.1 = (bf16[256,256]{1,0:T(8,128)(2,1)S(1)}, bf16[256,256]{1,0:T(8,128)(2,1)}, u32[]{:S(2)}) copy-start(bf16[256,256]{1,0:T(8,128)(2,1)} %constant.30.order_ref.restore_ref) | copy-start | bytes 393220
  0.6 52.7 %copy-start.5 = (bf16[128,256]{1,0:T(8,128)(2,1)S(1)}, bf16[128,256]{1,0:T(8,128)(2,1)}, u32[]{:S(2)}) copy-start(bf16[128,256]{1,0:T(8,128)(2,1)} %constant.31.table_ref) | copy-start | bytes 196612
  0.7 78.6 %copy-start.7 = (bf16[128,128]{1,0:T(8,128)(2,1)S(1)}, bf16[128,128]{1,0:T(8,128)(2,1)}, u32[]{:S(2)}) copy-start(bf16[128,128]{1,0:T(8,128)(2,1)} %constant.32.rest_1_.order_ref) | copy-start | bytes 98308
  0.7 78.6 %copy-start.4 = (bf16[256,128]{1,0:T(8,128)(2,1)S(1)}, bf16[256,128]{1,0:T(8,128)(2,1)}, u32[]{:S(2)}) copy-start(bf16[256,128]{1,0:T(8,128)(2,1)} %constant.33.rest_2_.rows_ref) | copy-start | bytes 196612
  0.7 52.6 %copy-start.6 = (bf16[128,256]{1,0:T(8,128)(2,1)S(1)}, bf16[128,256]{1,0:T(8,128)(2,1)}, u32[]{:S(2)}) copy-start(bf16[128,256]{1,0:T(8,128)(2,1)} %constant.35.back_ref) | copy-start | bytes 196612
  3.6 49.7 %copy-start.3 = (bf16[16,128,256]{2,1,0:T(8,128)(2,1)S(1)}, bf16[16,128,256]{2,1,0:T(8,128)(2,1)}, u32[]{:S(2)}) copy-start(bf16[16,128,256]{2,1,0:T(8,128)(2,1)} %get-tuple-element.27.field_ref) | copy-start | bytes 3145732
  3.7 91.0 %copy-start.12 = (bf16[64,64]{1,0:T(8,128)(2,1)S(1)}, bf16[64,64]{1,0:T(8,128)(2,1)}, u32[]{:S(2)}) copy-start(bf16[64,64]{1,0:T(8,128)(2,1)} %param.15) | copy-start | bytes 24580
  35.5 17.8 %all-to-all-start.1 = ((bf16[8,32,1024]{2,1,0:T(8,128)(2,1)}), bf16[8,32,1024]{2,1,0:T(8,128)(2,1)S(1)}, u32[]{:S(2)}, u32[]{:S(2)}) async-start(bf16[8,32,1024]{2,1,0:T(8,128)(2,1)} %bitcast.30), calls=%async_computation.1 | async-start | bytes 1048576 | tf_op jit(solution)/shard_map/all_to_all | solution.py:512
  39.1 7.6 %collective-permute-start.1 = (bf16[1024,128]{1,0:T(8,128)(2,1)}, bf16[1024,128]{1,0:T(8,128)(2,1)S(1)}, u32[]{:S(2)}, u32[]{:S(2)}) collective-permute-start(bf16[1024,128]{1,0:T(8,128)(2,1)} %get-tuple-element.35.refs_0_), channel_id=1, source_target_pairs={{0,16},{8,24},{16,0},{24,8},{1,17},{9,25},{17,1},{25,9},{2,18},{10... | collective-permute-start | bytes 786440 | tf_op jit(solution)/shard_map/ppermute | solution.py:457
  40.7 20.5 %collective-permute-start = (bf16[1024,128]{1,0:T(8,128)(2,1)}, bf16[1024,128]{1,0:T(8,128)(2,1)}, u32[]{:S(2)}, u32[]{:S(2)}) collective-permute-start(bf16[1024,128]{1,0:T(8,128)(2,1)} %get-tuple-element.35.refs_0_), channel_id=1, source_target_pairs={{0,8},{8,0},{16,24},{24,16},{1,9},{9,1},{17,25},{25,17},{2,10},{10... | collective-permute-start | bytes 786440 | tf_op jit(solution)/shard_map/ppermute | solution.py:457
  46.8 49.3 %copy-start.8 = (bf16[1024,128]{1,0:T(8,128)(2,1)}, bf16[1024,128]{1,0:T(8,128)(2,1)S(1)}, u32[]{:S(2)}) copy-start(bf16[1024,128]{1,0:T(8,128)(2,1)S(1)} %collective-permute-done.1.refs_2_) | copy-start | bytes 786436
  46.8 14.5 %collective-permute-start.2 = (bf16[1024,128]{1,0:T(8,128)(2,1)S(1)}, bf16[1024,128]{1,0:T(8,128)(2,1)}, u32[]{:S(2)}, u32[]{:S(2)}) collective-permute-start(bf16[1024,128]{1,0:T(8,128)(2,1)S(1)} %collective-permute-done.1.refs_2_), channel_id=1, source_target_pairs={{0,8},{8,0},{16,24},{24,16},{1,9},{9,1},{17,25},{25,17},{2,10},{10... | collective-permute-start | bytes 786440 | tf_op jit(solution)/shard_map/ppermute | solution.py:457
  53.3 1.2 %copy-start = (bf16[16,128,256]{2,1,0:T(8,128)(2,1)S(1)}, bf16[16,128,256]{2,1,0:T(8,128)(2,1)}, u32[]{:S(2)}) copy-start(bf16[16,128,256]{2,1,0:T(8,128)(2,1)} %relayout.1.cot_ref) | copy-start | bytes 3145732
  61.2 18.1 %all-to-all-start.2 = ((bf16[8,16,2048]{2,1,0:T(8,128)(2,1)}), bf16[8,16,2048]{2,1,0:T(8,128)(2,1)S(1)}, u32[]{:S(2)}, u32[]{:S(2)}) async-start(bf16[8,16,2048]{2,1,0:T(8,128)(2,1)} %bitcast.8), calls=%async_computation.2 | async-start | bytes 1048576 | tf_op jit(solution)/shard_map/all_to_all | solution.py:512
  64.9 1.2 %collective-permute-start.3 = (f32[64,64]{1,0:T(8,128)S(1)}, f32[64,64]{1,0:T(8,128)S(1)}, u32[]{:S(2)}, u32[]{:S(2)}) collective-permute-start(f32[64,64]{1,0:T(8,128)S(1)} %get-tuple-element.31), channel_id=1, source_target_pairs={{0,8},{8,0},{16,24},{24,16},{1,9},{9,1},{17,25},{25,17},{2,10},{10... | collective-permute-start | bytes 49160 | tf_op jit(solution)/shard_map/ppermute | solution.py:457
  66.1 3.9 %collective-permute-start.4 = (f32[64,64]{1,0:T(8,128)S(1)}, f32[64,64]{1,0:T(8,128)S(1)}, u32[]{:S(2)}, u32[]{:S(2)}) collective-permute-start(f32[64,64]{1,0:T(8,128)S(1)} %add.14), channel_id=1, source_target_pairs={{0,16},{8,24},{16,0},{24,8},{1,17},{9,25},{17,1},{25,9},{2,18},{10... | collective-permute-start | bytes 49160 | tf_op jit(solution)/shard_map/ppermute | solution.py:457
  79.9 1.7 %copy-start.2 = (bf16[1024,128]{1,0:T(8,128)(2,1)}, bf16[1024,128]{1,0:T(8,128)(2,1)S(1)}, u32[]{:S(2)}) copy-start(bf16[1024,128]{1,0:T(8,128)(2,1)S(1)} %grad_spectra.1.rest_0_.refs_4_) | copy-start | bytes 786436
  79.9 10.9 %collective-permute-start.5 = (bf16[1024,128]{1,0:T(8,128)(2,1)S(1)}, bf16[1024,128]{1,0:T(8,128)(2,1)S(1)}, u32[]{:S(2)}, u32[]{:S(2)}) collective-permute-start(bf16[1024,128]{1,0:T(8,128)(2,1)S(1)} %grad_spectra.1.rest_0_.refs_4_), channel_id=1, source_target_pairs={{0,8},{8,0},{16,24},{24,16},{1,9},{9,1},{17,25},{25,17},{2,10},{10... | collective-permute-start | bytes 786440 | tf_op jit(solution)/shard_map/ppermute | solution.py:457
  80.0 10.8 %collective-permute-start.6 = (bf16[1024,128]{1,0:T(8,128)(2,1)S(1)}, bf16[1024,128]{1,0:T(8,128)(2,1)S(1)}, u32[]{:S(2)}, u32[]{:S(2)}) collective-permute-start(bf16[1024,128]{1,0:T(8,128)(2,1)S(1)} %grad_spectra.1.rest_0_.refs_4_), channel_id=1, source_target_pairs={{0,16},{8,24},{16,0},{24,8},{1,17},{9,25},{17,1},{25,9},{2,18},{10... | collective-permute-start | bytes 786440 | tf_op jit(solution)/shard_map/ppermute | solution.py:457
  90.8 5.2 %copy-start.9 = (bf16[1024,128]{1,0:T(8,128)(2,1)}, bf16[1024,128]{1,0:T(8,128)(2,1)S(1)}, u32[]{:S(2)}) copy-start(bf16[1024,128]{1,0:T(8,128)(2,1)S(1)} %collective-permute-done.5.refs_5_) | copy-start | bytes 786436
  90.8 5.2 %copy-start.10 = (bf16[1024,128]{1,0:T(8,128)(2,1)}, bf16[1024,128]{1,0:T(8,128)(2,1)S(1)}, u32[]{:S(2)}) copy-start(bf16[1024,128]{1,0:T(8,128)(2,1)S(1)} %collective-permute-done.6.refs_6_) | copy-start | bytes 786436
  90.8 22.7 %all-to-all-start.3 = ((bf16[8,32,1152]{2,1,0:T(8,128)(2,1)}), bf16[8,32,1152]{2,1,0:T(8,128)(2,1)S(1)}, u32[]{:S(2)}, u32[]{:S(2)}) async-start(bf16[8,32,1152]{2,1,0:T(8,128)(2,1)} %bitcast.28), calls=%async_computation.3 | async-start | bytes 1179648 | tf_op jit(solution)/shard_map/all_to_all | solution.py:512
  94.5 1.6 %collective-permute-start.7 = (bf16[1024,128]{1,0:T(8,128)(2,1)S(1)}, bf16[1024,128]{1,0:T(8,128)(2,1)S(1)}, u32[]{:S(2)}, u32[]{:S(2)}) collective-permute-start(bf16[1024,128]{1,0:T(8,128)(2,1)S(1)} %collective-permute-done.6.refs_6_), channel_id=1, source_target_pairs={{0,8},{8,0},{16,24},{24,16},{1,9},{9,1},{17,25},{25,17},{2,10},{10... | collective-permute-start | bytes 786440 | tf_op jit(solution)/shard_map/ppermute | solution.py:457
  96.0 0.7 copy-start.11
where the time goes:
time: 117 us; the launch traced here: 116 us
  Pallas kernels  50.9 us (44%)
  waiting for transfers between devices  22.7 us (19%)
  blocking collectives  22 us (19%)
  starting transfers between devices  15.7 us (13%)
  local copies, waits for them, and re-layouts  2.78 us (2%)
    pallas_call x8, Pallas kernels, call(): pl.pallas_call(kernel, out_shape=tuple(outs), grid=grid, in_specs=in_spec...  50.9 us
    all_to_all x1, blocking collectives, exchange(): lax.all_to_all(split, 'tile', split_axis=0, concat_axis=0, tiled=False)  22 us
    all_to_all x3, waiting for transfers between devices, exchange(): lax.all_to_all(split, 'tile', split_axis=0, concat_axis=0, tiled=False)  11.7 us
    ppermute x8, waiting for transfers between devices, swap(): lax.ppermute(values, axis, [(i, i ^ step) for i in range(lax.axis_size(ax...  11 us
    all_to_all x3, starting transfers between devices, exchange(): lax.all_to_all(split, 'tile', split_axis=0, concat_axis=0, tiled=False)  10.9 us
    ppermute x8, starting transfers between devices, swap(): lax.ppermute(values, axis, [(i, i ^ step) for i in range(lax.axis_size(ax...  4.86 us
    unnamed x27, local copies, waits for them, and re-layouts  2.78 us
  transfers between devices with their start and end apart: 11, of which 6 were waited for; matrix products, arithmetic and copies ran while one was open for 1% of the time, Pallas kernels for 30%

commit v1 on v0

--- a/solution.py
+++ b/solution.py
@@ -398,7 +398,7 @@
 
 def outer_kernel(samples, groups, *refs):
     specs, grads = refs[:groups], refs[groups : 2 * groups]
-    out_ref, real, imag, crossed = refs[2 * groups :]
+    out_ref, real, imag, crossed, exact = refs[2 * groups :]
     total, channels, both = real.shape
     outs = crossed.shape[1]
     half = both // 2
@@ -412,7 +412,10 @@
             real[n] = jnp.where(low, spec, other)
             imag[n] = jnp.where(low, other, -spec)
             grad = grads[g][s * outs : (s + 1) * outs, :]
-            crossed[n] = pltpu.roll(grad.astype(F32), half, 1).astype(BF16)
+            swapped = pltpu.roll(grad.astype(F32), half, 1)
+            crossed[n] = swapped.astype(BF16)
+            exact[2 * n] = grad[outs - PACK :, :].astype(F32)
+            exact[2 * n + 1] = swapped[outs - PACK :, :]
 
     def body(block, carry):
         into = rows_of(out_ref, block, GROUP * outs)
@@ -420,7 +423,10 @@
         for first in range(0, GROUP, 2):
             pair = range(first, first + 2)
             lefts = [[packed_row(view, c) for view in views] for c in pair]
-            for o in range(0, outs, PACK):
+            for c in pair:
+                value = running([(view[c : c + 1, :], exact[n]) for n, view in enumerate(views)])
+                into[(c + 1) * outs - PACK : (c + 1) * outs, :] = value
+            for o in range(0, outs - PACK, PACK):
                 right = []
                 for n in range(total):
                     at = n % samples * outs + o
@@ -624,7 +630,8 @@
         "mode_grad",
         (*all_spectra, *all_grads),
         (shape(flat_weight.shape, F32),),
-        [pltpu.VMEM((total, channels, both), F32)] * 2 + [pltpu.VMEM((total, channels, both), BF16)],
+        [pltpu.VMEM((total, channels, both), F32)] * 2
+        + [pltpu.VMEM((total, channels, both), BF16), pltpu.VMEM((2 * total, PACK, both), F32)],
         grid=(owned,),
         blocks={n: per_mode for n in range(2 * groups)},
         out_blocks={0: weight_block},

time: 117 us -> 118 us (level)
  transfers between devices with their start and end apart: 11 -> 11, of which waited for: 6 -> 6; matrix products, arithmetic and copies ran while one was open for 1% -> 1% of each run, Pallas kernels for 30% -> 31%
where the time goes in v1:
time: 118 us; the launch traced here: 117 us
  Pallas kernels  51.9 us (44%)
  waiting for transfers between devices  22.7 us (19%)
  blocking collectives  22 us (19%)
  starting transfers between devices  15.7 us (13%)
  local copies, waits for them, and re-layouts  2.78 us (2%)
    pallas_call x8, Pallas kernels, call(): pl.pallas_call(kernel, out_shape=tuple(outs), grid=grid, in_specs=in_spec...  51.9 us
    all_to_all x1, blocking collectives, exchange(): lax.all_to_all(split, 'tile', split_axis=0, concat_axis=0, tiled=False)  22 us
    all_to_all x3, waiting for transfers between devices, exchange(): lax.all_to_all(split, 'tile', split_axis=0, concat_axis=0, tiled=False)  11.7 us
    ppermute x8, waiting for transfers between devices, swap(): lax.ppermute(values, axis, [(i, i ^ step) for i in range(lax.axis_size(ax...  11 us
    all_to_all x3, starting transfers between devices, exchange(): lax.all_to_all(split, 'tile', split_axis=0, concat_axis=0, tiled=False)  10.9 us
    ppermute x8, starting transfers between devices, swap(): lax.ppermute(values, axis, [(i, i ^ step) for i in range(lax.axis_size(ax...  4.86 us
    unnamed x27, local copies, waits for them, and re-layouts  2.78 us
  transfers between devices with their start and end apart: 11, of which 6 were waited for; matrix products, arithmetic and copies ran while one was open for 1% of the time, Pallas kernels for 31%

profile of v1, /device:TPU:0, one launch (start us, length us, event | category | flops | bytes accessed | tf_op | source)
XLA Modules:
  0.0 116.8 jit_solution(2806536744921779203)
XLA Ops:
  0.6 0.0 copy-start.1
  0.6 0.0 copy-start.5
  0.7 0.0 copy-start.7
  0.7 0.0 copy-start.4
  0.7 0.0 copy-start.6
  0.7 3.0 %columns.1 = (bf16[16,128,256]{2,1,0:T(8,128)(2,1)}, bf16[128,2048]{1,0:T(8,128)(2,1)}) custom-call(bf16[256,256]{1,0:T(8,128)(2,1)} %constant.30.order_ref.restore_ref, bf16[128,256]{1,0:T(8,128)(2,1)} %constant.31.table_ref, bf16[2048,256]{1,0:T(8,128)(2,1)} %bitcast.20, bf16[2048,256]{1,0:T(8,128)(2,1)} %bitcast.21, bf16[2048,256]{1,0:T(8,128)(2,1)} %bitcast.22, ...), custom_call_target="tpu_custom_call" | custom-call | tf_op jit(solution)/shard_map/columns/pallas_call | solution.py:450
  3.7 22.0 %all_to_all.20 = bf16[8,16,2048]{2,1,0:T(8,128)(2,1)} all-to-all(bf16[8,16,2048]{2,1,0:T(8,128)(2,1)} %bitcast.31), channel_id=1, replica_groups=mesh['dp'=4,'tile'=8] {'tile'}, dimensions={0} | all-to-all | bytes 1048576 | tf_op jit(solution)/shard_map/all_to_all | solution.py:518
  25.7 9.8 %mix_forward.1 = (bf16[1024,128]{1,0:T(8,128)(2,1)}, bf16[256,1024]{1,0:T(8,128)(2,1)}) custom-call(bf16[128,2048]{1,0:T(8,128)(2,1)} %bitcast.29, bf16[128,128]{1,0:T(8,128)(2,1)} %constant.32.rest_1_.order_ref, bf16[256,128]{1,0:T(8,128)(2,1)} %constant.33.rest_2_.rows_ref, bf16[256,128]{1,0:T(8,128)(2,1)} %constant.34.rest_3_.rest_1_, ...), custom_call_target="tpu_custom_call" | custom-call | tf_op jit(solution)/shard_map/mix_forward/pallas_call | solution.py:450
  35.5 3.6 %all-to-all-start.1 = ((bf16[8,32,1024]{2,1,0:T(8,128)(2,1)}), bf16[8,32,1024]{2,1,0:T(8,128)(2,1)S(1)}, u32[]{:S(2)}, u32[]{:S(2)}) async-start(bf16[8,32,1024]{2,1,0:T(8,128)(2,1)} %bitcast.30), calls=%async_computation.1 | async-start | bytes 1048576 | tf_op jit(solution)/shard_map/all_to_all | solution.py:518
  39.1 1.5 %collective-permute-start.1 = (bf16[1024,128]{1,0:T(8,128)(2,1)}, bf16[1024,128]{1,0:T(8,128)(2,1)S(1)}, u32[]{:S(2)}, u32[]{:S(2)}) collective-permute-start(bf16[1024,128]{1,0:T(8,128)(2,1)} %get-tuple-element.35.refs_0_), channel_id=1, source_target_pairs={{0,16},{8,24},{16,0},{24,8},{1,17},{9,25},{17,1},{25,9},{2,18},{10... | collective-permute-start | bytes 786440 | tf_op jit(solution)/shard_map/ppermute | solution.py:463
  40.7 0.0 collective-permute-start
  40.7 6.1 %collective-permute-done.1.refs_2_ = bf16[1024,128]{1,0:T(8,128)(2,1)S(1)} collective-permute-done((bf16[1024,128]{1,0:T(8,128)(2,1)}, bf16[1024,128]{1,0:T(8,128)(2,1)S(1)}, u32[]{:S(2)}, u32[]{:S(2)}) %collective-permute-start.1) | collective-permute-done | bytes 262176 | tf_op jit(solution)/shard_map/ppermute | solution.py:463
  46.8 0.0 collective-permute-start.2
  46.8 0.8 copy.15
  47.6 2.6 %relayout.1.cot_ref = bf16[16,128,256]{2,1,0:T(8,128)(2,1)} custom-call(bf16[256,256]{1,0:T(8,128)(2,1)} %constant.30.order_ref.restore_ref, bf16[2048,256]{1,0:T(8,128)(2,1)} %bitcast.24, bf16[2048,256]{1,0:T(8,128)(2,1)} %bitcast.25, bf16[2048,256]{1,0:T(8,128)(2,1)} %bitcast.26, bf16[2048,256]{1,0:T(8,128)(2,1)} %bitcast.27), custom_call_target="tpu_custom_call" | custom-call | tf_op jit(solution)/shard_map/relayout/pallas_call | solution.py:450
  50.2 0.1 fusion.4.local_ref
  50.3 3.0 %all-to-all-done.1 = bf16[8,32,1024]{2,1,0:T(8,128)(2,1)S(1)} async-done(((bf16[8,32,1024]{2,1,0:T(8,128)(2,1)}), bf16[8,32,1024]{2,1,0:T(8,128)(2,1)S(1)}, u32[]{:S(2)}, u32[]{:S(2)}) %all-to-all-start.1) | async-done | bytes 524320 | tf_op jit(solution)/shard_map/all_to_all | solution.py:518
  53.3 0.0 copy-done.1
  53.3 0.0 copy-start
  53.3 1.2 %copy-done = bf16[16,128,256]{2,1,0:T(8,128)(2,1)S(1)} copy-done((bf16[16,128,256]{2,1,0:T(8,128)(2,1)S(1)}, bf16[16,128,256]{2,1,0:T(8,128)(2,1)}, u32[]{:S(2)}) %copy-start) | copy-done | bytes 1048600
  54.6 6.6 %pixels.1 = (bf16[16,128,256]{2,1,0:T(8,128)(2,1)S(1)}, bf16[128,2048]{1,0:T(8,128)(2,1)}, f32[64,64]{1,0:T(8,128)S(1)}) custom-call(bf16[256,1024]{1,0:T(8,128)(2,1)S(1)} %bitcast.16, bf16[256,256]{1,0:T(8,128)(2,1)S(1)} %copy-done.1, bf16[128,256]{1,0:T(8,128)(2,1)S(1)} %copy-done.6, bf16[128,128]{1,0:T(8,128)(2,1)S(1)} %fusion.4.local_ref, ...), custom_call_target="tpu_custom_call" | custom-call | tf_op jit(solution)/shard_map/pixels/pallas_call | solution.py:450
  61.2 0.0 collective-permute-done.refs_1_
  61.2 0.0 collective-permute-done.2.refs_3_
  61.2 3.6 %all-to-all-start.2 = ((bf16[8,16,2048]{2,1,0:T(8,128)(2,1)}), bf16[8,16,2048]{2,1,0:T(8,128)(2,1)S(1)}, u32[]{:S(2)}, u32[]{:S(2)}) async-start(bf16[8,16,2048]{2,1,0:T(8,128)(2,1)} %bitcast.8), calls=%async_computation.2 | async-start | bytes 1048576 | tf_op jit(solution)/shard_map/all_to_all | solution.py:518
  64.9 0.0 collective-permute-start.3
  64.9 1.2 %collective-permute-done.3 = f32[64,64]{1,0:T(8,128)S(1)} collective-permute-done((f32[64,64]{1,0:T(8,128)S(1)}, f32[64,64]{1,0:T(8,128)S(1)}, u32[]{:S(2)}, u32[]{:S(2)}) %collective-permute-start.3) | collective-permute-done | bytes 16416 | tf_op jit(solution)/shard_map/ppermute | solution.py:463
  66.1 1.5 %collective-permute-start.4 = (f32[64,64]{1,0:T(8,128)S(1)}, f32[64,64]{1,0:T(8,128)S(1)}, u32[]{:S(2)}, u32[]{:S(2)}) collective-permute-start(f32[64,64]{1,0:T(8,128)S(1)} %add.14), channel_id=1, source_target_pairs={{0,16},{8,24},{16,0},{24,8},{1,17},{9,25},{17,1},{25,9},{2,18},{10... | collective-permute-start | bytes 49160 | tf_op jit(solution)/shard_map/ppermute | solution.py:463
  67.6 2.4 %collective-permute-done.4 = f32[64,64]{1,0:T(8,128)S(1)} collective-permute-done((f32[64,64]{1,0:T(8,128)S(1)}, f32[64,64]{1,0:T(8,128)S(1)}, u32[]{:S(2)}, u32[]{:S(2)}) %collective-permute-start.4) | collective-permute-done | bytes 16416 | tf_op jit(solution)/shard_map/ppermute | solution.py:463
  70.0 0.6 add.15.rest_2_
  70.6 8.7 %all-to-all-done.2 = bf16[8,16,2048]{2,1,0:T(8,128)(2,1)S(1)} async-done(((bf16[8,16,2048]{2,1,0:T(8,128)(2,1)}), bf16[8,16,2048]{2,1,0:T(8,128)(2,1)S(1)}, u32[]{:S(2)}, u32[]{:S(2)}) %all-to-all-start.2) | async-done | bytes 524320 | tf_op jit(solution)/shard_map/all_to_all | solution.py:518
  79.3 0.0 copy-done.7
  79.3 0.6 grad_spectra.1.rest_0_.refs_4_
  79.9 0.0 copy-start.2
  79.9 0.1 collective-permute-start.5
  80.0 1.6 %collective-permute-start.6 = (bf16[1024,128]{1,0:T(8,128)(2,1)S(1)}, bf16[1024,128]{1,0:T(8,128)(2,1)S(1)}, u32[]{:S(2)}, u32[]{:S(2)}) collective-permute-start(bf16[1024,128]{1,0:T(8,128)(2,1)S(1)} %grad_spectra.1.rest_0_.refs_4_), channel_id=1, source_target_pairs={{0,16},{8,24},{16,0},{24,8},{1,17},{9,25},{17,1},{25,9},{2,18},{10... | collective-permute-start | bytes 786440 | tf_op jit(solution)/shard_map/ppermute | solution.py:463
  81.6 9.2 %mix_backward.1 = bf16[256,1152]{1,0:T(8,128)(2,1)} custom-call(bf16[1024,128]{1,0:T(8,128)(2,1)} %copy-done.2, bf16[256,128]{1,0:T(8,128)(2,1)} %constant.34.rest_3_.rest_1_, f32[64,64]{1,0:T(8,128)} %add.15.rest_2_, bf16[32768,128]{1,0:T(8,128)(2,1)} %bitcast.18), custom_call_target="tpu_custom_call" | custom-call | tf_op jit(solution)/shard_map/mix_backward/pallas_call | solution.py:450
  90.8 0.0 collective-permute-done.5.refs_5_
  90.8 0.0 collective-permute-done.6.refs_6_
  90.8 0.0 copy-start.10
  90.8 3.6 %all-to-all-start.3 = ((bf16[8,32,1152]{2,1,0:T(8,128)(2,1)}), bf16[8,32,1152]{2,1,0:T(8,128)(2,1)S(1)}, u32[]{:S(2)}, u32[]{:S(2)}) async-start(bf16[8,32,1152]{2,1,0:T(8,128)(2,1)} %bitcast.28), calls=%async_computation.3 | async-start | bytes 1179648 | tf_op jit(solution)/shard_map/all_to_all | solution.py:518
  94.5 0.1 collective-permute-start.7
  94.6 0.1 fusion.5.local_ref
  94.7 1.3 %collective-permute-done.7.refs_7_ = bf16[1024,128]{1,0:T(8,128)(2,1)S(1)} collective-permute-done((bf16[1024,128]{1,0:T(8,128)(2,1)S(1)}, bf16[1024,128]{1,0:T(8,128)(2,1)S(1)}, u32[]{:S(2)}, u32[]{:S(2)}) %collective-permute-start.7) | collective-permute-done | bytes 262176 | tf_op jit(solution)/shard_map/ppermute | solution.py:463
  96.0 0.0 copy-start.11
  96.0 0.7 copy-done.11
  96.7 17.7 %mode_grad.1 = f32[32768,128]{1,0:T(8,128)} custom-call(bf16[1024,128]{1,0:T(8,128)(2,1)} %get-tuple-element.35.refs_0_, bf16[1024,128]{1,0:T(8,128)(2,1)} %collective-permute-done.refs_1_, bf16[1024,128]{1,0:T(8,128)(2,1)} %copy-done.8, bf16[1024,128]{1,0:T(8,128)(2,1)} %collective-permute-done.2.refs_3_, bf16[1024,128]{1,0:T(8,128)(2,1)} %copy-done.2, ...), custom_call_target="tpu_custom_call" | custom-call | tf_op jit(solution)/shard_map/mode_grad/pallas_call | solution.py:450
  114.5 0.0 all-to-all-done.3
  114.5 2.3 %final.1 = (bf16[2048,256]{1,0:T(8,128)(2,1)}, f32[64,64]{1,0:T(8,128)}) custom-call(bf16[256,1152]{1,0:T(8,128)(2,1)S(1)} %bitcast.14, bf16[256,256]{1,0:T(8,128)(2,1)S(1)} %copy-done.1, bf16[128,256]{1,0:T(8,128)(2,1)S(1)} %copy-done.6, bf16[128,128]{1,0:T(8,128)(2,1)S(1)} %fusion.5.local_ref, bf16[16,128,256]{2,1,0:T(8,128)(2,1)S(1)} %get-tuple-element.43.grad_ref, ...), custom_call_target="tpu_custom_call" | custom-call | tf_op jit(solution)/shard_map/final/pallas_call | solution.py:450
  (14 shorter events, 0.0 us)
Async XLA Ops:
  0.6 52.7 %copy-start.1 = (bf16[256,256]{1,0:T(8,128)(2,1)S(1)}, bf16[256,256]{1,0:T(8,128)(2,1)}, u32[]{:S(2)}) copy-start(bf16[256,256]{1,0:T(8,128)(2,1)} %constant.30.order_ref.restore_ref) | copy-start | bytes 393220
  0.6 52.7 %copy-start.5 = (bf16[128,256]{1,0:T(8,128)(2,1)S(1)}, bf16[128,256]{1,0:T(8,128)(2,1)}, u32[]{:S(2)}) copy-start(bf16[128,256]{1,0:T(8,128)(2,1)} %constant.31.table_ref) | copy-start | bytes 196612
  0.7 78.6 %copy-start.7 = (bf16[128,128]{1,0:T(8,128)(2,1)S(1)}, bf16[128,128]{1,0:T(8,128)(2,1)}, u32[]{:S(2)}) copy-start(bf16[128,128]{1,0:T(8,128)(2,1)} %constant.32.rest_1_.order_ref) | copy-start | bytes 98308
  0.7 78.6 %copy-start.4 = (bf16[256,128]{1,0:T(8,128)(2,1)S(1)}, bf16[256,128]{1,0:T(8,128)(2,1)}, u32[]{:S(2)}) copy-start(bf16[256,128]{1,0:T(8,128)(2,1)} %constant.33.rest_2_.rows_ref) | copy-start | bytes 196612
  0.7 52.6 %copy-start.6 = (bf16[128,256]{1,0:T(8,128)(2,1)S(1)}, bf16[128,256]{1,0:T(8,128)(2,1)}, u32[]{:S(2)}) copy-start(bf16[128,256]{1,0:T(8,128)(2,1)} %constant.35.back_ref) | copy-start | bytes 196612
  3.6 49.7 %copy-start.3 = (bf16[16,128,256]{2,1,0:T(8,128)(2,1)S(1)}, bf16[16,128,256]{2,1,0:T(8,128)(2,1)}, u32[]{:S(2)}) copy-start(bf16[16,128,256]{2,1,0:T(8,128)(2,1)} %get-tuple-element.27.field_ref) | copy-start | bytes 3145732
  3.7 91.0 %copy-start.12 = (bf16[64,64]{1,0:T(8,128)(2,1)S(1)}, bf16[64,64]{1,0:T(8,128)(2,1)}, u32[]{:S(2)}) copy-start(bf16[64,64]{1,0:T(8,128)(2,1)} %param.15) | copy-start | bytes 24580
  35.5 17.8 %all-to-all-start.1 = ((bf16[8,32,1024]{2,1,0:T(8,128)(2,1)}), bf16[8,32,1024]{2,1,0:T(8,128)(2,1)S(1)}, u32[]{:S(2)}, u32[]{:S(2)}) async-start(bf16[8,32,1024]{2,1,0:T(8,128)(2,1)} %bitcast.30), calls=%async_computation.1 | async-start | bytes 1048576 | tf_op jit(solution)/shard_map/all_to_all | solution.py:518
  39.1 7.6 %collective-permute-start.1 = (bf16[1024,128]{1,0:T(8,128)(2,1)}, bf16[1024,128]{1,0:T(8,128)(2,1)S(1)}, u32[]{:S(2)}, u32[]{:S(2)}) collective-permute-start(bf16[1024,128]{1,0:T(8,128)(2,1)} %get-tuple-element.35.refs_0_), channel_id=1, source_target_pairs={{0,16},{8,24},{16,0},{24,8},{1,17},{9,25},{17,1},{25,9},{2,18},{10... | collective-permute-start | bytes 786440 | tf_op jit(solution)/shard_map/ppermute | solution.py:463
  40.7 20.5 %collective-permute-start = (bf16[1024,128]{1,0:T(8,128)(2,1)}, bf16[1024,128]{1,0:T(8,128)(2,1)}, u32[]{:S(2)}, u32[]{:S(2)}) collective-permute-start(bf16[1024,128]{1,0:T(8,128)(2,1)} %get-tuple-element.35.refs_0_), channel_id=1, source_target_pairs={{0,8},{8,0},{16,24},{24,16},{1,9},{9,1},{17,25},{25,17},{2,10},{10... | collective-permute-start | bytes 786440 | tf_op jit(solution)/shard_map/ppermute | solution.py:463
  46.8 49.3 %copy-start.8 = (bf16[1024,128]{1,0:T(8,128)(2,1)}, bf16[1024,128]{1,0:T(8,128)(2,1)S(1)}, u32[]{:S(2)}) copy-start(bf16[1024,128]{1,0:T(8,128)(2,1)S(1)} %collective-permute-done.1.refs_2_) | copy-start | bytes 786436
  46.8 14.5 %collective-permute-start.2 = (bf16[1024,128]{1,0:T(8,128)(2,1)S(1)}, bf16[1024,128]{1,0:T(8,128)(2,1)}, u32[]{:S(2)}, u32[]{:S(2)}) collective-permute-start(bf16[1024,128]{1,0:T(8,128)(2,1)S(1)} %collective-permute-done.1.refs_2_), channel_id=1, source_target_pairs={{0,8},{8,0},{16,24},{24,16},{1,9},{9,1},{17,25},{25,17},{2,10},{10... | collective-permute-start | bytes 786440 | tf_op jit(solution)/shard_map/ppermute | solution.py:463
  53.3 1.2 %copy-start = (bf16[16,128,256]{2,1,0:T(8,128)(2,1)S(1)}, bf16[16,128,256]{2,1,0:T(8,128)(2,1)}, u32[]{:S(2)}) copy-start(bf16[16,128,256]{2,1,0:T(8,128)(2,1)} %relayout.1.cot_ref) | copy-start | bytes 3145732
  61.2 18.1 %all-to-all-start.2 = ((bf16[8,16,2048]{2,1,0:T(8,128)(2,1)}), bf16[8,16,2048]{2,1,0:T(8,128)(2,1)S(1)}, u32[]{:S(2)}, u32[]{:S(2)}) async-start(bf16[8,16,2048]{2,1,0:T(8,128)(2,1)} %bitcast.8), calls=%async_computation.2 | async-start | bytes 1048576 | tf_op jit(solution)/shard_map/all_to_all | solution.py:518
  64.9 1.2 %collective-permute-start.3 = (f32[64,64]{1,0:T(8,128)S(1)}, f32[64,64]{1,0:T(8,128)S(1)}, u32[]{:S(2)}, u32[]{:S(2)}) collective-permute-start(f32[64,64]{1,0:T(8,128)S(1)} %get-tuple-element.31), channel_id=1, source_target_pairs={{0,8},{8,0},{16,24},{24,16},{1,9},{9,1},{17,25},{25,17},{2,10},{10... | collective-permute-start | bytes 49160 | tf_op jit(solution)/shard_map/ppermute | solution.py:463
  66.1 3.9 %collective-permute-start.4 = (f32[64,64]{1,0:T(8,128)S(1)}, f32[64,64]{1,0:T(8,128)S(1)}, u32[]{:S(2)}, u32[]{:S(2)}) collective-permute-start(f32[64,64]{1,0:T(8,128)S(1)} %add.14), channel_id=1, source_target_pairs={{0,16},{8,24},{16,0},{24,8},{1,17},{9,25},{17,1},{25,9},{2,18},{10... | collective-permute-start | bytes 49160 | tf_op jit(solution)/shard_map/ppermute | solution.py:463
  79.9 1.7 %copy-start.2 = (bf16[1024,128]{1,0:T(8,128)(2,1)}, bf16[1024,128]{1,0:T(8,128)(2,1)S(1)}, u32[]{:S(2)}) copy-start(bf16[1024,128]{1,0:T(8,128)(2,1)S(1)} %grad_spectra.1.rest_0_.refs_4_) | copy-start | bytes 786436
  79.9 10.9 %collective-permute-start.5 = (bf16[1024,128]{1,0:T(8,128)(2,1)S(1)}, bf16[1024,128]{1,0:T(8,128)(2,1)S(1)}, u32[]{:S(2)}, u32[]{:S(2)}) collective-permute-start(bf16[1024,128]{1,0:T(8,128)(2,1)S(1)} %grad_spectra.1.rest_0_.refs_4_), channel_id=1, source_target_pairs={{0,8},{8,0},{16,24},{24,16},{1,9},{9,1},{17,25},{25,17},{2,10},{10... | collective-permute-start | bytes 786440 | tf_op jit(solution)/shard_map/ppermute | solution.py:463
  80.0 10.8 %collective-permute-start.6 = (bf16[1024,128]{1,0:T(8,128)(2,1)S(1)}, bf16[1024,128]{1,0:T(8,128)(2,1)S(1)}, u32[]{:S(2)}, u32[]{:S(2)}) collective-permute-start(bf16[1024,128]{1,0:T(8,128)(2,1)S(1)} %grad_spectra.1.rest_0_.refs_4_), channel_id=1, source_target_pairs={{0,16},{8,24},{16,0},{24,8},{1,17},{9,25},{17,1},{25,9},{2,18},{10... | collective-permute-start | bytes 786440 | tf_op jit(solution)/shard_map/ppermute | solution.py:463
  90.8 5.2 %copy-start.9 = (bf16[1024,128]{1,0:T(8,128)(2,1)}, bf16[1024,128]{1,0:T(8,128)(2,1)S(1)}, u32[]{:S(2)}) copy-start(bf16[1024,128]{1,0:T(8,128)(2,1)S(1)} %collective-permute-done.5.refs_5_) | copy-start | bytes 786436
  90.8 5.2 %copy-start.10 = (bf16[1024,128]{1,0:T(8,128)(2,1)}, bf16[1024,128]{1,0:T(8,128)(2,1)S(1)}, u32[]{:S(2)}) copy-start(bf16[1024,128]{1,0:T(8,128)(2,1)S(1)} %collective-permute-done.6.refs_6_) | copy-start | bytes 786436
  90.8 23.7 %all-to-all-start.3 = ((bf16[8,32,1152]{2,1,0:T(8,128)(2,1)}), bf16[8,32,1152]{2,1,0:T(8,128)(2,1)S(1)}, u32[]{:S(2)}, u32[]{:S(2)}) async-start(bf16[8,32,1152]{2,1,0:T(8,128)(2,1)} %bitcast.28), calls=%async_computation.3 | async-start | bytes 1179648 | tf_op jit(solution)/shard_map/all_to_all | solution.py:518
  94.5 1.6 %collective-permute-start.7 = (bf16[1024,128]{1,0:T(8,128)(2,1)S(1)}, bf16[1024,128]{1,0:T(8,128)(2,1)S(1)}, u32[]{:S(2)}, u32[]{:S(2)}) collective-permute-start(bf16[1024,128]{1,0:T(8,128)(2,1)S(1)} %collective-permute-done.6.refs_6_), channel_id=1, source_target_pairs={{0,8},{8,0},{16,24},{24,16},{1,9},{9,1},{17,25},{25,17},{2,10},{10... | collective-permute-start | bytes 786440 | tf_op jit(solution)/shard_map/ppermute | solution.py:463
  96.0 0.7 copy-start.11

commit v2 on v0

--- a/solution.py
+++ b/solution.py
@@ -398,39 +398,46 @@
 
 def outer_kernel(samples, groups, *refs):
     specs, grads = refs[:groups], refs[groups : 2 * groups]
-    out_ref, real, imag, crossed = refs[2 * groups :]
-    total, channels, both = real.shape
-    outs = crossed.shape[1]
+    out_ref, plain, joint, right, apart = refs[2 * groups :]
+    total, channels, both = plain.shape
+    outs = right.shape[1]
     half = both // 2
     low = low_half((channels, both), half)
-
     for g in range(groups):
         for s in range(samples):
             n = g * samples + s
             spec = specs[g][s * channels : (s + 1) * channels, :].astype(F32)
-            other = pltpu.roll(spec, half, 1)
-            real[n] = jnp.where(low, spec, other)
-            imag[n] = jnp.where(low, other, -spec)
-            grad = grads[g][s * outs : (s + 1) * outs, :]
-            crossed[n] = pltpu.roll(grad.astype(F32), half, 1).astype(BF16)
+            plain[n] = spec
+            added = spec + pltpu.roll(spec, half, 1)
+            joint[n] = jnp.where(low[: channels // 2], added[: channels // 2], added[channels // 2 :])
+            grad = grads[g][s * outs : (s + 1) * outs, :].astype(F32)
+            right[n] = grad
+            difference = pltpu.roll(grad, half, 1) - grad
+            apart[n] = jnp.where(low, difference, -difference)
+    blocks = channels // 2 // GROUP
+    tile_low = low_half((ROWS, both), half)
 
     def body(block, carry):
-        into = rows_of(out_ref, block, GROUP * outs)
-        views = [rows_of(store.at[n], block, GROUP) for n in range(total) for store in (real, imag)]
-        for first in range(0, GROUP, 2):
-            pair = range(first, first + 2)
-            lefts = [[packed_row(view, c) for view in views] for c in pair]
-            for o in range(0, outs, PACK):
-                right = []
-                for n in range(total):
-                    at = n % samples * outs + o
-                    right += [grads[n // samples][at : at + PACK, :], crossed[n, o : o + PACK, :]]
-                results = [running(list(zip(left, right))) for left in lefts]
-                for c, result in zip(pair, results):
-                    into[c * outs + o : c * outs + o + PACK, :] = result.astype(F32)
+        near, far = rows_of(out_ref, block, GROUP * outs), rows_of(out_ref, block + blocks, GROUP * outs)
+        first = [rows_of(plain.at[n], block, GROUP) for n in range(total)]
+        second = [rows_of(plain.at[n], block + blocks, GROUP) for n in range(total)]
+        third = [rows_of(joint.at[n], block, GROUP) for n in range(total)]
+        for c in range(GROUP):
+            rows = [[view[c : c + 1, :] for view in views] for views in (first, second, third)]
+            for o in range(0, outs, ROWS):
+                tiles = [right[n, o : o + ROWS, :] for n in range(total)]
+                others = [apart[n, o : o + ROWS, :] for n in range(total)]
+                one, two = (running(list(zip(row, tiles))) for row in rows[:2])
+                both_joint = running(list(zip(rows[2], others)))
+                for value, extra, into in (
+                    (one, pltpu.roll(both_joint, half, 1), near),
+                    (two, both_joint, far),
+                ):
+                    result = pltpu.roll(value, half, 1) + jnp.where(tile_low, value, extra - value)
+                    into[c * outs + o : c * outs + o + ROWS, :] = result
         return carry
 
-    lax.fori_loop(0, channels // GROUP, body, 0)
+    lax.fori_loop(0, blocks, body, 0)
 
 
 def whole(extent):
@@ -624,7 +631,12 @@
         "mode_grad",
         (*all_spectra, *all_grads),
         (shape(flat_weight.shape, F32),),
-        [pltpu.VMEM((total, channels, both), F32)] * 2 + [pltpu.VMEM((total, channels, both), BF16)],
+        [
+            pltpu.VMEM((total, channels, both), F32),
+            pltpu.VMEM((total, channels // 2, both), F32),
+            pltpu.VMEM((total, channels, both), F32),
+            pltpu.VMEM((total, channels, both), F32),
+        ],
         grid=(owned,),
         blocks={n: per_mode for n in range(2 * groups)},
         out_blocks={0: weight_block},

time: 117 us -> 124 us (1.060)
  Pallas kernels: 50.9 us -> 58.1 us
    pallas_call x8, Pallas kernels: 50.9 us -> 58.1 us  [call(): pl.pallas_call(kernel, out_shape=tuple(outs), grid=grid, in_specs=in_spec...]
  transfers between devices with their start and end apart: 11 -> 11, of which waited for: 6 -> 6; matrix products, arithmetic and copies ran while one was open for 1% -> 1% of each run, Pallas kernels for 30% -> 34%
where the time goes in v2:
time: 124 us; the launch traced here: 123 us
  Pallas kernels  58.1 us (47%)
  waiting for transfers between devices  22.7 us (18%)
  blocking collectives  22 us (18%)
  starting transfers between devices  15.7 us (13%)
  local copies, waits for them, and re-layouts  2.78 us (2%)
    pallas_call x8, Pallas kernels, call(): pl.pallas_call(kernel, out_shape=tuple(outs), grid=grid, in_specs=in_spec...  58.1 us
    all_to_all x1, blocking collectives, exchange(): lax.all_to_all(split, 'tile', split_axis=0, concat_axis=0, tiled=False)  22 us
    all_to_all x3, waiting for transfers between devices, exchange(): lax.all_to_all(split, 'tile', split_axis=0, concat_axis=0, tiled=False)  11.7 us
    ppermute x8, waiting for transfers between devices, swap(): lax.ppermute(values, axis, [(i, i ^ step) for i in range(lax.axis_size(ax...  11 us
    all_to_all x3, starting transfers between devices, exchange(): lax.all_to_all(split, 'tile', split_axis=0, concat_axis=0, tiled=False)  10.9 us
    ppermute x8, starting transfers between devices, swap(): lax.ppermute(values, axis, [(i, i ^ step) for i in range(lax.axis_size(ax...  4.86 us
    unnamed x27, local copies, waits for them, and re-layouts  2.78 us
  transfers between devices with their start and end apart: 11, of which 6 were waited for; matrix products, arithmetic and copies ran while one was open for 1% of the time, Pallas kernels for 34%

profile of v2, /device:TPU:0, one launch (start us, length us, event | category | flops | bytes accessed | tf_op | source)
XLA Modules:
  0.0 122.9 jit_solution(13542247623367017629)
XLA Ops:
  0.6 0.0 copy-start.1
  0.6 0.0 copy-start.5
  0.7 0.0 copy-start.7
  0.7 0.0 copy-start.4
  0.7 0.0 copy-start.6
  0.7 3.0 %columns.1 = (bf16[16,128,256]{2,1,0:T(8,128)(2,1)}, bf16[128,2048]{1,0:T(8,128)(2,1)}) custom-call(bf16[256,256]{1,0:T(8,128)(2,1)} %constant.30.order_ref.restore_ref, bf16[128,256]{1,0:T(8,128)(2,1)} %constant.31.table_ref, bf16[2048,256]{1,0:T(8,128)(2,1)} %bitcast.20, bf16[2048,256]{1,0:T(8,128)(2,1)} %bitcast.21, bf16[2048,256]{1,0:T(8,128)(2,1)} %bitcast.22, ...), custom_call_target="tpu_custom_call" | custom-call | tf_op jit(solution)/shard_map/columns/pallas_call | solution.py:451
  3.7 22.0 %all_to_all.20 = bf16[8,16,2048]{2,1,0:T(8,128)(2,1)} all-to-all(bf16[8,16,2048]{2,1,0:T(8,128)(2,1)} %bitcast.31), channel_id=1, replica_groups=mesh['dp'=4,'tile'=8] {'tile'}, dimensions={0} | all-to-all | bytes 1048576 | tf_op jit(solution)/shard_map/all_to_all | solution.py:519
  25.7 9.8 %mix_forward.1 = (bf16[1024,128]{1,0:T(8,128)(2,1)}, bf16[256,1024]{1,0:T(8,128)(2,1)}) custom-call(bf16[128,2048]{1,0:T(8,128)(2,1)} %bitcast.29, bf16[128,128]{1,0:T(8,128)(2,1)} %constant.32.rest_1_.order_ref, bf16[256,128]{1,0:T(8,128)(2,1)} %constant.33.rest_2_.rows_ref, bf16[256,128]{1,0:T(8,128)(2,1)} %constant.34.rest_3_.rest_1_, ...), custom_call_target="tpu_custom_call" | custom-call | tf_op jit(solution)/shard_map/mix_forward/pallas_call | solution.py:451
  35.5 3.6 %all-to-all-start.1 = ((bf16[8,32,1024]{2,1,0:T(8,128)(2,1)}), bf16[8,32,1024]{2,1,0:T(8,128)(2,1)S(1)}, u32[]{:S(2)}, u32[]{:S(2)}) async-start(bf16[8,32,1024]{2,1,0:T(8,128)(2,1)} %bitcast.30), calls=%async_computation.1 | async-start | bytes 1048576 | tf_op jit(solution)/shard_map/all_to_all | solution.py:519
  39.1 1.5 %collective-permute-start.1 = (bf16[1024,128]{1,0:T(8,128)(2,1)}, bf16[1024,128]{1,0:T(8,128)(2,1)S(1)}, u32[]{:S(2)}, u32[]{:S(2)}) collective-permute-start(bf16[1024,128]{1,0:T(8,128)(2,1)} %get-tuple-element.35.refs_0_), channel_id=1, source_target_pairs={{0,16},{8,24},{16,0},{24,8},{1,17},{9,25},{17,1},{25,9},{2,18},{10... | collective-permute-start | bytes 786440 | tf_op jit(solution)/shard_map/ppermute | solution.py:464
  40.7 0.0 collective-permute-start
  40.7 6.1 %collective-permute-done.1.refs_2_ = bf16[1024,128]{1,0:T(8,128)(2,1)S(1)} collective-permute-done((bf16[1024,128]{1,0:T(8,128)(2,1)}, bf16[1024,128]{1,0:T(8,128)(2,1)S(1)}, u32[]{:S(2)}, u32[]{:S(2)}) %collective-permute-start.1) | collective-permute-done | bytes 262176 | tf_op jit(solution)/shard_map/ppermute | solution.py:464
  46.8 0.0 collective-permute-start.2
  46.8 0.8 copy.15
  47.6 2.6 %relayout.1.cot_ref = bf16[16,128,256]{2,1,0:T(8,128)(2,1)} custom-call(bf16[256,256]{1,0:T(8,128)(2,1)} %constant.30.order_ref.restore_ref, bf16[2048,256]{1,0:T(8,128)(2,1)} %bitcast.24, bf16[2048,256]{1,0:T(8,128)(2,1)} %bitcast.25, bf16[2048,256]{1,0:T(8,128)(2,1)} %bitcast.26, bf16[2048,256]{1,0:T(8,128)(2,1)} %bitcast.27), custom_call_target="tpu_custom_call" | custom-call | tf_op jit(solution)/shard_map/relayout/pallas_call | solution.py:451
  50.2 0.1 fusion.4.local_ref
  50.3 3.0 %all-to-all-done.1 = bf16[8,32,1024]{2,1,0:T(8,128)(2,1)S(1)} async-done(((bf16[8,32,1024]{2,1,0:T(8,128)(2,1)}), bf16[8,32,1024]{2,1,0:T(8,128)(2,1)S(1)}, u32[]{:S(2)}, u32[]{:S(2)}) %all-to-all-start.1) | async-done | bytes 524320 | tf_op jit(solution)/shard_map/all_to_all | solution.py:519
  53.3 0.0 copy-done.1
  53.3 0.0 copy-start
  53.3 1.2 copy-done
  54.6 6.6 %pixels.1 = (bf16[16,128,256]{2,1,0:T(8,128)(2,1)S(1)}, bf16[128,2048]{1,0:T(8,128)(2,1)}, f32[64,64]{1,0:T(8,128)S(1)}) custom-call(bf16[256,1024]{1,0:T(8,128)(2,1)S(1)} %bitcast.16, bf16[256,256]{1,0:T(8,128)(2,1)S(1)} %copy-done.1, bf16[128,256]{1,0:T(8,128)(2,1)S(1)} %copy-done.6, bf16[128,128]{1,0:T(8,128)(2,1)S(1)} %fusion.4.local_ref, ...), custom_call_target="tpu_custom_call" | custom-call | tf_op jit(solution)/shard_map/pixels/pallas_call | solution.py:451
  61.2 0.0 collective-permute-done.refs_1_
  61.2 0.0 collective-permute-done.2.refs_3_
  61.2 3.6 %all-to-all-start.2 = ((bf16[8,16,2048]{2,1,0:T(8,128)(2,1)}), bf16[8,16,2048]{2,1,0:T(8,128)(2,1)S(1)}, u32[]{:S(2)}, u32[]{:S(2)}) async-start(bf16[8,16,2048]{2,1,0:T(8,128)(2,1)} %bitcast.8), calls=%async_computation.2 | async-start | bytes 1048576 | tf_op jit(solution)/shard_map/all_to_all | solution.py:519
  64.9 0.0 collective-permute-start.3
  64.9 1.2 collective-permute-done.3
  66.1 1.5 %collective-permute-start.4 = (f32[64,64]{1,0:T(8,128)S(1)}, f32[64,64]{1,0:T(8,128)S(1)}, u32[]{:S(2)}, u32[]{:S(2)}) collective-permute-start(f32[64,64]{1,0:T(8,128)S(1)} %add.14), channel_id=1, source_target_pairs={{0,16},{8,24},{16,0},{24,8},{1,17},{9,25},{17,1},{25,9},{2,18},{10... | collective-permute-start | bytes 49160 | tf_op jit(solution)/shard_map/ppermute | solution.py:464
  67.6 2.4 %collective-permute-done.4 = f32[64,64]{1,0:T(8,128)S(1)} collective-permute-done((f32[64,64]{1,0:T(8,128)S(1)}, f32[64,64]{1,0:T(8,128)S(1)}, u32[]{:S(2)}, u32[]{:S(2)}) %collective-permute-start.4) | collective-permute-done | bytes 16416 | tf_op jit(solution)/shard_map/ppermute | solution.py:464
  70.0 0.6 add.15.rest_2_
  70.6 8.7 %all-to-all-done.2 = bf16[8,16,2048]{2,1,0:T(8,128)(2,1)S(1)} async-done(((bf16[8,16,2048]{2,1,0:T(8,128)(2,1)}), bf16[8,16,2048]{2,1,0:T(8,128)(2,1)S(1)}, u32[]{:S(2)}, u32[]{:S(2)}) %all-to-all-start.2) | async-done | bytes 524320 | tf_op jit(solution)/shard_map/all_to_all | solution.py:519
  79.3 0.0 copy-done.7
  79.3 0.6 grad_spectra.1.rest_0_.refs_4_
  79.9 0.0 copy-start.2
  79.9 0.1 collective-permute-start.5
  80.0 1.6 %collective-permute-start.6 = (bf16[1024,128]{1,0:T(8,128)(2,1)S(1)}, bf16[1024,128]{1,0:T(8,128)(2,1)S(1)}, u32[]{:S(2)}, u32[]{:S(2)}) collective-permute-start(bf16[1024,128]{1,0:T(8,128)(2,1)S(1)} %grad_spectra.1.rest_0_.refs_4_), channel_id=1, source_target_pairs={{0,16},{8,24},{16,0},{24,8},{1,17},{9,25},{17,1},{25,9},{2,18},{10... | collective-permute-start | bytes 786440 | tf_op jit(solution)/shard_map/ppermute | solution.py:464
  81.6 9.2 %mix_backward.1 = bf16[256,1152]{1,0:T(8,128)(2,1)} custom-call(bf16[1024,128]{1,0:T(8,128)(2,1)} %copy-done.2, bf16[256,128]{1,0:T(8,128)(2,1)} %constant.34.rest_3_.rest_1_, f32[64,64]{1,0:T(8,128)} %add.15.rest_2_, bf16[32768,128]{1,0:T(8,128)(2,1)} %bitcast.18), custom_call_target="tpu_custom_call" | custom-call | tf_op jit(solution)/shard_map/mix_backward/pallas_call | solution.py:451
  90.8 0.0 collective-permute-done.5.refs_5_
  90.8 0.0 collective-permute-done.6.refs_6_
  90.8 0.0 copy-start.10
  90.8 3.6 %all-to-all-start.3 = ((bf16[8,32,1152]{2,1,0:T(8,128)(2,1)}), bf16[8,32,1152]{2,1,0:T(8,128)(2,1)S(1)}, u32[]{:S(2)}, u32[]{:S(2)}) async-start(bf16[8,32,1152]{2,1,0:T(8,128)(2,1)} %bitcast.28), calls=%async_computation.3 | async-start | bytes 1179648 | tf_op jit(solution)/shard_map/all_to_all | solution.py:519
  94.5 0.1 collective-permute-start.7
  94.6 0.1 fusion.5.local_ref
  94.7 1.3 %collective-permute-done.7.refs_7_ = bf16[1024,128]{1,0:T(8,128)(2,1)S(1)} collective-permute-done((bf16[1024,128]{1,0:T(8,128)(2,1)S(1)}, bf16[1024,128]{1,0:T(8,128)(2,1)S(1)}, u32[]{:S(2)}, u32[]{:S(2)}) %collective-permute-start.7) | collective-permute-done | bytes 262176 | tf_op jit(solution)/shard_map/ppermute | solution.py:464
  96.0 0.0 copy-start.11
  96.0 0.7 copy-done.11
  96.7 23.9 %mode_grad.1 = f32[32768,128]{1,0:T(8,128)} custom-call(bf16[1024,128]{1,0:T(8,128)(2,1)} %get-tuple-element.35.refs_0_, bf16[1024,128]{1,0:T(8,128)(2,1)} %collective-permute-done.refs_1_, bf16[1024,128]{1,0:T(8,128)(2,1)} %copy-done.8, bf16[1024,128]{1,0:T(8,128)(2,1)} %collective-permute-done.2.refs_3_, bf16[1024,128]{1,0:T(8,128)(2,1)} %copy-done.2, ...), custom_call_target="tpu_custom_call" | custom-call | tf_op jit(solution)/shard_map/mode_grad/pallas_call | solution.py:451
  120.6 0.0 all-to-all-done.3
  120.6 2.3 %final.1 = (bf16[2048,256]{1,0:T(8,128)(2,1)}, f32[64,64]{1,0:T(8,128)}) custom-call(bf16[256,1152]{1,0:T(8,128)(2,1)S(1)} %bitcast.14, bf16[256,256]{1,0:T(8,128)(2,1)S(1)} %copy-done.1, bf16[128,256]{1,0:T(8,128)(2,1)S(1)} %copy-done.6, bf16[128,128]{1,0:T(8,128)(2,1)S(1)} %fusion.5.local_ref, bf16[16,128,256]{2,1,0:T(8,128)(2,1)S(1)} %get-tuple-element.43.grad_ref, ...), custom_call_target="tpu_custom_call" | custom-call | tf_op jit(solution)/shard_map/final/pallas_call | solution.py:451
  (14 shorter events, 0.0 us)
Async XLA Ops:
  0.6 52.7 %copy-start.1 = (bf16[256,256]{1,0:T(8,128)(2,1)S(1)}, bf16[256,256]{1,0:T(8,128)(2,1)}, u32[]{:S(2)}) copy-start(bf16[256,256]{1,0:T(8,128)(2,1)} %constant.30.order_ref.restore_ref) | copy-start | bytes 393220
  0.6 52.7 %copy-start.5 = (bf16[128,256]{1,0:T(8,128)(2,1)S(1)}, bf16[128,256]{1,0:T(8,128)(2,1)}, u32[]{:S(2)}) copy-start(bf16[128,256]{1,0:T(8,128)(2,1)} %constant.31.table_ref) | copy-start | bytes 196612
  0.7 78.6 %copy-start.7 = (bf16[128,128]{1,0:T(8,128)(2,1)S(1)}, bf16[128,128]{1,0:T(8,128)(2,1)}, u32[]{:S(2)}) copy-start(bf16[128,128]{1,0:T(8,128)(2,1)} %constant.32.rest_1_.order_ref) | copy-start | bytes 98308
  0.7 78.6 %copy-start.4 = (bf16[256,128]{1,0:T(8,128)(2,1)S(1)}, bf16[256,128]{1,0:T(8,128)(2,1)}, u32[]{:S(2)}) copy-start(bf16[256,128]{1,0:T(8,128)(2,1)} %constant.33.rest_2_.rows_ref) | copy-start | bytes 196612
  0.7 52.6 %copy-start.6 = (bf16[128,256]{1,0:T(8,128)(2,1)S(1)}, bf16[128,256]{1,0:T(8,128)(2,1)}, u32[]{:S(2)}) copy-start(bf16[128,256]{1,0:T(8,128)(2,1)} %constant.35.back_ref) | copy-start | bytes 196612
  3.6 49.7 %copy-start.3 = (bf16[16,128,256]{2,1,0:T(8,128)(2,1)S(1)}, bf16[16,128,256]{2,1,0:T(8,128)(2,1)}, u32[]{:S(2)}) copy-start(bf16[16,128,256]{2,1,0:T(8,128)(2,1)} %get-tuple-element.27.field_ref) | copy-start | bytes 3145732
  3.7 91.0 %copy-start.12 = (bf16[64,64]{1,0:T(8,128)(2,1)S(1)}, bf16[64,64]{1,0:T(8,128)(2,1)}, u32[]{:S(2)}) copy-start(bf16[64,64]{1,0:T(8,128)(2,1)} %param.15) | copy-start | bytes 24580
  35.5 17.8 %all-to-all-start.1 = ((bf16[8,32,1024]{2,1,0:T(8,128)(2,1)}), bf16[8,32,1024]{2,1,0:T(8,128)(2,1)S(1)}, u32[]{:S(2)}, u32[]{:S(2)}) async-start(bf16[8,32,1024]{2,1,0:T(8,128)(2,1)} %bitcast.30), calls=%async_computation.1 | async-start | bytes 1048576 | tf_op jit(solution)/shard_map/all_to_all | solution.py:519
  39.1 7.6 %collective-permute-start.1 = (bf16[1024,128]{1,0:T(8,128)(2,1)}, bf16[1024,128]{1,0:T(8,128)(2,1)S(1)}, u32[]{:S(2)}, u32[]{:S(2)}) collective-permute-start(bf16[1024,128]{1,0:T(8,128)(2,1)} %get-tuple-element.35.refs_0_), channel_id=1, source_target_pairs={{0,16},{8,24},{16,0},{24,8},{1,17},{9,25},{17,1},{25,9},{2,18},{10... | collective-permute-start | bytes 786440 | tf_op jit(solution)/shard_map/ppermute | solution.py:464
  40.7 20.5 %collective-permute-start = (bf16[1024,128]{1,0:T(8,128)(2,1)}, bf16[1024,128]{1,0:T(8,128)(2,1)}, u32[]{:S(2)}, u32[]{:S(2)}) collective-permute-start(bf16[1024,128]{1,0:T(8,128)(2,1)} %get-tuple-element.35.refs_0_), channel_id=1, source_target_pairs={{0,8},{8,0},{16,24},{24,16},{1,9},{9,1},{17,25},{25,17},{2,10},{10... | collective-permute-start | bytes 786440 | tf_op jit(solution)/shard_map/ppermute | solution.py:464
  46.8 49.3 %copy-start.8 = (bf16[1024,128]{1,0:T(8,128)(2,1)}, bf16[1024,128]{1,0:T(8,128)(2,1)S(1)}, u32[]{:S(2)}) copy-start(bf16[1024,128]{1,0:T(8,128)(2,1)S(1)} %collective-permute-done.1.refs_2_) | copy-start | bytes 786436
  46.8 14.5 %collective-permute-start.2 = (bf16[1024,128]{1,0:T(8,128)(2,1)S(1)}, bf16[1024,128]{1,0:T(8,128)(2,1)}, u32[]{:S(2)}, u32[]{:S(2)}) collective-permute-start(bf16[1024,128]{1,0:T(8,128)(2,1)S(1)} %collective-permute-done.1.refs_2_), channel_id=1, source_target_pairs={{0,8},{8,0},{16,24},{24,16},{1,9},{9,1},{17,25},{25,17},{2,10},{10... | collective-permute-start | bytes 786440 | tf_op jit(solution)/shard_map/ppermute | solution.py:464
  53.3 1.2 copy-start
  61.2 18.1 %all-to-all-start.2 = ((bf16[8,16,2048]{2,1,0:T(8,128)(2,1)}), bf16[8,16,2048]{2,1,0:T(8,128)(2,1)S(1)}, u32[]{:S(2)}, u32[]{:S(2)}) async-start(bf16[8,16,2048]{2,1,0:T(8,128)(2,1)} %bitcast.8), calls=%async_computation.2 | async-start | bytes 1048576 | tf_op jit(solution)/shard_map/all_to_all | solution.py:519
  64.9 1.2 collective-permute-start.3
  66.1 3.9 %collective-permute-start.4 = (f32[64,64]{1,0:T(8,128)S(1)}, f32[64,64]{1,0:T(8,128)S(1)}, u32[]{:S(2)}, u32[]{:S(2)}) collective-permute-start(f32[64,64]{1,0:T(8,128)S(1)} %add.14), channel_id=1, source_target_pairs={{0,16},{8,24},{16,0},{24,8},{1,17},{9,25},{17,1},{25,9},{2,18},{10... | collective-permute-start | bytes 49160 | tf_op jit(solution)/shard_map/ppermute | solution.py:464
  79.9 1.7 %copy-start.2 = (bf16[1024,128]{1,0:T(8,128)(2,1)}, bf16[1024,128]{1,0:T(8,128)(2,1)S(1)}, u32[]{:S(2)}) copy-start(bf16[1024,128]{1,0:T(8,128)(2,1)S(1)} %grad_spectra.1.rest_0_.refs_4_) | copy-start | bytes 786436
  79.9 10.9 %collective-permute-start.5 = (bf16[1024,128]{1,0:T(8,128)(2,1)S(1)}, bf16[1024,128]{1,0:T(8,128)(2,1)S(1)}, u32[]{:S(2)}, u32[]{:S(2)}) collective-permute-start(bf16[1024,128]{1,0:T(8,128)(2,1)S(1)} %grad_spectra.1.rest_0_.refs_4_), channel_id=1, source_target_pairs={{0,8},{8,0},{16,24},{24,16},{1,9},{9,1},{17,25},{25,17},{2,10},{10... | collective-permute-start | bytes 786440 | tf_op jit(solution)/shard_map/ppermute | solution.py:464
  80.0 10.8 %collective-permute-start.6 = (bf16[1024,128]{1,0:T(8,128)(2,1)S(1)}, bf16[1024,128]{1,0:T(8,128)(2,1)S(1)}, u32[]{:S(2)}, u32[]{:S(2)}) collective-permute-start(bf16[1024,128]{1,0:T(8,128)(2,1)S(1)} %grad_spectra.1.rest_0_.refs_4_), channel_id=1, source_target_pairs={{0,16},{8,24},{16,0},{24,8},{1,17},{9,25},{17,1},{25,9},{2,18},{10... | collective-permute-start | bytes 786440 | tf_op jit(solution)/shard_map/ppermute | solution.py:464
  90.8 5.2 %copy-start.9 = (bf16[1024,128]{1,0:T(8,128)(2,1)}, bf16[1024,128]{1,0:T(8,128)(2,1)S(1)}, u32[]{:S(2)}) copy-start(bf16[1024,128]{1,0:T(8,128)(2,1)S(1)} %collective-permute-done.5.refs_5_) | copy-start | bytes 786436
  90.8 5.2 %copy-start.10 = (bf16[1024,128]{1,0:T(8,128)(2,1)}, bf16[1024,128]{1,0:T(8,128)(2,1)S(1)}, u32[]{:S(2)}) copy-start(bf16[1024,128]{1,0:T(8,128)(2,1)S(1)} %collective-permute-done.6.refs_6_) | copy-start | bytes 786436
  90.8 29.8 %all-to-all-start.3 = ((bf16[8,32,1152]{2,1,0:T(8,128)(2,1)}), bf16[8,32,1152]{2,1,0:T(8,128)(2,1)S(1)}, u32[]{:S(2)}, u32[]{:S(2)}) async-start(bf16[8,32,1152]{2,1,0:T(8,128)(2,1)} %bitcast.28), calls=%async_computation.3 | async-start | bytes 1179648 | tf_op jit(solution)/shard_map/all_to_all | solution.py:519
  94.5 1.6 %collective-permute-start.7 = (bf16[1024,128]{1,0:T(8,128)(2,1)S(1)}, bf16[1024,128]{1,0:T(8,128)(2,1)S(1)}, u32[]{:S(2)}, u32[]{:S(2)}) collective-permute-start(bf16[1024,128]{1,0:T(8,128)(2,1)S(1)} %collective-permute-done.6.refs_6_), channel_id=1, source_target_pairs={{0,8},{8,0},{16,24},{24,16},{1,9},{9,1},{17,25},{25,17},{2,10},{10... | collective-permute-start | bytes 786440 | tf_op jit(solution)/shard_map/ppermute | solution.py:464
  96.0 0.7 copy-start.11

commit v3 on v0

--- a/solution.py
+++ b/solution.py
@@ -257,7 +257,7 @@
         for s in range(samples):
             rows = []
             for store in (real, imag):
-                part = rows_of(store, (q * lanes + s * channels) // GROUP + block, GROUP)
+                part = rows_of(store, (q * lanes + s * channels) // GROUP + block, GROUP)[...]
                 rows.append([packed_row(part, step) for step in range(GROUP)])
             for o in range(0, outs, PACK):
                 column = [view[step * outs + o : step * outs + o + PACK, :] for step in range(GROUP)]
@@ -416,7 +416,7 @@
 
     def body(block, carry):
         into = rows_of(out_ref, block, GROUP * outs)
-        views = [rows_of(store.at[n], block, GROUP) for n in range(total) for store in (real, imag)]
+        views = [rows_of(store.at[n], block, GROUP)[...] for n in range(total) for store in (real, imag)]
         for first in range(0, GROUP, 2):
             pair = range(first, first + 2)
             lefts = [[packed_row(view, c) for view in views] for c in pair]

time: 117 us -> 116 us (level)
  no operation moved by 1% of the time
where the time goes in v3:
time: 116 us; the launch traced here: 115 us
  Pallas kernels  50.6 us (44%)
  waiting for transfers between devices  22.7 us (20%)
  blocking collectives  22 us (19%)
  starting transfers between devices  15.7 us (14%)
  local copies, waits for them, and re-layouts  2.78 us (2%)
    pallas_call x8, Pallas kernels, call(): pl.pallas_call(kernel, out_shape=tuple(outs), grid=grid, in_specs=in_spec...  50.6 us
    all_to_all x1, blocking collectives, exchange(): lax.all_to_all(split, 'tile', split_axis=0, concat_axis=0, tiled=False)  22 us
    all_to_all x3, waiting for transfers between devices, exchange(): lax.all_to_all(split, 'tile', split_axis=0, concat_axis=0, tiled=False)  11.7 us
    ppermute x8, waiting for transfers between devices, swap(): lax.ppermute(values, axis, [(i, i ^ step) for i in range(lax.axis_size(ax...  11 us
    all_to_all x3, starting transfers between devices, exchange(): lax.all_to_all(split, 'tile', split_axis=0, concat_axis=0, tiled=False)  10.9 us
    ppermute x8, starting transfers between devices, swap(): lax.ppermute(values, axis, [(i, i ^ step) for i in range(lax.axis_size(ax...  4.86 us
    unnamed x27, local copies, waits for them, and re-layouts  2.78 us
  transfers between devices with their start and end apart: 11, of which 6 were waited for; matrix products, arithmetic and copies ran while one was open for 1% of the time, Pallas kernels for 30%

profile of v3, /device:TPU:0, one launch (start us, length us, event | category | flops | bytes accessed | tf_op | source)
XLA Modules:
  0.0 115.4 jit_solution(12190958545201506201)
XLA Ops:
  0.6 0.0 copy-start.1
  0.6 0.0 copy-start.5
  0.7 0.0 copy-start.7
  0.7 0.0 copy-start.4
  0.7 0.0 copy-start.6
  0.7 3.0 %columns.1 = (bf16[16,128,256]{2,1,0:T(8,128)(2,1)}, bf16[128,2048]{1,0:T(8,128)(2,1)}) custom-call(bf16[256,256]{1,0:T(8,128)(2,1)} %constant.30.order_ref.restore_ref, bf16[128,256]{1,0:T(8,128)(2,1)} %constant.31.table_ref, bf16[2048,256]{1,0:T(8,128)(2,1)} %bitcast.20, bf16[2048,256]{1,0:T(8,128)(2,1)} %bitcast.21, bf16[2048,256]{1,0:T(8,128)(2,1)} %bitcast.22, ...), custom_call_target="tpu_custom_call" | custom-call | tf_op jit(solution)/shard_map/columns/pallas_call | solution.py:444
  3.7 22.0 %all_to_all.20 = bf16[8,16,2048]{2,1,0:T(8,128)(2,1)} all-to-all(bf16[8,16,2048]{2,1,0:T(8,128)(2,1)} %bitcast.31), channel_id=1, replica_groups=mesh['dp'=4,'tile'=8] {'tile'}, dimensions={0} | all-to-all | bytes 1048576 | tf_op jit(solution)/shard_map/all_to_all | solution.py:512
  25.7 9.8 %mix_forward.1 = (bf16[1024,128]{1,0:T(8,128)(2,1)}, bf16[256,1024]{1,0:T(8,128)(2,1)}) custom-call(bf16[128,2048]{1,0:T(8,128)(2,1)} %bitcast.29, bf16[128,128]{1,0:T(8,128)(2,1)} %constant.32.rest_1_.order_ref, bf16[256,128]{1,0:T(8,128)(2,1)} %constant.33.rest_2_.rows_ref, bf16[256,128]{1,0:T(8,128)(2,1)} %constant.34.rest_3_.rest_1_, ...), custom_call_target="tpu_custom_call" | custom-call | tf_op jit(solution)/shard_map/mix_forward/pallas_call | solution.py:444
  35.5 3.6 %all-to-all-start.1 = ((bf16[8,32,1024]{2,1,0:T(8,128)(2,1)}), bf16[8,32,1024]{2,1,0:T(8,128)(2,1)S(1)}, u32[]{:S(2)}, u32[]{:S(2)}) async-start(bf16[8,32,1024]{2,1,0:T(8,128)(2,1)} %bitcast.30), calls=%async_computation.1 | async-start | bytes 1048576 | tf_op jit(solution)/shard_map/all_to_all | solution.py:512
  39.1 1.5 %collective-permute-start.1 = (bf16[1024,128]{1,0:T(8,128)(2,1)}, bf16[1024,128]{1,0:T(8,128)(2,1)S(1)}, u32[]{:S(2)}, u32[]{:S(2)}) collective-permute-start(bf16[1024,128]{1,0:T(8,128)(2,1)} %get-tuple-element.35.refs_0_), channel_id=1, source_target_pairs={{0,16},{8,24},{16,0},{24,8},{1,17},{9,25},{17,1},{25,9},{2,18},{10... | collective-permute-start | bytes 786440 | tf_op jit(solution)/shard_map/ppermute | solution.py:457
  40.7 0.0 collective-permute-start
  40.7 6.1 %collective-permute-done.1.refs_2_ = bf16[1024,128]{1,0:T(8,128)(2,1)S(1)} collective-permute-done((bf16[1024,128]{1,0:T(8,128)(2,1)}, bf16[1024,128]{1,0:T(8,128)(2,1)S(1)}, u32[]{:S(2)}, u32[]{:S(2)}) %collective-permute-start.1) | collective-permute-done | bytes 262176 | tf_op jit(solution)/shard_map/ppermute | solution.py:457
  46.8 0.0 collective-permute-start.2
  46.8 0.8 copy.15
  47.6 2.6 %relayout.1.cot_ref = bf16[16,128,256]{2,1,0:T(8,128)(2,1)} custom-call(bf16[256,256]{1,0:T(8,128)(2,1)} %constant.30.order_ref.restore_ref, bf16[2048,256]{1,0:T(8,128)(2,1)} %bitcast.24, bf16[2048,256]{1,0:T(8,128)(2,1)} %bitcast.25, bf16[2048,256]{1,0:T(8,128)(2,1)} %bitcast.26, bf16[2048,256]{1,0:T(8,128)(2,1)} %bitcast.27), custom_call_target="tpu_custom_call" | custom-call | tf_op jit(solution)/shard_map/relayout/pallas_call | solution.py:444
  50.2 0.1 fusion.4.local_ref
  50.3 3.0 %all-to-all-done.1 = bf16[8,32,1024]{2,1,0:T(8,128)(2,1)S(1)} async-done(((bf16[8,32,1024]{2,1,0:T(8,128)(2,1)}), bf16[8,32,1024]{2,1,0:T(8,128)(2,1)S(1)}, u32[]{:S(2)}, u32[]{:S(2)}) %all-to-all-start.1) | async-done | bytes 524320 | tf_op jit(solution)/shard_map/all_to_all | solution.py:512
  53.3 0.0 copy-done.1
  53.3 0.0 copy-start
  53.3 1.2 %copy-done = bf16[16,128,256]{2,1,0:T(8,128)(2,1)S(1)} copy-done((bf16[16,128,256]{2,1,0:T(8,128)(2,1)S(1)}, bf16[16,128,256]{2,1,0:T(8,128)(2,1)}, u32[]{:S(2)}) %copy-start) | copy-done | bytes 1048600
  54.6 6.6 %pixels.1 = (bf16[16,128,256]{2,1,0:T(8,128)(2,1)S(1)}, bf16[128,2048]{1,0:T(8,128)(2,1)}, f32[64,64]{1,0:T(8,128)S(1)}) custom-call(bf16[256,1024]{1,0:T(8,128)(2,1)S(1)} %bitcast.16, bf16[256,256]{1,0:T(8,128)(2,1)S(1)} %copy-done.1, bf16[128,256]{1,0:T(8,128)(2,1)S(1)} %copy-done.6, bf16[128,128]{1,0:T(8,128)(2,1)S(1)} %fusion.4.local_ref, ...), custom_call_target="tpu_custom_call" | custom-call | tf_op jit(solution)/shard_map/pixels/pallas_call | solution.py:444
  61.2 0.0 collective-permute-done.refs_1_
  61.2 0.0 collective-permute-done.2.refs_3_
  61.2 3.6 %all-to-all-start.2 = ((bf16[8,16,2048]{2,1,0:T(8,128)(2,1)}), bf16[8,16,2048]{2,1,0:T(8,128)(2,1)S(1)}, u32[]{:S(2)}, u32[]{:S(2)}) async-start(bf16[8,16,2048]{2,1,0:T(8,128)(2,1)} %bitcast.8), calls=%async_computation.2 | async-start | bytes 1048576 | tf_op jit(solution)/shard_map/all_to_all | solution.py:512
  64.9 0.0 collective-permute-start.3
  64.9 1.2 %collective-permute-done.3 = f32[64,64]{1,0:T(8,128)S(1)} collective-permute-done((f32[64,64]{1,0:T(8,128)S(1)}, f32[64,64]{1,0:T(8,128)S(1)}, u32[]{:S(2)}, u32[]{:S(2)}) %collective-permute-start.3) | collective-permute-done | bytes 16416 | tf_op jit(solution)/shard_map/ppermute | solution.py:457
  66.1 1.5 %collective-permute-start.4 = (f32[64,64]{1,0:T(8,128)S(1)}, f32[64,64]{1,0:T(8,128)S(1)}, u32[]{:S(2)}, u32[]{:S(2)}) collective-permute-start(f32[64,64]{1,0:T(8,128)S(1)} %add.14), channel_id=1, source_target_pairs={{0,16},{8,24},{16,0},{24,8},{1,17},{9,25},{17,1},{25,9},{2,18},{10... | collective-permute-start | bytes 49160 | tf_op jit(solution)/shard_map/ppermute | solution.py:457
  67.6 2.4 %collective-permute-done.4 = f32[64,64]{1,0:T(8,128)S(1)} collective-permute-done((f32[64,64]{1,0:T(8,128)S(1)}, f32[64,64]{1,0:T(8,128)S(1)}, u32[]{:S(2)}, u32[]{:S(2)}) %collective-permute-start.4) | collective-permute-done | bytes 16416 | tf_op jit(solution)/shard_map/ppermute | solution.py:457
  70.0 0.6 add.15.rest_2_
  70.6 8.7 %all-to-all-done.2 = bf16[8,16,2048]{2,1,0:T(8,128)(2,1)S(1)} async-done(((bf16[8,16,2048]{2,1,0:T(8,128)(2,1)}), bf16[8,16,2048]{2,1,0:T(8,128)(2,1)S(1)}, u32[]{:S(2)}, u32[]{:S(2)}) %all-to-all-start.2) | async-done | bytes 524320 | tf_op jit(solution)/shard_map/all_to_all | solution.py:512
  79.3 0.0 copy-done.7
  79.3 0.6 grad_spectra.1.rest_0_.refs_4_
  79.9 0.0 copy-start.2
  79.9 0.1 collective-permute-start.5
  80.0 1.6 %collective-permute-start.6 = (bf16[1024,128]{1,0:T(8,128)(2,1)S(1)}, bf16[1024,128]{1,0:T(8,128)(2,1)S(1)}, u32[]{:S(2)}, u32[]{:S(2)}) collective-permute-start(bf16[1024,128]{1,0:T(8,128)(2,1)S(1)} %grad_spectra.1.rest_0_.refs_4_), channel_id=1, source_target_pairs={{0,16},{8,24},{16,0},{24,8},{1,17},{9,25},{17,1},{25,9},{2,18},{10... | collective-permute-start | bytes 786440 | tf_op jit(solution)/shard_map/ppermute | solution.py:457
  81.6 9.2 %mix_backward.1 = bf16[256,1152]{1,0:T(8,128)(2,1)} custom-call(bf16[1024,128]{1,0:T(8,128)(2,1)} %copy-done.2, bf16[256,128]{1,0:T(8,128)(2,1)} %constant.34.rest_3_.rest_1_, f32[64,64]{1,0:T(8,128)} %add.15.rest_2_, bf16[32768,128]{1,0:T(8,128)(2,1)} %bitcast.18), custom_call_target="tpu_custom_call" | custom-call | tf_op jit(solution)/shard_map/mix_backward/pallas_call | solution.py:444
  90.8 0.0 collective-permute-done.5.refs_5_
  90.8 0.0 collective-permute-done.6.refs_6_
  90.8 0.0 copy-start.10
  90.8 3.6 %all-to-all-start.3 = ((bf16[8,32,1152]{2,1,0:T(8,128)(2,1)}), bf16[8,32,1152]{2,1,0:T(8,128)(2,1)S(1)}, u32[]{:S(2)}, u32[]{:S(2)}) async-start(bf16[8,32,1152]{2,1,0:T(8,128)(2,1)} %bitcast.28), calls=%async_computation.3 | async-start | bytes 1179648 | tf_op jit(solution)/shard_map/all_to_all | solution.py:512
  94.5 0.1 collective-permute-start.7
  94.6 0.1 fusion.5.local_ref
  94.7 1.3 %collective-permute-done.7.refs_7_ = bf16[1024,128]{1,0:T(8,128)(2,1)S(1)} collective-permute-done((bf16[1024,128]{1,0:T(8,128)(2,1)S(1)}, bf16[1024,128]{1,0:T(8,128)(2,1)S(1)}, u32[]{:S(2)}, u32[]{:S(2)}) %collective-permute-start.7) | collective-permute-done | bytes 262176 | tf_op jit(solution)/shard_map/ppermute | solution.py:457
  96.0 0.0 copy-start.11
  96.0 0.7 copy-done.11
  96.7 16.4 %mode_grad.1 = f32[32768,128]{1,0:T(8,128)} custom-call(bf16[1024,128]{1,0:T(8,128)(2,1)} %get-tuple-element.35.refs_0_, bf16[1024,128]{1,0:T(8,128)(2,1)} %collective-permute-done.refs_1_, bf16[1024,128]{1,0:T(8,128)(2,1)} %copy-done.8, bf16[1024,128]{1,0:T(8,128)(2,1)} %collective-permute-done.2.refs_3_, bf16[1024,128]{1,0:T(8,128)(2,1)} %copy-done.2, ...), custom_call_target="tpu_custom_call" | custom-call | tf_op jit(solution)/shard_map/mode_grad/pallas_call | solution.py:444
  113.1 0.0 all-to-all-done.3
  113.1 2.3 %final.1 = (bf16[2048,256]{1,0:T(8,128)(2,1)}, f32[64,64]{1,0:T(8,128)}) custom-call(bf16[256,1152]{1,0:T(8,128)(2,1)S(1)} %bitcast.14, bf16[256,256]{1,0:T(8,128)(2,1)S(1)} %copy-done.1, bf16[128,256]{1,0:T(8,128)(2,1)S(1)} %copy-done.6, bf16[128,128]{1,0:T(8,128)(2,1)S(1)} %fusion.5.local_ref, bf16[16,128,256]{2,1,0:T(8,128)(2,1)S(1)} %get-tuple-element.43.grad_ref, ...), custom_call_target="tpu_custom_call" | custom-call | tf_op jit(solution)/shard_map/final/pallas_call | solution.py:444
  (14 shorter events, 0.0 us)
Async XLA Ops:
  0.6 52.7 %copy-start.1 = (bf16[256,256]{1,0:T(8,128)(2,1)S(1)}, bf16[256,256]{1,0:T(8,128)(2,1)}, u32[]{:S(2)}) copy-start(bf16[256,256]{1,0:T(8,128)(2,1)} %constant.30.order_ref.restore_ref) | copy-start | bytes 393220
  0.6 52.7 %copy-start.5 = (bf16[128,256]{1,0:T(8,128)(2,1)S(1)}, bf16[128,256]{1,0:T(8,128)(2,1)}, u32[]{:S(2)}) copy-start(bf16[128,256]{1,0:T(8,128)(2,1)} %constant.31.table_ref) | copy-start | bytes 196612
  0.7 78.6 %copy-start.7 = (bf16[128,128]{1,0:T(8,128)(2,1)S(1)}, bf16[128,128]{1,0:T(8,128)(2,1)}, u32[]{:S(2)}) copy-start(bf16[128,128]{1,0:T(8,128)(2,1)} %constant.32.rest_1_.order_ref) | copy-start | bytes 98308
  0.7 78.6 %copy-start.4 = (bf16[256,128]{1,0:T(8,128)(2,1)S(1)}, bf16[256,128]{1,0:T(8,128)(2,1)}, u32[]{:S(2)}) copy-start(bf16[256,128]{1,0:T(8,128)(2,1)} %constant.33.rest_2_.rows_ref) | copy-start | bytes 196612
  0.7 52.6 %copy-start.6 = (bf16[128,256]{1,0:T(8,128)(2,1)S(1)}, bf16[128,256]{1,0:T(8,128)(2,1)}, u32[]{:S(2)}) copy-start(bf16[128,256]{1,0:T(8,128)(2,1)} %constant.35.back_ref) | copy-start | bytes 196612
  3.6 49.7 %copy-start.3 = (bf16[16,128,256]{2,1,0:T(8,128)(2,1)S(1)}, bf16[16,128,256]{2,1,0:T(8,128)(2,1)}, u32[]{:S(2)}) copy-start(bf16[16,128,256]{2,1,0:T(8,128)(2,1)} %get-tuple-element.27.field_ref) | copy-start | bytes 3145732
  3.7 91.0 %copy-start.12 = (bf16[64,64]{1,0:T(8,128)(2,1)S(1)}, bf16[64,64]{1,0:T(8,128)(2,1)}, u32[]{:S(2)}) copy-start(bf16[64,64]{1,0:T(8,128)(2,1)} %param.15) | copy-start | bytes 24580
  35.5 17.8 %all-to-all-start.1 = ((bf16[8,32,1024]{2,1,0:T(8,128)(2,1)}), bf16[8,32,1024]{2,1,0:T(8,128)(2,1)S(1)}, u32[]{:S(2)}, u32[]{:S(2)}) async-start(bf16[8,32,1024]{2,1,0:T(8,128)(2,1)} %bitcast.30), calls=%async_computation.1 | async-start | bytes 1048576 | tf_op jit(solution)/shard_map/all_to_all | solution.py:512
  39.1 7.6 %collective-permute-start.1 = (bf16[1024,128]{1,0:T(8,128)(2,1)}, bf16[1024,128]{1,0:T(8,128)(2,1)S(1)}, u32[]{:S(2)}, u32[]{:S(2)}) collective-permute-start(bf16[1024,128]{1,0:T(8,128)(2,1)} %get-tuple-element.35.refs_0_), channel_id=1, source_target_pairs={{0,16},{8,24},{16,0},{24,8},{1,17},{9,25},{17,1},{25,9},{2,18},{10... | collective-permute-start | bytes 786440 | tf_op jit(solution)/shard_map/ppermute | solution.py:457
  40.7 20.5 %collective-permute-start = (bf16[1024,128]{1,0:T(8,128)(2,1)}, bf16[1024,128]{1,0:T(8,128)(2,1)}, u32[]{:S(2)}, u32[]{:S(2)}) collective-permute-start(bf16[1024,128]{1,0:T(8,128)(2,1)} %get-tuple-element.35.refs_0_), channel_id=1, source_target_pairs={{0,8},{8,0},{16,24},{24,16},{1,9},{9,1},{17,25},{25,17},{2,10},{10... | collective-permute-start | bytes 786440 | tf_op jit(solution)/shard_map/ppermute | solution.py:457
  46.8 49.3 %copy-start.8 = (bf16[1024,128]{1,0:T(8,128)(2,1)}, bf16[1024,128]{1,0:T(8,128)(2,1)S(1)}, u32[]{:S(2)}) copy-start(bf16[1024,128]{1,0:T(8,128)(2,1)S(1)} %collective-permute-done.1.refs_2_) | copy-start | bytes 786436
  46.8 14.5 %collective-permute-start.2 = (bf16[1024,128]{1,0:T(8,128)(2,1)S(1)}, bf16[1024,128]{1,0:T(8,128)(2,1)}, u32[]{:S(2)}, u32[]{:S(2)}) collective-permute-start(bf16[1024,128]{1,0:T(8,128)(2,1)S(1)} %collective-permute-done.1.refs_2_), channel_id=1, source_target_pairs={{0,8},{8,0},{16,24},{24,16},{1,9},{9,1},{17,25},{25,17},{2,10},{10... | collective-permute-start | bytes 786440 | tf_op jit(solution)/shard_map/ppermute | solution.py:457
  53.3 1.2 %copy-start = (bf16[16,128,256]{2,1,0:T(8,128)(2,1)S(1)}, bf16[16,128,256]{2,1,0:T(8,128)(2,1)}, u32[]{:S(2)}) copy-start(bf16[16,128,256]{2,1,0:T(8,128)(2,1)} %relayout.1.cot_ref) | copy-start | bytes 3145732
  61.2 18.1 %all-to-all-start.2 = ((bf16[8,16,2048]{2,1,0:T(8,128)(2,1)}), bf16[8,16,2048]{2,1,0:T(8,128)(2,1)S(1)}, u32[]{:S(2)}, u32[]{:S(2)}) async-start(bf16[8,16,2048]{2,1,0:T(8,128)(2,1)} %bitcast.8), calls=%async_computation.2 | async-start | bytes 1048576 | tf_op jit(solution)/shard_map/all_to_all | solution.py:512
  64.9 1.2 %collective-permute-start.3 = (f32[64,64]{1,0:T(8,128)S(1)}, f32[64,64]{1,0:T(8,128)S(1)}, u32[]{:S(2)}, u32[]{:S(2)}) collective-permute-start(f32[64,64]{1,0:T(8,128)S(1)} %get-tuple-element.31), channel_id=1, source_target_pairs={{0,8},{8,0},{16,24},{24,16},{1,9},{9,1},{17,25},{25,17},{2,10},{10... | collective-permute-start | bytes 49160 | tf_op jit(solution)/shard_map/ppermute | solution.py:457
  66.1 3.9 %collective-permute-start.4 = (f32[64,64]{1,0:T(8,128)S(1)}, f32[64,64]{1,0:T(8,128)S(1)}, u32[]{:S(2)}, u32[]{:S(2)}) collective-permute-start(f32[64,64]{1,0:T(8,128)S(1)} %add.14), channel_id=1, source_target_pairs={{0,16},{8,24},{16,0},{24,8},{1,17},{9,25},{17,1},{25,9},{2,18},{10... | collective-permute-start | bytes 49160 | tf_op jit(solution)/shard_map/ppermute | solution.py:457
  79.9 1.7 %copy-start.2 = (bf16[1024,128]{1,0:T(8,128)(2,1)}, bf16[1024,128]{1,0:T(8,128)(2,1)S(1)}, u32[]{:S(2)}) copy-start(bf16[1024,128]{1,0:T(8,128)(2,1)S(1)} %grad_spectra.1.rest_0_.refs_4_) | copy-start | bytes 786436
  79.9 10.9 %collective-permute-start.5 = (bf16[1024,128]{1,0:T(8,128)(2,1)S(1)}, bf16[1024,128]{1,0:T(8,128)(2,1)S(1)}, u32[]{:S(2)}, u32[]{:S(2)}) collective-permute-start(bf16[1024,128]{1,0:T(8,128)(2,1)S(1)} %grad_spectra.1.rest_0_.refs_4_), channel_id=1, source_target_pairs={{0,8},{8,0},{16,24},{24,16},{1,9},{9,1},{17,25},{25,17},{2,10},{10... | collective-permute-start | bytes 786440 | tf_op jit(solution)/shard_map/ppermute | solution.py:457
  80.0 10.8 %collective-permute-start.6 = (bf16[1024,128]{1,0:T(8,128)(2,1)S(1)}, bf16[1024,128]{1,0:T(8,128)(2,1)S(1)}, u32[]{:S(2)}, u32[]{:S(2)}) collective-permute-start(bf16[1024,128]{1,0:T(8,128)(2,1)S(1)} %grad_spectra.1.rest_0_.refs_4_), channel_id=1, source_target_pairs={{0,16},{8,24},{16,0},{24,8},{1,17},{9,25},{17,1},{25,9},{2,18},{10... | collective-permute-start | bytes 786440 | tf_op jit(solution)/shard_map/ppermute | solution.py:457
  90.8 5.2 %copy-start.9 = (bf16[1024,128]{1,0:T(8,128)(2,1)}, bf16[1024,128]{1,0:T(8,128)(2,1)S(1)}, u32[]{:S(2)}) copy-start(bf16[1024,128]{1,0:T(8,128)(2,1)S(1)} %collective-permute-done.5.refs_5_) | copy-start | bytes 786436
  90.8 5.2 %copy-start.10 = (bf16[1024,128]{1,0:T(8,128)(2,1)}, bf16[1024,128]{1,0:T(8,128)(2,1)S(1)}, u32[]{:S(2)}) copy-start(bf16[1024,128]{1,0:T(8,128)(2,1)S(1)} %collective-permute-done.6.refs_6_) | copy-start | bytes 786436
  90.8 22.3 %all-to-all-start.3 = ((bf16[8,32,1152]{2,1,0:T(8,128)(2,1)}), bf16[8,32,1152]{2,1,0:T(8,128)(2,1)S(1)}, u32[]{:S(2)}, u32[]{:S(2)}) async-start(bf16[8,32,1152]{2,1,0:T(8,128)(2,1)} %bitcast.28), calls=%async_computation.3 | async-start | bytes 1179648 | tf_op jit(solution)/shard_map/all_to_all | solution.py:512
  94.5 1.6 %collective-permute-start.7 = (bf16[1024,128]{1,0:T(8,128)(2,1)S(1)}, bf16[1024,128]{1,0:T(8,128)(2,1)S(1)}, u32[]{:S(2)}, u32[]{:S(2)}) collective-permute-start(bf16[1024,128]{1,0:T(8,128)(2,1)S(1)} %collective-permute-done.6.refs_6_), channel_id=1, source_target_pairs={{0,8},{8,0},{16,24},{24,16},{1,9},{9,1},{17,25},{25,17},{2,10},{10... | collective-permute-start | bytes 786440 | tf_op jit(solution)/shard_map/ppermute | solution.py:457
  96.0 0.7 copy-start.11

commit v4 on v3

--- a/solution.py
+++ b/solution.py
@@ -542,7 +542,6 @@
         (field_shape, to_modes),
         blocks=field_blocks(2),
     )
-    arrived = exchange(send)
     (cot_rows,) = call(
         relayout_kernel,
         "relayout",
@@ -550,6 +549,7 @@
         (field_shape,),
         blocks=field_blocks(1),
     )
+    arrived, cot_rows = lax.optimization_barrier((exchange(send), cot_rows))
     spectra, send = call(
         functools.partial(forward_kernel, spec_scale, samples, owned),
         "mix_forward",
@@ -613,7 +613,7 @@
         out_blocks={0: in_place},
     )
     send, near = lax.optimization_barrier((send, near))
-    all_grads = gather_far(near, "dp")
+    send, *all_grads = lax.optimization_barrier((send, *gather_far(near, "dp")))
     arrived = exchange(send)
 
     groups = lax.axis_size("dp")

time: 116 us -> 117 us (level)
  blocking collectives: 22 us -> 0 us
  waiting for transfers between devices: 22.7 us -> 38.7 us
  starting transfers between devices: 15.7 us -> 23.2 us
    all_to_all x1 -> x0, blocking collectives: 22 us -> none  [exchange(): lax.all_to_all(split, 'tile', split_axis=0, concat_axis=0, tiled=False)]
    all_to_all x3 -> x4, waiting for transfers between devices: 11.7 us -> 27.1 us  [exchange(): lax.all_to_all(split, 'tile', split_axis=0, concat_axis=0, tiled=False)]
    all_to_all x3 -> x4, starting transfers between devices: 10.9 us -> 18.3 us  [exchange(): lax.all_to_all(split, 'tile', split_axis=0, concat_axis=0, tiled=False)]
    unnamed x27 -> x29, local copies, waits for them, and re-layouts: 2.78 us -> 2.18 us
  transfers between devices with their start and end apart: 11 -> 12, of which waited for: 6 -> 7; matrix products, arithmetic and copies ran while one was open for 1% -> 1% of each run, Pallas kernels for 30% -> 30%
where the time goes in v4:
time: 117 us; the launch traced here: 116 us
  Pallas kernels  50.5 us (43%)
  waiting for transfers between devices  38.7 us (33%)
  starting transfers between devices  23.2 us (20%)
  local copies, waits for them, and re-layouts  2.18 us (2%)
    pallas_call x8, Pallas kernels, call(): pl.pallas_call(kernel, out_shape=tuple(outs), grid=grid, in_specs=in_spec...  50.5 us
    all_to_all x4, waiting for transfers between devices, exchange(): lax.all_to_all(split, 'tile', split_axis=0, concat_axis=0, tiled=False)  27.1 us
    all_to_all x4, starting transfers between devices, exchange(): lax.all_to_all(split, 'tile', split_axis=0, concat_axis=0, tiled=False)  18.3 us
    ppermute x8, waiting for transfers between devices, swap(): lax.ppermute(values, axis, [(i, i ^ step) for i in range(lax.axis_size(ax...  11.6 us
    ppermute x8, starting transfers between devices, swap(): lax.ppermute(values, axis, [(i, i ^ step) for i in range(lax.axis_size(ax...  4.93 us
  transfers between devices with their start and end apart: 12, of which 7 were waited for; matrix products, arithmetic and copies ran while one was open for 1% of the time, Pallas kernels for 30%

profile of v4, /device:TPU:0, one launch (start us, length us, event | category | flops | bytes accessed | tf_op | source)
XLA Modules:
  0.0 116.3 jit_solution(3692660920308859835)
XLA Ops:
  0.6 0.0 copy-start.1
  0.6 0.0 copy-start.5
  0.7 0.0 copy-start.7
  0.7 0.0 copy-start.4
  0.7 0.0 copy-start.6
  0.7 3.0 %columns.1 = (bf16[16,128,256]{2,1,0:T(8,128)(2,1)}, bf16[128,2048]{1,0:T(8,128)(2,1)}) custom-call(bf16[256,256]{1,0:T(8,128)(2,1)} %constant.30.order_ref.restore_ref, bf16[128,256]{1,0:T(8,128)(2,1)} %constant.31.table_ref, bf16[2048,256]{1,0:T(8,128)(2,1)} %bitcast.20, bf16[2048,256]{1,0:T(8,128)(2,1)} %bitcast.21, bf16[2048,256]{1,0:T(8,128)(2,1)} %bitcast.22, ...), custom_call_target="tpu_custom_call" | custom-call | tf_op jit(solution)/shard_map/columns/pallas_call | solution.py:444
  3.7 7.4 %all-to-all-start = ((bf16[8,16,2048]{2,1,0:T(8,128)(2,1)}), bf16[8,16,2048]{2,1,0:T(8,128)(2,1)S(1)}, u32[]{:S(2)}, u32[]{:S(2)}) async-start(bf16[8,16,2048]{2,1,0:T(8,128)(2,1)} %bitcast.31), calls=%async_computation | async-start | bytes 1048576 | tf_op jit(solution)/shard_map/all_to_all | solution.py:512
  11.0 2.6 %relayout.1.cot_ref = bf16[16,128,256]{2,1,0:T(8,128)(2,1)} custom-call(bf16[256,256]{1,0:T(8,128)(2,1)} %constant.30.order_ref.restore_ref, bf16[2048,256]{1,0:T(8,128)(2,1)} %bitcast.24, bf16[2048,256]{1,0:T(8,128)(2,1)} %bitcast.25, bf16[2048,256]{1,0:T(8,128)(2,1)} %bitcast.26, bf16[2048,256]{1,0:T(8,128)(2,1)} %bitcast.27), custom_call_target="tpu_custom_call" | custom-call | tf_op jit(solution)/shard_map/relayout/pallas_call | solution.py:444
  13.7 11.9 %all-to-all-done = bf16[8,16,2048]{2,1,0:T(8,128)(2,1)S(1)} async-done(((bf16[8,16,2048]{2,1,0:T(8,128)(2,1)}), bf16[8,16,2048]{2,1,0:T(8,128)(2,1)S(1)}, u32[]{:S(2)}, u32[]{:S(2)}) %all-to-all-start) | async-done | bytes 524320 | tf_op jit(solution)/shard_map/all_to_all | solution.py:512
  25.5 0.8 copy-done.8
  26.3 9.8 %mix_forward.1 = (bf16[1024,128]{1,0:T(8,128)(2,1)}, bf16[256,1024]{1,0:T(8,128)(2,1)}) custom-call(bf16[128,2048]{1,0:T(8,128)(2,1)} %bitcast.29, bf16[128,128]{1,0:T(8,128)(2,1)} %constant.32.rest_1_.order_ref, bf16[256,128]{1,0:T(8,128)(2,1)} %constant.33.rest_2_.rows_ref, bf16[256,128]{1,0:T(8,128)(2,1)} %constant.34.rest_3_.rest_1_, ...), custom_call_target="tpu_custom_call" | custom-call | tf_op jit(solution)/shard_map/mix_forward/pallas_call | solution.py:444
  36.2 3.6 %all-to-all-start.1 = ((bf16[8,32,1024]{2,1,0:T(8,128)(2,1)}), bf16[8,32,1024]{2,1,0:T(8,128)(2,1)S(1)}, u32[]{:S(2)}, u32[]{:S(2)}) async-start(bf16[8,32,1024]{2,1,0:T(8,128)(2,1)} %bitcast.30), calls=%async_computation.1 | async-start | bytes 1048576 | tf_op jit(solution)/shard_map/all_to_all | solution.py:512
  39.8 1.5 %collective-permute-start.1 = (bf16[1024,128]{1,0:T(8,128)(2,1)}, bf16[1024,128]{1,0:T(8,128)(2,1)S(1)}, u32[]{:S(2)}, u32[]{:S(2)}) collective-permute-start(bf16[1024,128]{1,0:T(8,128)(2,1)} %get-tuple-element.48.refs_0_), channel_id=1, source_target_pairs={{0,16},{8,24},{16,0},{24,8},{1,17},{9,25},{17,1},{25,9},{2,18},{10... | collective-permute-start | bytes 786440 | tf_op jit(solution)/shard_map/ppermute | solution.py:457
  41.3 0.0 collective-permute-start
  41.3 6.6 %collective-permute-done.1.refs_2_ = bf16[1024,128]{1,0:T(8,128)(2,1)S(1)} collective-permute-done((bf16[1024,128]{1,0:T(8,128)(2,1)}, bf16[1024,128]{1,0:T(8,128)(2,1)S(1)}, u32[]{:S(2)}, u32[]{:S(2)}) %collective-permute-start.1) | collective-permute-done | bytes 262176 | tf_op jit(solution)/shard_map/ppermute | solution.py:457
  48.0 0.0 collective-permute-start.2
  48.0 0.1 copy.15
  48.1 0.1 fusion.4.local_ref
  48.2 6.3 %all-to-all-done.1 = bf16[8,32,1024]{2,1,0:T(8,128)(2,1)S(1)} async-done(((bf16[8,32,1024]{2,1,0:T(8,128)(2,1)}), bf16[8,32,1024]{2,1,0:T(8,128)(2,1)S(1)}, u32[]{:S(2)}, u32[]{:S(2)}) %all-to-all-start.1) | async-done | bytes 524320 | tf_op jit(solution)/shard_map/all_to_all | solution.py:512
  54.5 0.0 copy-done.5
  54.5 0.0 copy-start
  54.5 1.2 %copy-done = bf16[16,128,256]{2,1,0:T(8,128)(2,1)S(1)} copy-done((bf16[16,128,256]{2,1,0:T(8,128)(2,1)S(1)}, bf16[16,128,256]{2,1,0:T(8,128)(2,1)}, u32[]{:S(2)}) %copy-start) | copy-done | bytes 1048600
  55.7 6.6 %pixels.1 = (bf16[16,128,256]{2,1,0:T(8,128)(2,1)S(1)}, bf16[128,2048]{1,0:T(8,128)(2,1)}, f32[64,64]{1,0:T(8,128)S(1)}) custom-call(bf16[256,1024]{1,0:T(8,128)(2,1)S(1)} %bitcast.16, bf16[256,256]{1,0:T(8,128)(2,1)S(1)} %copy-done.1, bf16[128,256]{1,0:T(8,128)(2,1)S(1)} %copy-done.6, bf16[128,128]{1,0:T(8,128)(2,1)S(1)} %fusion.4.local_ref, ...), custom_call_target="tpu_custom_call" | custom-call | tf_op jit(solution)/shard_map/pixels/pallas_call | solution.py:444
  62.4 0.0 collective-permute-done.refs_1_
  62.4 0.0 collective-permute-done.2.refs_3_
  62.4 3.6 %all-to-all-start.2 = ((bf16[8,16,2048]{2,1,0:T(8,128)(2,1)}), bf16[8,16,2048]{2,1,0:T(8,128)(2,1)S(1)}, u32[]{:S(2)}, u32[]{:S(2)}) async-start(bf16[8,16,2048]{2,1,0:T(8,128)(2,1)} %bitcast.8), calls=%async_computation.2 | async-start | bytes 1048576 | tf_op jit(solution)/shard_map/all_to_all | solution.py:512
  66.0 0.0 collective-permute-start.3
  66.0 1.2 %collective-permute-done.3 = f32[64,64]{1,0:T(8,128)S(1)} collective-permute-done((f32[64,64]{1,0:T(8,128)S(1)}, f32[64,64]{1,0:T(8,128)S(1)}, u32[]{:S(2)}, u32[]{:S(2)}) %collective-permute-start.3) | collective-permute-done | bytes 16416 | tf_op jit(solution)/shard_map/ppermute | solution.py:457
  67.2 1.5 %collective-permute-start.4 = (f32[64,64]{1,0:T(8,128)S(1)}, f32[64,64]{1,0:T(8,128)S(1)}, u32[]{:S(2)}, u32[]{:S(2)}) collective-permute-start(f32[64,64]{1,0:T(8,128)S(1)} %add.14), channel_id=1, source_target_pairs={{0,16},{8,24},{16,0},{24,8},{1,17},{9,25},{17,1},{25,9},{2,18},{10... | collective-permute-start | bytes 49160 | tf_op jit(solution)/shard_map/ppermute | solution.py:457
  68.8 2.4 %collective-permute-done.4 = f32[64,64]{1,0:T(8,128)S(1)} collective-permute-done((f32[64,64]{1,0:T(8,128)S(1)}, f32[64,64]{1,0:T(8,128)S(1)}, u32[]{:S(2)}, u32[]{:S(2)}) %collective-permute-start.4) | collective-permute-done | bytes 16416 | tf_op jit(solution)/shard_map/ppermute | solution.py:457
  71.2 0.6 add.15.rest_2_
  71.8 8.9 %all-to-all-done.2 = bf16[8,16,2048]{2,1,0:T(8,128)(2,1)S(1)} async-done(((bf16[8,16,2048]{2,1,0:T(8,128)(2,1)}), bf16[8,16,2048]{2,1,0:T(8,128)(2,1)S(1)}, u32[]{:S(2)}, u32[]{:S(2)}) %all-to-all-start.2) | async-done | bytes 524320 | tf_op jit(solution)/shard_map/all_to_all | solution.py:512
  80.7 0.6 grad_spectra.1.rest_0_.refs_4_
  81.3 0.0 copy-start.2
  81.3 0.1 collective-permute-start.5
  81.4 1.6 %collective-permute-start.6 = (bf16[1024,128]{1,0:T(8,128)(2,1)S(1)}, bf16[1024,128]{1,0:T(8,128)(2,1)S(1)}, u32[]{:S(2)}, u32[]{:S(2)}) collective-permute-start(bf16[1024,128]{1,0:T(8,128)(2,1)S(1)} %grad_spectra.1.rest_0_.refs_4_), channel_id=1, source_target_pairs={{0,16},{8,24},{16,0},{24,8},{1,17},{9,25},{17,1},{25,9},{2,18},{10... | collective-permute-start | bytes 786440 | tf_op jit(solution)/shard_map/ppermute | solution.py:457
  83.0 0.0 copy-done.2
  83.0 9.2 %mix_backward.1 = bf16[256,1152]{1,0:T(8,128)(2,1)} custom-call(bf16[1024,128]{1,0:T(8,128)(2,1)} %copy-done.2, bf16[256,128]{1,0:T(8,128)(2,1)} %constant.34.rest_3_.rest_1_, f32[64,64]{1,0:T(8,128)} %add.15.rest_2_, bf16[32768,128]{1,0:T(8,128)(2,1)} %bitcast.18), custom_call_target="tpu_custom_call" | custom-call | tf_op jit(solution)/shard_map/mix_backward/pallas_call | solution.py:444
  92.2 0.0 collective-permute-done.5.refs_5_
  92.2 0.0 copy-start.10
  92.2 0.0 collective-permute-done.6.refs_6_
  92.2 0.2 collective-permute-start.7
  92.4 1.4 %collective-permute-done.7.refs_7_ = bf16[1024,128]{1,0:T(8,128)(2,1)S(1)} collective-permute-done((bf16[1024,128]{1,0:T(8,128)(2,1)S(1)}, bf16[1024,128]{1,0:T(8,128)(2,1)S(1)}, u32[]{:S(2)}, u32[]{:S(2)}) %collective-permute-start.7) | collective-permute-done | bytes 262176 | tf_op jit(solution)/shard_map/ppermute | solution.py:457
  93.8 3.6 %all-to-all-start.3 = ((bf16[8,32,1152]{2,1,0:T(8,128)(2,1)}), bf16[8,32,1152]{2,1,0:T(8,128)(2,1)S(1)}, u32[]{:S(2)}, u32[]{:S(2)}) async-start(bf16[8,32,1152]{2,1,0:T(8,128)(2,1)} %bitcast.28), calls=%async_computation.3 | async-start | bytes 1179648 | tf_op jit(solution)/shard_map/all_to_all | solution.py:512
  97.4 0.1 fusion.5.local_ref
  97.6 16.4 %mode_grad.1 = f32[32768,128]{1,0:T(8,128)} custom-call(bf16[1024,128]{1,0:T(8,128)(2,1)} %get-tuple-element.48.refs_0_, bf16[1024,128]{1,0:T(8,128)(2,1)} %collective-permute-done.refs_1_, bf16[1024,128]{1,0:T(8,128)(2,1)} %copy-done.9, bf16[1024,128]{1,0:T(8,128)(2,1)} %collective-permute-done.2.refs_3_, bf16[1024,128]{1,0:T(8,128)(2,1)} %copy-done.2, ...), custom_call_target="tpu_custom_call" | custom-call | tf_op jit(solution)/shard_map/mode_grad/pallas_call | solution.py:444
  114.0 0.0 all-to-all-done.3
  114.0 2.3 %final.1 = (bf16[2048,256]{1,0:T(8,128)(2,1)}, f32[64,64]{1,0:T(8,128)}) custom-call(bf16[256,1152]{1,0:T(8,128)(2,1)S(1)} %bitcast.14, bf16[256,256]{1,0:T(8,128)(2,1)S(1)} %copy-done.1, bf16[128,256]{1,0:T(8,128)(2,1)S(1)} %copy-done.6, bf16[128,128]{1,0:T(8,128)(2,1)S(1)} %fusion.5.local_ref, bf16[16,128,256]{2,1,0:T(8,128)(2,1)S(1)} %get-tuple-element.57.grad_ref, ...), custom_call_target="tpu_custom_call" | custom-call | tf_op jit(solution)/shard_map/final/pallas_call | solution.py:444
  (17 shorter events, 0.0 us)
Async XLA Ops:
  0.6 53.9 %copy-start.1 = (bf16[256,256]{1,0:T(8,128)(2,1)S(1)}, bf16[256,256]{1,0:T(8,128)(2,1)}, u32[]{:S(2)}) copy-start(bf16[256,256]{1,0:T(8,128)(2,1)} %constant.30.order_ref.restore_ref) | copy-start | bytes 393220
  0.6 53.8 %copy-start.5 = (bf16[128,256]{1,0:T(8,128)(2,1)S(1)}, bf16[128,256]{1,0:T(8,128)(2,1)}, u32[]{:S(2)}) copy-start(bf16[128,256]{1,0:T(8,128)(2,1)} %constant.31.table_ref) | copy-start | bytes 196612
  0.7 80.0 %copy-start.7 = (bf16[128,128]{1,0:T(8,128)(2,1)S(1)}, bf16[128,128]{1,0:T(8,128)(2,1)}, u32[]{:S(2)}) copy-start(bf16[128,128]{1,0:T(8,128)(2,1)} %constant.32.rest_1_.order_ref) | copy-start | bytes 98308
  0.7 80.0 %copy-start.4 = (bf16[256,128]{1,0:T(8,128)(2,1)S(1)}, bf16[256,128]{1,0:T(8,128)(2,1)}, u32[]{:S(2)}) copy-start(bf16[256,128]{1,0:T(8,128)(2,1)} %constant.33.rest_2_.rows_ref) | copy-start | bytes 196612
  0.7 53.8 %copy-start.6 = (bf16[128,256]{1,0:T(8,128)(2,1)S(1)}, bf16[128,256]{1,0:T(8,128)(2,1)}, u32[]{:S(2)}) copy-start(bf16[128,256]{1,0:T(8,128)(2,1)} %constant.35.back_ref) | copy-start | bytes 196612
  0.7 47.3 %copy-start.13 = (bf16[64,64]{1,0:T(8,128)(2,1)S(1)}, bf16[64,64]{1,0:T(8,128)(2,1)}, u32[]{:S(2)}) copy-start(bf16[64,64]{1,0:T(8,128)(2,1)} %param.15) | copy-start | bytes 24580
  3.7 50.8 %copy-start.3 = (bf16[16,128,256]{2,1,0:T(8,128)(2,1)S(1)}, bf16[16,128,256]{2,1,0:T(8,128)(2,1)}, u32[]{:S(2)}) copy-start(bf16[16,128,256]{2,1,0:T(8,128)(2,1)} %get-tuple-element.35.field_ref) | copy-start | bytes 3145732
  3.7 21.9 %all-to-all-start = ((bf16[8,16,2048]{2,1,0:T(8,128)(2,1)}), bf16[8,16,2048]{2,1,0:T(8,128)(2,1)S(1)}, u32[]{:S(2)}, u32[]{:S(2)}) async-start(bf16[8,16,2048]{2,1,0:T(8,128)(2,1)} %bitcast.31), calls=%async_computation | async-start | bytes 1048576 | tf_op jit(solution)/shard_map/all_to_all | solution.py:512
  25.5 0.8 copy-start.8
  36.2 18.3 %all-to-all-start.1 = ((bf16[8,32,1024]{2,1,0:T(8,128)(2,1)}), bf16[8,32,1024]{2,1,0:T(8,128)(2,1)S(1)}, u32[]{:S(2)}, u32[]{:S(2)}) async-start(bf16[8,32,1024]{2,1,0:T(8,128)(2,1)} %bitcast.30), calls=%async_computation.1 | async-start | bytes 1048576 | tf_op jit(solution)/shard_map/all_to_all | solution.py:512
  39.8 8.2 %collective-permute-start.1 = (bf16[1024,128]{1,0:T(8,128)(2,1)}, bf16[1024,128]{1,0:T(8,128)(2,1)S(1)}, u32[]{:S(2)}, u32[]{:S(2)}) collective-permute-start(bf16[1024,128]{1,0:T(8,128)(2,1)} %get-tuple-element.48.refs_0_), channel_id=1, source_target_pairs={{0,16},{8,24},{16,0},{24,8},{1,17},{9,25},{17,1},{25,9},{2,18},{10... | collective-permute-start | bytes 786440 | tf_op jit(solution)/shard_map/ppermute | solution.py:457
  41.3 21.1 %collective-permute-start = (bf16[1024,128]{1,0:T(8,128)(2,1)}, bf16[1024,128]{1,0:T(8,128)(2,1)}, u32[]{:S(2)}, u32[]{:S(2)}) collective-permute-start(bf16[1024,128]{1,0:T(8,128)(2,1)} %get-tuple-element.48.refs_0_), channel_id=1, source_target_pairs={{0,8},{8,0},{16,24},{24,16},{1,9},{9,1},{17,25},{25,17},{2,10},{10... | collective-permute-start | bytes 786440 | tf_op jit(solution)/shard_map/ppermute | solution.py:457
  48.0 49.6 %copy-start.9 = (bf16[1024,128]{1,0:T(8,128)(2,1)}, bf16[1024,128]{1,0:T(8,128)(2,1)S(1)}, u32[]{:S(2)}) copy-start(bf16[1024,128]{1,0:T(8,128)(2,1)S(1)} %collective-permute-done.1.refs_2_) | copy-start | bytes 786436
  48.0 14.4 %collective-permute-start.2 = (bf16[1024,128]{1,0:T(8,128)(2,1)S(1)}, bf16[1024,128]{1,0:T(8,128)(2,1)}, u32[]{:S(2)}, u32[]{:S(2)}) collective-permute-start(bf16[1024,128]{1,0:T(8,128)(2,1)S(1)} %collective-permute-done.1.refs_2_), channel_id=1, source_target_pairs={{0,8},{8,0},{16,24},{24,16},{1,9},{9,1},{17,25},{25,17},{2,10},{10... | collective-permute-start | bytes 786440 | tf_op jit(solution)/shard_map/ppermute | solution.py:457
  54.5 1.2 %copy-start = (bf16[16,128,256]{2,1,0:T(8,128)(2,1)S(1)}, bf16[16,128,256]{2,1,0:T(8,128)(2,1)}, u32[]{:S(2)}) copy-start(bf16[16,128,256]{2,1,0:T(8,128)(2,1)} %relayout.1.cot_ref) | copy-start | bytes 3145732
  62.4 18.3 %all-to-all-start.2 = ((bf16[8,16,2048]{2,1,0:T(8,128)(2,1)}), bf16[8,16,2048]{2,1,0:T(8,128)(2,1)S(1)}, u32[]{:S(2)}, u32[]{:S(2)}) async-start(bf16[8,16,2048]{2,1,0:T(8,128)(2,1)} %bitcast.8), calls=%async_computation.2 | async-start | bytes 1048576 | tf_op jit(solution)/shard_map/all_to_all | solution.py:512
  66.0 1.2 %collective-permute-start.3 = (f32[64,64]{1,0:T(8,128)S(1)}, f32[64,64]{1,0:T(8,128)S(1)}, u32[]{:S(2)}, u32[]{:S(2)}) collective-permute-start(f32[64,64]{1,0:T(8,128)S(1)} %get-tuple-element.40), channel_id=1, source_target_pairs={{0,8},{8,0},{16,24},{24,16},{1,9},{9,1},{17,25},{25,17},{2,10},{10... | collective-permute-start | bytes 49160 | tf_op jit(solution)/shard_map/ppermute | solution.py:457
  67.2 3.9 %collective-permute-start.4 = (f32[64,64]{1,0:T(8,128)S(1)}, f32[64,64]{1,0:T(8,128)S(1)}, u32[]{:S(2)}, u32[]{:S(2)}) collective-permute-start(f32[64,64]{1,0:T(8,128)S(1)} %add.14), channel_id=1, source_target_pairs={{0,16},{8,24},{16,0},{24,8},{1,17},{9,25},{17,1},{25,9},{2,18},{10... | collective-permute-start | bytes 49160 | tf_op jit(solution)/shard_map/ppermute | solution.py:457
  81.3 1.7 %copy-start.2 = (bf16[1024,128]{1,0:T(8,128)(2,1)}, bf16[1024,128]{1,0:T(8,128)(2,1)S(1)}, u32[]{:S(2)}) copy-start(bf16[1024,128]{1,0:T(8,128)(2,1)S(1)} %grad_spectra.1.rest_0_.refs_4_) | copy-start | bytes 786436
  81.3 10.9 %collective-permute-start.5 = (bf16[1024,128]{1,0:T(8,128)(2,1)S(1)}, bf16[1024,128]{1,0:T(8,128)(2,1)S(1)}, u32[]{:S(2)}, u32[]{:S(2)}) collective-permute-start(bf16[1024,128]{1,0:T(8,128)(2,1)S(1)} %grad_spectra.1.rest_0_.refs_4_), channel_id=1, source_target_pairs={{0,8},{8,0},{16,24},{24,16},{1,9},{9,1},{17,25},{25,17},{2,10},{10... | collective-permute-start | bytes 786440 | tf_op jit(solution)/shard_map/ppermute | solution.py:457
  81.4 10.8 %collective-permute-start.6 = (bf16[1024,128]{1,0:T(8,128)(2,1)S(1)}, bf16[1024,128]{1,0:T(8,128)(2,1)S(1)}, u32[]{:S(2)}, u32[]{:S(2)}) collective-permute-start(bf16[1024,128]{1,0:T(8,128)(2,1)S(1)} %grad_spectra.1.rest_0_.refs_4_), channel_id=1, source_target_pairs={{0,16},{8,24},{16,0},{24,8},{1,17},{9,25},{17,1},{25,9},{2,18},{10... | collective-permute-start | bytes 786440 | tf_op jit(solution)/shard_map/ppermute | solution.py:457
  92.2 5.4 %copy-start.10 = (bf16[1024,128]{1,0:T(8,128)(2,1)}, bf16[1024,128]{1,0:T(8,128)(2,1)S(1)}, u32[]{:S(2)}) copy-start(bf16[1024,128]{1,0:T(8,128)(2,1)S(1)} %collective-permute-done.5.refs_5_) | copy-start | bytes 786436
  92.2 5.3 %copy-start.11 = (bf16[1024,128]{1,0:T(8,128)(2,1)}, bf16[1024,128]{1,0:T(8,128)(2,1)S(1)}, u32[]{:S(2)}) copy-start(bf16[1024,128]{1,0:T(8,128)(2,1)S(1)} %collective-permute-done.6.refs_6_) | copy-start | bytes 786436
  92.2 1.6 %collective-permute-start.7 = (bf16[1024,128]{1,0:T(8,128)(2,1)S(1)}, bf16[1024,128]{1,0:T(8,128)(2,1)S(1)}, u32[]{:S(2)}, u32[]{:S(2)}) collective-permute-start(bf16[1024,128]{1,0:T(8,128)(2,1)S(1)} %collective-permute-done.6.refs_6_), channel_id=1, source_target_pairs={{0,8},{8,0},{16,24},{24,16},{1,9},{9,1},{17,25},{25,17},{2,10},{10... | collective-permute-start | bytes 786440 | tf_op jit(solution)/shard_map/ppermute | solution.py:457
  93.8 3.7 %copy-start.12 = (bf16[1024,128]{1,0:T(8,128)(2,1)}, bf16[1024,128]{1,0:T(8,128)(2,1)S(1)}, u32[]{:S(2)}) copy-start(bf16[1024,128]{1,0:T(8,128)(2,1)S(1)} %collective-permute-done.7.refs_7_) | copy-start | bytes 786436
  93.8 20.2 %all-to-all-start.3 = ((bf16[8,32,1152]{2,1,0:T(8,128)(2,1)}), bf16[8,32,1152]{2,1,0:T(8,128)(2,1)S(1)}, u32[]{:S(2)}, u32[]{:S(2)}) async-start(bf16[8,32,1152]{2,1,0:T(8,128)(2,1)} %bitcast.28), calls=%async_computation.3 | async-start | bytes 1179648 | tf_op jit(solution)/shard_map/all_to_all | solution.py:512

commit v5 on v4

--- a/solution.py
+++ b/solution.py
@@ -542,6 +542,7 @@
         (field_shape, to_modes),
         blocks=field_blocks(2),
     )
+    arrived = exchange(send)
     (cot_rows,) = call(
         relayout_kernel,
         "relayout",
@@ -549,7 +550,6 @@
         (field_shape,),
         blocks=field_blocks(1),
     )
-    arrived, cot_rows = lax.optimization_barrier((exchange(send), cot_rows))
     spectra, send = call(
         functools.partial(forward_kernel, spec_scale, samples, owned),
         "mix_forward",

time: 117 us -> 116 us (level)
  blocking collectives: 0 us -> 22 us
  waiting for transfers between devices: 38.7 us -> 22.8 us
  starting transfers between devices: 23.2 us -> 15.8 us
    all_to_all x0 -> x1, blocking collectives: none -> 22 us  [exchange(): lax.all_to_all(split, 'tile', split_axis=0, concat_axis=0, tiled=False)]
    all_to_all x4 -> x3, waiting for transfers between devices: 27.1 us -> 11.7 us  [exchange(): lax.all_to_all(split, 'tile', split_axis=0, concat_axis=0, tiled=False)]
    all_to_all x4 -> x3, starting transfers between devices: 18.3 us -> 10.9 us  [exchange(): lax.all_to_all(split, 'tile', split_axis=0, concat_axis=0, tiled=False)]
  transfers between devices with their start and end apart: 12 -> 11, of which waited for: 7 -> 6; matrix products, arithmetic and copies ran while one was open for 1% -> 1% of each run, Pallas kernels for 30% -> 30%
where the time goes in v5:
time: 116 us; the launch traced here: 115 us
  Pallas kernels  50.6 us (44%)
  waiting for transfers between devices  22.8 us (20%)
  blocking collectives  22 us (19%)
  starting transfers between devices  15.8 us (14%)
  local copies, waits for them, and re-layouts  2.08 us (2%)
    pallas_call x8, Pallas kernels, call(): pl.pallas_call(kernel, out_shape=tuple(outs), grid=grid, in_specs=in_spec...  50.6 us
    all_to_all x1, blocking collectives, exchange(): lax.all_to_all(split, 'tile', split_axis=0, concat_axis=0, tiled=False)  22 us
    all_to_all x3, waiting for transfers between devices, exchange(): lax.all_to_all(split, 'tile', split_axis=0, concat_axis=0, tiled=False)  11.7 us
    ppermute x8, waiting for transfers between devices, swap(): lax.ppermute(values, axis, [(i, i ^ step) for i in range(lax.axis_size(ax...  11.1 us
    all_to_all x3, starting transfers between devices, exchange(): lax.all_to_all(split, 'tile', split_axis=0, concat_axis=0, tiled=False)  10.9 us
    ppermute x8, starting transfers between devices, swap(): lax.ppermute(values, axis, [(i, i ^ step) for i in range(lax.axis_size(ax...  4.95 us
  transfers between devices with their start and end apart: 11, of which 6 were waited for; matrix products, arithmetic and copies ran while one was open for 1% of the time, Pallas kernels for 30%

profile of v5, /device:TPU:0, one launch (start us, length us, event | category | flops | bytes accessed | tf_op | source)
XLA Modules:
  0.0 114.9 jit_solution(10084576939801929253)
XLA Ops:
  0.6 0.0 copy-start.1
  0.6 0.0 copy-start.5
  0.7 0.0 copy-start.7
  0.7 0.0 copy-start.4
  0.7 0.0 copy-start.6
  0.7 3.0 %columns.1 = (bf16[16,128,256]{2,1,0:T(8,128)(2,1)}, bf16[128,2048]{1,0:T(8,128)(2,1)}) custom-call(bf16[256,256]{1,0:T(8,128)(2,1)} %constant.30.order_ref.restore_ref, bf16[128,256]{1,0:T(8,128)(2,1)} %constant.31.table_ref, bf16[2048,256]{1,0:T(8,128)(2,1)} %bitcast.20, bf16[2048,256]{1,0:T(8,128)(2,1)} %bitcast.21, bf16[2048,256]{1,0:T(8,128)(2,1)} %bitcast.22, ...), custom_call_target="tpu_custom_call" | custom-call | tf_op jit(solution)/shard_map/columns/pallas_call | solution.py:444
  3.7 22.0 %all_to_all.20 = bf16[8,16,2048]{2,1,0:T(8,128)(2,1)} all-to-all(bf16[8,16,2048]{2,1,0:T(8,128)(2,1)} %bitcast.31), channel_id=1, replica_groups=mesh['dp'=4,'tile'=8] {'tile'}, dimensions={0} | all-to-all | bytes 1048576 | tf_op jit(solution)/shard_map/all_to_all | solution.py:512
  25.7 9.8 %mix_forward.1 = (bf16[1024,128]{1,0:T(8,128)(2,1)}, bf16[256,1024]{1,0:T(8,128)(2,1)}) custom-call(bf16[128,2048]{1,0:T(8,128)(2,1)} %bitcast.29, bf16[128,128]{1,0:T(8,128)(2,1)} %constant.32.rest_1_.order_ref, bf16[256,128]{1,0:T(8,128)(2,1)} %constant.33.rest_2_.rows_ref, bf16[256,128]{1,0:T(8,128)(2,1)} %constant.34.rest_3_.rest_1_, ...), custom_call_target="tpu_custom_call" | custom-call | tf_op jit(solution)/shard_map/mix_forward/pallas_call | solution.py:444
  35.5 3.6 %all-to-all-start.1 = ((bf16[8,32,1024]{2,1,0:T(8,128)(2,1)}), bf16[8,32,1024]{2,1,0:T(8,128)(2,1)S(1)}, u32[]{:S(2)}, u32[]{:S(2)}) async-start(bf16[8,32,1024]{2,1,0:T(8,128)(2,1)} %bitcast.30), calls=%async_computation.1 | async-start | bytes 1048576 | tf_op jit(solution)/shard_map/all_to_all | solution.py:512
  39.1 1.5 %collective-permute-start.1 = (bf16[1024,128]{1,0:T(8,128)(2,1)}, bf16[1024,128]{1,0:T(8,128)(2,1)S(1)}, u32[]{:S(2)}, u32[]{:S(2)}) collective-permute-start(bf16[1024,128]{1,0:T(8,128)(2,1)} %get-tuple-element.44.refs_0_), channel_id=1, source_target_pairs={{0,16},{8,24},{16,0},{24,8},{1,17},{9,25},{17,1},{25,9},{2,18},{10... | collective-permute-start | bytes 786440 | tf_op jit(solution)/shard_map/ppermute | solution.py:457
  40.7 0.0 collective-permute-start
  40.7 6.1 %collective-permute-done.1.refs_2_ = bf16[1024,128]{1,0:T(8,128)(2,1)S(1)} collective-permute-done((bf16[1024,128]{1,0:T(8,128)(2,1)}, bf16[1024,128]{1,0:T(8,128)(2,1)S(1)}, u32[]{:S(2)}, u32[]{:S(2)}) %collective-permute-start.1) | collective-permute-done | bytes 262176 | tf_op jit(solution)/shard_map/ppermute | solution.py:457
  46.8 0.0 collective-permute-start.2
  46.8 0.8 copy.15
  47.6 2.6 %relayout.1.cot_ref = bf16[16,128,256]{2,1,0:T(8,128)(2,1)} custom-call(bf16[256,256]{1,0:T(8,128)(2,1)} %constant.30.order_ref.restore_ref, bf16[2048,256]{1,0:T(8,128)(2,1)} %bitcast.24, bf16[2048,256]{1,0:T(8,128)(2,1)} %bitcast.25, bf16[2048,256]{1,0:T(8,128)(2,1)} %bitcast.26, bf16[2048,256]{1,0:T(8,128)(2,1)} %bitcast.27), custom_call_target="tpu_custom_call" | custom-call | tf_op jit(solution)/shard_map/relayout/pallas_call | solution.py:444
  50.2 0.1 fusion.4.local_ref
  50.3 3.0 %all-to-all-done.1 = bf16[8,32,1024]{2,1,0:T(8,128)(2,1)S(1)} async-done(((bf16[8,32,1024]{2,1,0:T(8,128)(2,1)}), bf16[8,32,1024]{2,1,0:T(8,128)(2,1)S(1)}, u32[]{:S(2)}, u32[]{:S(2)}) %all-to-all-start.1) | async-done | bytes 524320 | tf_op jit(solution)/shard_map/all_to_all | solution.py:512
  53.3 0.0 copy-done.1
  53.3 0.0 copy-done.5
  53.3 0.0 copy-start
  53.3 1.2 %copy-done = bf16[16,128,256]{2,1,0:T(8,128)(2,1)S(1)} copy-done((bf16[16,128,256]{2,1,0:T(8,128)(2,1)S(1)}, bf16[16,128,256]{2,1,0:T(8,128)(2,1)}, u32[]{:S(2)}) %copy-start) | copy-done | bytes 1048600
  54.6 6.6 %pixels.1 = (bf16[16,128,256]{2,1,0:T(8,128)(2,1)S(1)}, bf16[128,2048]{1,0:T(8,128)(2,1)}, f32[64,64]{1,0:T(8,128)S(1)}) custom-call(bf16[256,1024]{1,0:T(8,128)(2,1)S(1)} %bitcast.16, bf16[256,256]{1,0:T(8,128)(2,1)S(1)} %copy-done.1, bf16[128,256]{1,0:T(8,128)(2,1)S(1)} %copy-done.6, bf16[128,128]{1,0:T(8,128)(2,1)S(1)} %fusion.4.local_ref, ...), custom_call_target="tpu_custom_call" | custom-call | tf_op jit(solution)/shard_map/pixels/pallas_call | solution.py:444
  61.2 0.0 collective-permute-done.refs_1_
  61.2 0.0 collective-permute-done.2.refs_3_
  61.2 3.6 %all-to-all-start.2 = ((bf16[8,16,2048]{2,1,0:T(8,128)(2,1)}), bf16[8,16,2048]{2,1,0:T(8,128)(2,1)S(1)}, u32[]{:S(2)}, u32[]{:S(2)}) async-start(bf16[8,16,2048]{2,1,0:T(8,128)(2,1)} %bitcast.8), calls=%async_computation.2 | async-start | bytes 1048576 | tf_op jit(solution)/shard_map/all_to_all | solution.py:512
  64.9 0.0 collective-permute-start.3
  64.9 1.2 %collective-permute-done.3 = f32[64,64]{1,0:T(8,128)S(1)} collective-permute-done((f32[64,64]{1,0:T(8,128)S(1)}, f32[64,64]{1,0:T(8,128)S(1)}, u32[]{:S(2)}, u32[]{:S(2)}) %collective-permute-start.3) | collective-permute-done | bytes 16416 | tf_op jit(solution)/shard_map/ppermute | solution.py:457
  66.1 1.5 %collective-permute-start.4 = (f32[64,64]{1,0:T(8,128)S(1)}, f32[64,64]{1,0:T(8,128)S(1)}, u32[]{:S(2)}, u32[]{:S(2)}) collective-permute-start(f32[64,64]{1,0:T(8,128)S(1)} %add.14), channel_id=1, source_target_pairs={{0,16},{8,24},{16,0},{24,8},{1,17},{9,25},{17,1},{25,9},{2,18},{10... | collective-permute-start | bytes 49160 | tf_op jit(solution)/shard_map/ppermute | solution.py:457
  67.6 2.4 %collective-permute-done.4 = f32[64,64]{1,0:T(8,128)S(1)} collective-permute-done((f32[64,64]{1,0:T(8,128)S(1)}, f32[64,64]{1,0:T(8,128)S(1)}, u32[]{:S(2)}, u32[]{:S(2)}) %collective-permute-start.4) | collective-permute-done | bytes 16416 | tf_op jit(solution)/shard_map/ppermute | solution.py:457
  70.0 0.6 add.15.rest_2_
  70.6 8.7 %all-to-all-done.2 = bf16[8,16,2048]{2,1,0:T(8,128)(2,1)S(1)} async-done(((bf16[8,16,2048]{2,1,0:T(8,128)(2,1)}), bf16[8,16,2048]{2,1,0:T(8,128)(2,1)S(1)}, u32[]{:S(2)}, u32[]{:S(2)}) %all-to-all-start.2) | async-done | bytes 524320 | tf_op jit(solution)/shard_map/all_to_all | solution.py:512
  79.3 0.0 copy-done.4
  79.3 0.6 grad_spectra.1.rest_0_.refs_4_
  79.9 0.1 collective-permute-start.5
  80.0 1.6 %collective-permute-start.6 = (bf16[1024,128]{1,0:T(8,128)(2,1)S(1)}, bf16[1024,128]{1,0:T(8,128)(2,1)S(1)}, u32[]{:S(2)}, u32[]{:S(2)}) collective-permute-start(bf16[1024,128]{1,0:T(8,128)(2,1)S(1)} %grad_spectra.1.rest_0_.refs_4_), channel_id=1, source_target_pairs={{0,16},{8,24},{16,0},{24,8},{1,17},{9,25},{17,1},{25,9},{2,18},{10... | collective-permute-start | bytes 786440 | tf_op jit(solution)/shard_map/ppermute | solution.py:457
  81.6 0.0 copy-done.2
  81.6 9.2 %mix_backward.1 = bf16[256,1152]{1,0:T(8,128)(2,1)} custom-call(bf16[1024,128]{1,0:T(8,128)(2,1)} %copy-done.2, bf16[256,128]{1,0:T(8,128)(2,1)} %constant.34.rest_3_.rest_1_, f32[64,64]{1,0:T(8,128)} %add.15.rest_2_, bf16[32768,128]{1,0:T(8,128)(2,1)} %bitcast.18), custom_call_target="tpu_custom_call" | custom-call | tf_op jit(solution)/shard_map/mix_backward/pallas_call | solution.py:444
  90.8 0.0 collective-permute-done.5.refs_5_
  90.8 0.0 copy-start.9
  90.8 0.0 collective-permute-done.6.refs_6_
  90.8 0.2 collective-permute-start.7
  91.0 1.4 %collective-permute-done.7.refs_7_ = bf16[1024,128]{1,0:T(8,128)(2,1)S(1)} collective-permute-done((bf16[1024,128]{1,0:T(8,128)(2,1)S(1)}, bf16[1024,128]{1,0:T(8,128)(2,1)S(1)}, u32[]{:S(2)}, u32[]{:S(2)}) %collective-permute-start.7) | collective-permute-done | bytes 262176 | tf_op jit(solution)/shard_map/ppermute | solution.py:457
  92.4 3.6 %all-to-all-start.3 = ((bf16[8,32,1152]{2,1,0:T(8,128)(2,1)}), bf16[8,32,1152]{2,1,0:T(8,128)(2,1)S(1)}, u32[]{:S(2)}, u32[]{:S(2)}) async-start(bf16[8,32,1152]{2,1,0:T(8,128)(2,1)} %bitcast.28), calls=%async_computation.3 | async-start | bytes 1179648 | tf_op jit(solution)/shard_map/all_to_all | solution.py:512
  96.1 0.1 fusion.5.local_ref
  96.1 0.0 copy-done.8
  96.2 16.4 %mode_grad.1 = f32[32768,128]{1,0:T(8,128)} custom-call(bf16[1024,128]{1,0:T(8,128)(2,1)} %get-tuple-element.44.refs_0_, bf16[1024,128]{1,0:T(8,128)(2,1)} %collective-permute-done.refs_1_, bf16[1024,128]{1,0:T(8,128)(2,1)} %copy-done.8, bf16[1024,128]{1,0:T(8,128)(2,1)} %collective-permute-done.2.refs_3_, bf16[1024,128]{1,0:T(8,128)(2,1)} %copy-done.2, ...), custom_call_target="tpu_custom_call" | custom-call | tf_op jit(solution)/shard_map/mode_grad/pallas_call | solution.py:444
  112.6 0.0 all-to-all-done.3
  112.6 2.3 %final.1 = (bf16[2048,256]{1,0:T(8,128)(2,1)}, f32[64,64]{1,0:T(8,128)}) custom-call(bf16[256,1152]{1,0:T(8,128)(2,1)S(1)} %bitcast.14, bf16[256,256]{1,0:T(8,128)(2,1)S(1)} %copy-done.1, bf16[128,256]{1,0:T(8,128)(2,1)S(1)} %copy-done.6, bf16[128,128]{1,0:T(8,128)(2,1)S(1)} %fusion.5.local_ref, bf16[16,128,256]{2,1,0:T(8,128)(2,1)S(1)} %get-tuple-element.53.grad_ref, ...), custom_call_target="tpu_custom_call" | custom-call | tf_op jit(solution)/shard_map/final/pallas_call | solution.py:444
  (14 shorter events, 0.0 us)
Async XLA Ops:
  0.6 52.7 %copy-start.1 = (bf16[256,256]{1,0:T(8,128)(2,1)S(1)}, bf16[256,256]{1,0:T(8,128)(2,1)}, u32[]{:S(2)}) copy-start(bf16[256,256]{1,0:T(8,128)(2,1)} %constant.30.order_ref.restore_ref) | copy-start | bytes 393220
  0.6 52.7 %copy-start.5 = (bf16[128,256]{1,0:T(8,128)(2,1)S(1)}, bf16[128,256]{1,0:T(8,128)(2,1)}, u32[]{:S(2)}) copy-start(bf16[128,256]{1,0:T(8,128)(2,1)} %constant.31.table_ref) | copy-start | bytes 196612
  0.7 78.6 %copy-start.7 = (bf16[128,128]{1,0:T(8,128)(2,1)S(1)}, bf16[128,128]{1,0:T(8,128)(2,1)}, u32[]{:S(2)}) copy-start(bf16[128,128]{1,0:T(8,128)(2,1)} %constant.32.rest_1_.order_ref) | copy-start | bytes 98308
  0.7 78.6 %copy-start.4 = (bf16[256,128]{1,0:T(8,128)(2,1)S(1)}, bf16[256,128]{1,0:T(8,128)(2,1)}, u32[]{:S(2)}) copy-start(bf16[256,128]{1,0:T(8,128)(2,1)} %constant.33.rest_2_.rows_ref) | copy-start | bytes 196612
  0.7 52.6 %copy-start.6 = (bf16[128,256]{1,0:T(8,128)(2,1)S(1)}, bf16[128,256]{1,0:T(8,128)(2,1)}, u32[]{:S(2)}) copy-start(bf16[128,256]{1,0:T(8,128)(2,1)} %constant.35.back_ref) | copy-start | bytes 196612
  3.6 49.7 %copy-start.3 = (bf16[16,128,256]{2,1,0:T(8,128)(2,1)S(1)}, bf16[16,128,256]{2,1,0:T(8,128)(2,1)}, u32[]{:S(2)}) copy-start(bf16[16,128,256]{2,1,0:T(8,128)(2,1)} %get-tuple-element.32.field_ref) | copy-start | bytes 3145732
  3.7 92.4 %copy-start.12 = (bf16[64,64]{1,0:T(8,128)(2,1)S(1)}, bf16[64,64]{1,0:T(8,128)(2,1)}, u32[]{:S(2)}) copy-start(bf16[64,64]{1,0:T(8,128)(2,1)} %param.15) | copy-start | bytes 24580
  35.5 17.8 %all-to-all-start.1 = ((bf16[8,32,1024]{2,1,0:T(8,128)(2,1)}), bf16[8,32,1024]{2,1,0:T(8,128)(2,1)S(1)}, u32[]{:S(2)}, u32[]{:S(2)}) async-start(bf16[8,32,1024]{2,1,0:T(8,128)(2,1)} %bitcast.30), calls=%async_computation.1 | async-start | bytes 1048576 | tf_op jit(solution)/shard_map/all_to_all | solution.py:512
  39.1 7.6 %collective-permute-start.1 = (bf16[1024,128]{1,0:T(8,128)(2,1)}, bf16[1024,128]{1,0:T(8,128)(2,1)S(1)}, u32[]{:S(2)}, u32[]{:S(2)}) collective-permute-start(bf16[1024,128]{1,0:T(8,128)(2,1)} %get-tuple-element.44.refs_0_), channel_id=1, source_target_pairs={{0,16},{8,24},{16,0},{24,8},{1,17},{9,25},{17,1},{25,9},{2,18},{10... | collective-permute-start | bytes 786440 | tf_op jit(solution)/shard_map/ppermute | solution.py:457
  40.7 20.5 %collective-permute-start = (bf16[1024,128]{1,0:T(8,128)(2,1)}, bf16[1024,128]{1,0:T(8,128)(2,1)}, u32[]{:S(2)}, u32[]{:S(2)}) collective-permute-start(bf16[1024,128]{1,0:T(8,128)(2,1)} %get-tuple-element.44.refs_0_), channel_id=1, source_target_pairs={{0,8},{8,0},{16,24},{24,16},{1,9},{9,1},{17,25},{25,17},{2,10},{10... | collective-permute-start | bytes 786440 | tf_op jit(solution)/shard_map/ppermute | solution.py:457
  46.8 49.4 %copy-start.8 = (bf16[1024,128]{1,0:T(8,128)(2,1)}, bf16[1024,128]{1,0:T(8,128)(2,1)S(1)}, u32[]{:S(2)}) copy-start(bf16[1024,128]{1,0:T(8,128)(2,1)S(1)} %collective-permute-done.1.refs_2_) | copy-start | bytes 786436
  46.8 14.5 %collective-permute-start.2 = (bf16[1024,128]{1,0:T(8,128)(2,1)S(1)}, bf16[1024,128]{1,0:T(8,128)(2,1)}, u32[]{:S(2)}, u32[]{:S(2)}) collective-permute-start(bf16[1024,128]{1,0:T(8,128)(2,1)S(1)} %collective-permute-done.1.refs_2_), channel_id=1, source_target_pairs={{0,8},{8,0},{16,24},{24,16},{1,9},{9,1},{17,25},{25,17},{2,10},{10... | collective-permute-start | bytes 786440 | tf_op jit(solution)/shard_map/ppermute | solution.py:457
  53.3 1.2 %copy-start = (bf16[16,128,256]{2,1,0:T(8,128)(2,1)S(1)}, bf16[16,128,256]{2,1,0:T(8,128)(2,1)}, u32[]{:S(2)}) copy-start(bf16[16,128,256]{2,1,0:T(8,128)(2,1)} %relayout.1.cot_ref) | copy-start | bytes 3145732
  61.2 18.1 %all-to-all-start.2 = ((bf16[8,16,2048]{2,1,0:T(8,128)(2,1)}), bf16[8,16,2048]{2,1,0:T(8,128)(2,1)S(1)}, u32[]{:S(2)}, u32[]{:S(2)}) async-start(bf16[8,16,2048]{2,1,0:T(8,128)(2,1)} %bitcast.8), calls=%async_computation.2 | async-start | bytes 1048576 | tf_op jit(solution)/shard_map/all_to_all | solution.py:512
  64.9 1.2 %collective-permute-start.3 = (f32[64,64]{1,0:T(8,128)S(1)}, f32[64,64]{1,0:T(8,128)S(1)}, u32[]{:S(2)}, u32[]{:S(2)}) collective-permute-start(f32[64,64]{1,0:T(8,128)S(1)} %get-tuple-element.36), channel_id=1, source_target_pairs={{0,8},{8,0},{16,24},{24,16},{1,9},{9,1},{17,25},{25,17},{2,10},{10... | collective-permute-start | bytes 49160 | tf_op jit(solution)/shard_map/ppermute | solution.py:457
  66.1 3.9 %collective-permute-start.4 = (f32[64,64]{1,0:T(8,128)S(1)}, f32[64,64]{1,0:T(8,128)S(1)}, u32[]{:S(2)}, u32[]{:S(2)}) collective-permute-start(f32[64,64]{1,0:T(8,128)S(1)} %add.14), channel_id=1, source_target_pairs={{0,16},{8,24},{16,0},{24,8},{1,17},{9,25},{17,1},{25,9},{2,18},{10... | collective-permute-start | bytes 49160 | tf_op jit(solution)/shard_map/ppermute | solution.py:457
  79.9 1.7 %copy-start.2 = (bf16[1024,128]{1,0:T(8,128)(2,1)}, bf16[1024,128]{1,0:T(8,128)(2,1)S(1)}, u32[]{:S(2)}) copy-start(bf16[1024,128]{1,0:T(8,128)(2,1)S(1)} %grad_spectra.1.rest_0_.refs_4_) | copy-start | bytes 786436
  79.9 10.9 %collective-permute-start.5 = (bf16[1024,128]{1,0:T(8,128)(2,1)S(1)}, bf16[1024,128]{1,0:T(8,128)(2,1)S(1)}, u32[]{:S(2)}, u32[]{:S(2)}) collective-permute-start(bf16[1024,128]{1,0:T(8,128)(2,1)S(1)} %grad_spectra.1.rest_0_.refs_4_), channel_id=1, source_target_pairs={{0,8},{8,0},{16,24},{24,16},{1,9},{9,1},{17,25},{25,17},{2,10},{10... | collective-permute-start | bytes 786440 | tf_op jit(solution)/shard_map/ppermute | solution.py:457
  80.0 10.8 %collective-permute-start.6 = (bf16[1024,128]{1,0:T(8,128)(2,1)S(1)}, bf16[1024,128]{1,0:T(8,128)(2,1)S(1)}, u32[]{:S(2)}, u32[]{:S(2)}) collective-permute-start(bf16[1024,128]{1,0:T(8,128)(2,1)S(1)} %grad_spectra.1.rest_0_.refs_4_), channel_id=1, source_target_pairs={{0,16},{8,24},{16,0},{24,8},{1,17},{9,25},{17,1},{25,9},{2,18},{10... | collective-permute-start | bytes 786440 | tf_op jit(solution)/shard_map/ppermute | solution.py:457
  90.8 5.4 %copy-start.9 = (bf16[1024,128]{1,0:T(8,128)(2,1)}, bf16[1024,128]{1,0:T(8,128)(2,1)S(1)}, u32[]{:S(2)}) copy-start(bf16[1024,128]{1,0:T(8,128)(2,1)S(1)} %collective-permute-done.5.refs_5_) | copy-start | bytes 786436
  90.8 5.3 %copy-start.10 = (bf16[1024,128]{1,0:T(8,128)(2,1)}, bf16[1024,128]{1,0:T(8,128)(2,1)S(1)}, u32[]{:S(2)}) copy-start(bf16[1024,128]{1,0:T(8,128)(2,1)S(1)} %collective-permute-done.6.refs_6_) | copy-start | bytes 786436
  90.8 1.6 %collective-permute-start.7 = (bf16[1024,128]{1,0:T(8,128)(2,1)S(1)}, bf16[1024,128]{1,0:T(8,128)(2,1)S(1)}, u32[]{:S(2)}, u32[]{:S(2)}) collective-permute-start(bf16[1024,128]{1,0:T(8,128)(2,1)S(1)} %collective-permute-done.6.refs_6_), channel_id=1, source_target_pairs={{0,8},{8,0},{16,24},{24,16},{1,9},{9,1},{17,25},{25,17},{2,10},{10... | collective-permute-start | bytes 786440 | tf_op jit(solution)/shard_map/ppermute | solution.py:457
  92.4 3.7 %copy-start.11 = (bf16[1024,128]{1,0:T(8,128)(2,1)}, bf16[1024,128]{1,0:T(8,128)(2,1)S(1)}, u32[]{:S(2)}) copy-start(bf16[1024,128]{1,0:T(8,128)(2,1)S(1)} %collective-permute-done.7.refs_7_) | copy-start | bytes 786436
  92.4 20.2 %all-to-all-start.3 = ((bf16[8,32,1152]{2,1,0:T(8,128)(2,1)}), bf16[8,32,1152]{2,1,0:T(8,128)(2,1)S(1)}, u32[]{:S(2)}, u32[]{:S(2)}) async-start(bf16[8,32,1152]{2,1,0:T(8,128)(2,1)} %bitcast.28), calls=%async_computation.3 | async-start | bytes 1179648 | tf_op jit(solution)/shard_map/all_to_all | solution.py:512

commit v6 on v5

--- a/solution.py
+++ b/solution.py
@@ -17,7 +17,7 @@
 PACK = 16
 GROUP = 8
 SPLIT = 4
-AHEAD = 3
+AHEAD = 2
 
 
 def row_tables(height, modes):
@@ -570,7 +570,7 @@
     )
     all_spectra = gather_far(gather_near(spectra, "dp"), "dp")
     arrived = exchange(send)
-    steps = 4
+    steps = 8
     row_block = pl.BlockSpec((steps, lanes, width), lambda n: (n, 0, 0))
     gate_rows, send, local_sum = call(
         functools.partial(pixels_kernel, mode_scale, th),

time: 116 us -> 115 us (level)
  no operation moved by 1% of the time
where the time goes in v6:
time: 115 us; the launch traced here: 114 us
  Pallas kernels  50.2 us (44%)
  waiting for transfers between devices  22.8 us (20%)
  blocking collectives  22 us (19%)
  starting transfers between devices  15.8 us (14%)
  local copies, waits for them, and re-layouts  2.08 us (2%)
    pallas_call x8, Pallas kernels, call(): pl.pallas_call(kernel, out_shape=tuple(outs), grid=grid, in_specs=in_spec...  50.2 us
    all_to_all x1, blocking collectives, exchange(): lax.all_to_all(split, 'tile', split_axis=0, concat_axis=0, tiled=False)  22 us
    all_to_all x3, waiting for transfers between devices, exchange(): lax.all_to_all(split, 'tile', split_axis=0, concat_axis=0, tiled=False)  11.7 us
    ppermute x8, waiting for transfers between devices, swap(): lax.ppermute(values, axis, [(i, i ^ step) for i in range(lax.axis_size(ax...  11 us
    all_to_all x3, starting transfers between devices, exchange(): lax.all_to_all(split, 'tile', split_axis=0, concat_axis=0, tiled=False)  10.9 us
    ppermute x8, starting transfers between devices, swap(): lax.ppermute(values, axis, [(i, i ^ step) for i in range(lax.axis_size(ax...  4.96 us
  transfers between devices with their start and end apart: 11, of which 6 were waited for; matrix products, arithmetic and copies ran while one was open for 1% of the time, Pallas kernels for 30%

profile of v6, /device:TPU:0, one launch (start us, length us, event | category | flops | bytes accessed | tf_op | source)
XLA Modules:
  0.0 114.5 jit_solution(3004263158407691789)
XLA Ops:
  0.6 0.0 copy-start.1
  0.6 0.0 copy-start.5
  0.7 0.0 copy-start.7
  0.7 0.0 copy-start.4
  0.7 0.0 copy-start.6
  0.7 3.0 %columns.1 = (bf16[16,128,256]{2,1,0:T(8,128)(2,1)}, bf16[128,2048]{1,0:T(8,128)(2,1)}) custom-call(bf16[256,256]{1,0:T(8,128)(2,1)} %constant.30.order_ref.restore_ref, bf16[128,256]{1,0:T(8,128)(2,1)} %constant.31.table_ref, bf16[2048,256]{1,0:T(8,128)(2,1)} %bitcast.20, bf16[2048,256]{1,0:T(8,128)(2,1)} %bitcast.21, bf16[2048,256]{1,0:T(8,128)(2,1)} %bitcast.22, ...), custom_call_target="tpu_custom_call" | custom-call | tf_op jit(solution)/shard_map/columns/pallas_call | solution.py:444
  3.7 22.0 %all_to_all.20 = bf16[8,16,2048]{2,1,0:T(8,128)(2,1)} all-to-all(bf16[8,16,2048]{2,1,0:T(8,128)(2,1)} %bitcast.31), channel_id=1, replica_groups=mesh['dp'=4,'tile'=8] {'tile'}, dimensions={0} | all-to-all | bytes 1048576 | tf_op jit(solution)/shard_map/all_to_all | solution.py:512
  25.7 9.8 %mix_forward.1 = (bf16[1024,128]{1,0:T(8,128)(2,1)}, bf16[256,1024]{1,0:T(8,128)(2,1)}) custom-call(bf16[128,2048]{1,0:T(8,128)(2,1)} %bitcast.29, bf16[128,128]{1,0:T(8,128)(2,1)} %constant.32.rest_1_.order_ref, bf16[256,128]{1,0:T(8,128)(2,1)} %constant.33.rest_2_.rows_ref, bf16[256,128]{1,0:T(8,128)(2,1)} %constant.34.rest_3_.rest_1_, ...), custom_call_target="tpu_custom_call" | custom-call | tf_op jit(solution)/shard_map/mix_forward/pallas_call | solution.py:444
  35.5 3.6 %all-to-all-start.1 = ((bf16[8,32,1024]{2,1,0:T(8,128)(2,1)}), bf16[8,32,1024]{2,1,0:T(8,128)(2,1)S(1)}, u32[]{:S(2)}, u32[]{:S(2)}) async-start(bf16[8,32,1024]{2,1,0:T(8,128)(2,1)} %bitcast.30), calls=%async_computation.1 | async-start | bytes 1048576 | tf_op jit(solution)/shard_map/all_to_all | solution.py:512
  39.1 1.5 %collective-permute-start.1 = (bf16[1024,128]{1,0:T(8,128)(2,1)}, bf16[1024,128]{1,0:T(8,128)(2,1)S(1)}, u32[]{:S(2)}, u32[]{:S(2)}) collective-permute-start(bf16[1024,128]{1,0:T(8,128)(2,1)} %get-tuple-element.44.refs_0_), channel_id=1, source_target_pairs={{0,16},{8,24},{16,0},{24,8},{1,17},{9,25},{17,1},{25,9},{2,18},{10... | collective-permute-start | bytes 786440 | tf_op jit(solution)/shard_map/ppermute | solution.py:457
  40.7 0.0 collective-permute-start
  40.7 6.1 %collective-permute-done.1.refs_2_ = bf16[1024,128]{1,0:T(8,128)(2,1)S(1)} collective-permute-done((bf16[1024,128]{1,0:T(8,128)(2,1)}, bf16[1024,128]{1,0:T(8,128)(2,1)S(1)}, u32[]{:S(2)}, u32[]{:S(2)}) %collective-permute-start.1) | collective-permute-done | bytes 262176 | tf_op jit(solution)/shard_map/ppermute | solution.py:457
  46.7 0.0 collective-permute-start.2
  46.7 0.8 copy.15
  47.5 2.6 %relayout.1.cot_ref = bf16[16,128,256]{2,1,0:T(8,128)(2,1)} custom-call(bf16[256,256]{1,0:T(8,128)(2,1)} %constant.30.order_ref.restore_ref, bf16[2048,256]{1,0:T(8,128)(2,1)} %bitcast.24, bf16[2048,256]{1,0:T(8,128)(2,1)} %bitcast.25, bf16[2048,256]{1,0:T(8,128)(2,1)} %bitcast.26, bf16[2048,256]{1,0:T(8,128)(2,1)} %bitcast.27), custom_call_target="tpu_custom_call" | custom-call | tf_op jit(solution)/shard_map/relayout/pallas_call | solution.py:444
  50.2 0.1 fusion.4.local_ref
  50.3 3.0 %all-to-all-done.1 = bf16[8,32,1024]{2,1,0:T(8,128)(2,1)S(1)} async-done(((bf16[8,32,1024]{2,1,0:T(8,128)(2,1)}), bf16[8,32,1024]{2,1,0:T(8,128)(2,1)S(1)}, u32[]{:S(2)}, u32[]{:S(2)}) %all-to-all-start.1) | async-done | bytes 524320 | tf_op jit(solution)/shard_map/all_to_all | solution.py:512
  53.3 0.0 copy-done.1
  53.3 0.0 copy-done.5
  53.3 0.0 copy-done.6
  53.3 0.0 copy-done.3
  53.3 0.0 copy-start
  53.3 1.2 %copy-done = bf16[16,128,256]{2,1,0:T(8,128)(2,1)S(1)} copy-done((bf16[16,128,256]{2,1,0:T(8,128)(2,1)S(1)}, bf16[16,128,256]{2,1,0:T(8,128)(2,1)}, u32[]{:S(2)}) %copy-start) | copy-done | bytes 1048600
  54.5 6.3 %pixels.1 = (bf16[16,128,256]{2,1,0:T(8,128)(2,1)S(1)}, bf16[128,2048]{1,0:T(8,128)(2,1)}, f32[64,64]{1,0:T(8,128)S(1)}) custom-call(bf16[256,1024]{1,0:T(8,128)(2,1)S(1)} %bitcast.16, bf16[256,256]{1,0:T(8,128)(2,1)S(1)} %copy-done.1, bf16[128,256]{1,0:T(8,128)(2,1)S(1)} %copy-done.6, bf16[128,128]{1,0:T(8,128)(2,1)S(1)} %fusion.4.local_ref, ...), custom_call_target="tpu_custom_call" | custom-call | tf_op jit(solution)/shard_map/pixels/pallas_call | solution.py:444
  60.8 0.0 collective-permute-done.refs_1_
  60.8 0.0 collective-permute-done.2.refs_3_
  60.8 3.6 %all-to-all-start.2 = ((bf16[8,16,2048]{2,1,0:T(8,128)(2,1)}), bf16[8,16,2048]{2,1,0:T(8,128)(2,1)S(1)}, u32[]{:S(2)}, u32[]{:S(2)}) async-start(bf16[8,16,2048]{2,1,0:T(8,128)(2,1)} %bitcast.8), calls=%async_computation.2 | async-start | bytes 1048576 | tf_op jit(solution)/shard_map/all_to_all | solution.py:512
  64.5 0.0 collective-permute-start.3
  64.5 1.2 %collective-permute-done.3 = f32[64,64]{1,0:T(8,128)S(1)} collective-permute-done((f32[64,64]{1,0:T(8,128)S(1)}, f32[64,64]{1,0:T(8,128)S(1)}, u32[]{:S(2)}, u32[]{:S(2)}) %collective-permute-start.3) | collective-permute-done | bytes 16416 | tf_op jit(solution)/shard_map/ppermute | solution.py:457
  65.7 1.5 %collective-permute-start.4 = (f32[64,64]{1,0:T(8,128)S(1)}, f32[64,64]{1,0:T(8,128)S(1)}, u32[]{:S(2)}, u32[]{:S(2)}) collective-permute-start(f32[64,64]{1,0:T(8,128)S(1)} %add.14), channel_id=1, source_target_pairs={{0,16},{8,24},{16,0},{24,8},{1,17},{9,25},{17,1},{25,9},{2,18},{10... | collective-permute-start | bytes 49160 | tf_op jit(solution)/shard_map/ppermute | solution.py:457
  67.2 2.4 %collective-permute-done.4 = f32[64,64]{1,0:T(8,128)S(1)} collective-permute-done((f32[64,64]{1,0:T(8,128)S(1)}, f32[64,64]{1,0:T(8,128)S(1)}, u32[]{:S(2)}, u32[]{:S(2)}) %collective-permute-start.4) | collective-permute-done | bytes 16416 | tf_op jit(solution)/shard_map/ppermute | solution.py:457
  69.6 0.6 add.15.rest_2_
  70.2 8.7 %all-to-all-done.2 = bf16[8,16,2048]{2,1,0:T(8,128)(2,1)S(1)} async-done(((bf16[8,16,2048]{2,1,0:T(8,128)(2,1)}), bf16[8,16,2048]{2,1,0:T(8,128)(2,1)S(1)}, u32[]{:S(2)}, u32[]{:S(2)}) %all-to-all-start.2) | async-done | bytes 524320 | tf_op jit(solution)/shard_map/all_to_all | solution.py:512
  78.9 0.0 copy-done.7
  78.9 0.6 grad_spectra.1.rest_0_.refs_4_
  79.5 0.1 collective-permute-start.5
  79.6 1.6 %collective-permute-start.6 = (bf16[1024,128]{1,0:T(8,128)(2,1)S(1)}, bf16[1024,128]{1,0:T(8,128)(2,1)S(1)}, u32[]{:S(2)}, u32[]{:S(2)}) collective-permute-start(bf16[1024,128]{1,0:T(8,128)(2,1)S(1)} %grad_spectra.1.rest_0_.refs_4_), channel_id=1, source_target_pairs={{0,16},{8,24},{16,0},{24,8},{1,17},{9,25},{17,1},{25,9},{2,18},{10... | collective-permute-start | bytes 786440 | tf_op jit(solution)/shard_map/ppermute | solution.py:457
  81.2 9.2 %mix_backward.1 = bf16[256,1152]{1,0:T(8,128)(2,1)} custom-call(bf16[1024,128]{1,0:T(8,128)(2,1)} %copy-done.2, bf16[256,128]{1,0:T(8,128)(2,1)} %constant.34.rest_3_.rest_1_, f32[64,64]{1,0:T(8,128)} %add.15.rest_2_, bf16[32768,128]{1,0:T(8,128)(2,1)} %bitcast.18), custom_call_target="tpu_custom_call" | custom-call | tf_op jit(solution)/shard_map/mix_backward/pallas_call | solution.py:444
  90.4 0.0 collective-permute-done.5.refs_5_
  90.4 0.0 copy-start.9
  90.4 0.0 collective-permute-done.6.refs_6_
  90.4 0.2 collective-permute-start.7
  90.6 1.4 %collective-permute-done.7.refs_7_ = bf16[1024,128]{1,0:T(8,128)(2,1)S(1)} collective-permute-done((bf16[1024,128]{1,0:T(8,128)(2,1)S(1)}, bf16[1024,128]{1,0:T(8,128)(2,1)S(1)}, u32[]{:S(2)}, u32[]{:S(2)}) %collective-permute-start.7) | collective-permute-done | bytes 262176 | tf_op jit(solution)/shard_map/ppermute | solution.py:457
  92.0 3.6 %all-to-all-start.3 = ((bf16[8,32,1152]{2,1,0:T(8,128)(2,1)}), bf16[8,32,1152]{2,1,0:T(8,128)(2,1)S(1)}, u32[]{:S(2)}, u32[]{:S(2)}) async-start(bf16[8,32,1152]{2,1,0:T(8,128)(2,1)} %bitcast.28), calls=%async_computation.3 | async-start | bytes 1179648 | tf_op jit(solution)/shard_map/all_to_all | solution.py:512
  95.7 0.1 fusion.5.local_ref
  95.8 16.4 %mode_grad.1 = f32[32768,128]{1,0:T(8,128)} custom-call(bf16[1024,128]{1,0:T(8,128)(2,1)} %get-tuple-element.44.refs_0_, bf16[1024,128]{1,0:T(8,128)(2,1)} %collective-permute-done.refs_1_, bf16[1024,128]{1,0:T(8,128)(2,1)} %copy-done.8, bf16[1024,128]{1,0:T(8,128)(2,1)} %collective-permute-done.2.refs_3_, bf16[1024,128]{1,0:T(8,128)(2,1)} %copy-done.2, ...), custom_call_target="tpu_custom_call" | custom-call | tf_op jit(solution)/shard_map/mode_grad/pallas_call | solution.py:444
  112.2 0.0 all-to-all-done.3
  112.2 2.3 %final.1 = (bf16[2048,256]{1,0:T(8,128)(2,1)}, f32[64,64]{1,0:T(8,128)}) custom-call(bf16[256,1152]{1,0:T(8,128)(2,1)S(1)} %bitcast.14, bf16[256,256]{1,0:T(8,128)(2,1)S(1)} %copy-done.1, bf16[128,256]{1,0:T(8,128)(2,1)S(1)} %copy-done.6, bf16[128,128]{1,0:T(8,128)(2,1)S(1)} %fusion.5.local_ref, bf16[16,128,256]{2,1,0:T(8,128)(2,1)S(1)} %get-tuple-element.53.grad_ref, ...), custom_call_target="tpu_custom_call" | custom-call | tf_op jit(solution)/shard_map/final/pallas_call | solution.py:444
  (14 shorter events, 0.0 us)
Async XLA Ops:
  0.6 52.7 %copy-start.1 = (bf16[256,256]{1,0:T(8,128)(2,1)S(1)}, bf16[256,256]{1,0:T(8,128)(2,1)}, u32[]{:S(2)}) copy-start(bf16[256,256]{1,0:T(8,128)(2,1)} %constant.30.order_ref.restore_ref) | copy-start | bytes 393220
  0.6 52.7 %copy-start.5 = (bf16[128,256]{1,0:T(8,128)(2,1)S(1)}, bf16[128,256]{1,0:T(8,128)(2,1)}, u32[]{:S(2)}) copy-start(bf16[128,256]{1,0:T(8,128)(2,1)} %constant.31.table_ref) | copy-start | bytes 196612
  0.7 78.3 %copy-start.7 = (bf16[128,128]{1,0:T(8,128)(2,1)S(1)}, bf16[128,128]{1,0:T(8,128)(2,1)}, u32[]{:S(2)}) copy-start(bf16[128,128]{1,0:T(8,128)(2,1)} %constant.32.rest_1_.order_ref) | copy-start | bytes 98308
  0.7 78.2 %copy-start.4 = (bf16[256,128]{1,0:T(8,128)(2,1)S(1)}, bf16[256,128]{1,0:T(8,128)(2,1)}, u32[]{:S(2)}) copy-start(bf16[256,128]{1,0:T(8,128)(2,1)} %constant.33.rest_2_.rows_ref) | copy-start | bytes 196612
  0.7 52.6 %copy-start.6 = (bf16[128,256]{1,0:T(8,128)(2,1)S(1)}, bf16[128,256]{1,0:T(8,128)(2,1)}, u32[]{:S(2)}) copy-start(bf16[128,256]{1,0:T(8,128)(2,1)} %constant.35.back_ref) | copy-start | bytes 196612
  3.6 49.7 %copy-start.3 = (bf16[16,128,256]{2,1,0:T(8,128)(2,1)S(1)}, bf16[16,128,256]{2,1,0:T(8,128)(2,1)}, u32[]{:S(2)}) copy-start(bf16[16,128,256]{2,1,0:T(8,128)(2,1)} %get-tuple-element.32.field_ref) | copy-start | bytes 3145732
  3.7 92.0 %copy-start.12 = (bf16[64,64]{1,0:T(8,128)(2,1)S(1)}, bf16[64,64]{1,0:T(8,128)(2,1)}, u32[]{:S(2)}) copy-start(bf16[64,64]{1,0:T(8,128)(2,1)} %param.15) | copy-start | bytes 24580
  35.5 17.8 %all-to-all-start.1 = ((bf16[8,32,1024]{2,1,0:T(8,128)(2,1)}), bf16[8,32,1024]{2,1,0:T(8,128)(2,1)S(1)}, u32[]{:S(2)}, u32[]{:S(2)}) async-start(bf16[8,32,1024]{2,1,0:T(8,128)(2,1)} %bitcast.30), calls=%async_computation.1 | async-start | bytes 1048576 | tf_op jit(solution)/shard_map/all_to_all | solution.py:512
  39.1 7.6 %collective-permute-start.1 = (bf16[1024,128]{1,0:T(8,128)(2,1)}, bf16[1024,128]{1,0:T(8,128)(2,1)S(1)}, u32[]{:S(2)}, u32[]{:S(2)}) collective-permute-start(bf16[1024,128]{1,0:T(8,128)(2,1)} %get-tuple-element.44.refs_0_), channel_id=1, source_target_pairs={{0,16},{8,24},{16,0},{24,8},{1,17},{9,25},{17,1},{25,9},{2,18},{10... | collective-permute-start | bytes 786440 | tf_op jit(solution)/shard_map/ppermute | solution.py:457
  40.7 20.2 %collective-permute-start = (bf16[1024,128]{1,0:T(8,128)(2,1)}, bf16[1024,128]{1,0:T(8,128)(2,1)}, u32[]{:S(2)}, u32[]{:S(2)}) collective-permute-start(bf16[1024,128]{1,0:T(8,128)(2,1)} %get-tuple-element.44.refs_0_), channel_id=1, source_target_pairs={{0,8},{8,0},{16,24},{24,16},{1,9},{9,1},{17,25},{25,17},{2,10},{10... | collective-permute-start | bytes 786440 | tf_op jit(solution)/shard_map/ppermute | solution.py:457
  46.7 49.0 %copy-start.8 = (bf16[1024,128]{1,0:T(8,128)(2,1)}, bf16[1024,128]{1,0:T(8,128)(2,1)S(1)}, u32[]{:S(2)}) copy-start(bf16[1024,128]{1,0:T(8,128)(2,1)S(1)} %collective-permute-done.1.refs_2_) | copy-start | bytes 786436
  46.7 14.1 %collective-permute-start.2 = (bf16[1024,128]{1,0:T(8,128)(2,1)S(1)}, bf16[1024,128]{1,0:T(8,128)(2,1)}, u32[]{:S(2)}, u32[]{:S(2)}) collective-permute-start(bf16[1024,128]{1,0:T(8,128)(2,1)S(1)} %collective-permute-done.1.refs_2_), channel_id=1, source_target_pairs={{0,8},{8,0},{16,24},{24,16},{1,9},{9,1},{17,25},{25,17},{2,10},{10... | collective-permute-start | bytes 786440 | tf_op jit(solution)/shard_map/ppermute | solution.py:457
  53.3 1.2 %copy-start = (bf16[16,128,256]{2,1,0:T(8,128)(2,1)S(1)}, bf16[16,128,256]{2,1,0:T(8,128)(2,1)}, u32[]{:S(2)}) copy-start(bf16[16,128,256]{2,1,0:T(8,128)(2,1)} %relayout.1.cot_ref) | copy-start | bytes 3145732
  60.8 18.1 %all-to-all-start.2 = ((bf16[8,16,2048]{2,1,0:T(8,128)(2,1)}), bf16[8,16,2048]{2,1,0:T(8,128)(2,1)S(1)}, u32[]{:S(2)}, u32[]{:S(2)}) async-start(bf16[8,16,2048]{2,1,0:T(8,128)(2,1)} %bitcast.8), calls=%async_computation.2 | async-start | bytes 1048576 | tf_op jit(solution)/shard_map/all_to_all | solution.py:512
  64.5 1.2 %collective-permute-start.3 = (f32[64,64]{1,0:T(8,128)S(1)}, f32[64,64]{1,0:T(8,128)S(1)}, u32[]{:S(2)}, u32[]{:S(2)}) collective-permute-start(f32[64,64]{1,0:T(8,128)S(1)} %get-tuple-element.36), channel_id=1, source_target_pairs={{0,8},{8,0},{16,24},{24,16},{1,9},{9,1},{17,25},{25,17},{2,10},{10... | collective-permute-start | bytes 49160 | tf_op jit(solution)/shard_map/ppermute | solution.py:457
  65.7 3.9 %collective-permute-start.4 = (f32[64,64]{1,0:T(8,128)S(1)}, f32[64,64]{1,0:T(8,128)S(1)}, u32[]{:S(2)}, u32[]{:S(2)}) collective-permute-start(f32[64,64]{1,0:T(8,128)S(1)} %add.14), channel_id=1, source_target_pairs={{0,16},{8,24},{16,0},{24,8},{1,17},{9,25},{17,1},{25,9},{2,18},{10... | collective-permute-start | bytes 49160 | tf_op jit(solution)/shard_map/ppermute | solution.py:457
  79.5 1.7 %copy-start.2 = (bf16[1024,128]{1,0:T(8,128)(2,1)}, bf16[1024,128]{1,0:T(8,128)(2,1)S(1)}, u32[]{:S(2)}) copy-start(bf16[1024,128]{1,0:T(8,128)(2,1)S(1)} %grad_spectra.1.rest_0_.refs_4_) | copy-start | bytes 786436
  79.5 10.8 %collective-permute-start.5 = (bf16[1024,128]{1,0:T(8,128)(2,1)S(1)}, bf16[1024,128]{1,0:T(8,128)(2,1)S(1)}, u32[]{:S(2)}, u32[]{:S(2)}) collective-permute-start(bf16[1024,128]{1,0:T(8,128)(2,1)S(1)} %grad_spectra.1.rest_0_.refs_4_), channel_id=1, source_target_pairs={{0,8},{8,0},{16,24},{24,16},{1,9},{9,1},{17,25},{25,17},{2,10},{10... | collective-permute-start | bytes 786440 | tf_op jit(solution)/shard_map/ppermute | solution.py:457
  79.6 10.8 %collective-permute-start.6 = (bf16[1024,128]{1,0:T(8,128)(2,1)S(1)}, bf16[1024,128]{1,0:T(8,128)(2,1)S(1)}, u32[]{:S(2)}, u32[]{:S(2)}) collective-permute-start(bf16[1024,128]{1,0:T(8,128)(2,1)S(1)} %grad_spectra.1.rest_0_.refs_4_), channel_id=1, source_target_pairs={{0,16},{8,24},{16,0},{24,8},{1,17},{9,25},{17,1},{25,9},{2,18},{10... | collective-permute-start | bytes 786440 | tf_op jit(solution)/shard_map/ppermute | solution.py:457
  90.4 5.4 %copy-start.9 = (bf16[1024,128]{1,0:T(8,128)(2,1)}, bf16[1024,128]{1,0:T(8,128)(2,1)S(1)}, u32[]{:S(2)}) copy-start(bf16[1024,128]{1,0:T(8,128)(2,1)S(1)} %collective-permute-done.5.refs_5_) | copy-start | bytes 786436
  90.4 5.3 %copy-start.10 = (bf16[1024,128]{1,0:T(8,128)(2,1)}, bf16[1024,128]{1,0:T(8,128)(2,1)S(1)}, u32[]{:S(2)}) copy-start(bf16[1024,128]{1,0:T(8,128)(2,1)S(1)} %collective-permute-done.6.refs_6_) | copy-start | bytes 786436
  90.4 1.6 %collective-permute-start.7 = (bf16[1024,128]{1,0:T(8,128)(2,1)S(1)}, bf16[1024,128]{1,0:T(8,128)(2,1)S(1)}, u32[]{:S(2)}, u32[]{:S(2)}) collective-permute-start(bf16[1024,128]{1,0:T(8,128)(2,1)S(1)} %collective-permute-done.6.refs_6_), channel_id=1, source_target_pairs={{0,8},{8,0},{16,24},{24,16},{1,9},{9,1},{17,25},{25,17},{2,10},{10... | collective-permute-start | bytes 786440 | tf_op jit(solution)/shard_map/ppermute | solution.py:457
  92.0 3.7 %copy-start.11 = (bf16[1024,128]{1,0:T(8,128)(2,1)}, bf16[1024,128]{1,0:T(8,128)(2,1)S(1)}, u32[]{:S(2)}) copy-start(bf16[1024,128]{1,0:T(8,128)(2,1)S(1)} %collective-permute-done.7.refs_7_) | copy-start | bytes 786436
  92.0 20.2 %all-to-all-start.3 = ((bf16[8,32,1152]{2,1,0:T(8,128)(2,1)}), bf16[8,32,1152]{2,1,0:T(8,128)(2,1)S(1)}, u32[]{:S(2)}, u32[]{:S(2)}) async-start(bf16[8,32,1152]{2,1,0:T(8,128)(2,1)} %bitcast.28), calls=%async_computation.3 | async-start | bytes 1179648 | tf_op jit(solution)/shard_map/all_to_all | solution.py:512

commit v7 on v6

--- a/solution.py
+++ b/solution.py
@@ -570,7 +570,7 @@
     )
     all_spectra = gather_far(gather_near(spectra, "dp"), "dp")
     arrived = exchange(send)
-    steps = 8
+    steps = th
     row_block = pl.BlockSpec((steps, lanes, width), lambda n: (n, 0, 0))
     gate_rows, send, local_sum = call(
         functools.partial(pixels_kernel, mode_scale, th),

time: 115 us -> 113 us (0.983)
  Pallas kernels: 50.2 us -> 47.8 us
    pallas_call x8, Pallas kernels: 50.2 us -> 47.8 us  [call(): pl.pallas_call(kernel, out_shape=tuple(outs), grid=grid, in_specs=in_spec...]
  transfers between devices with their start and end apart: 11 -> 11, of which waited for: 6 -> 6; matrix products, arithmetic and copies ran while one was open for 1% -> 1% of each run, Pallas kernels for 30% -> 29%
where the time goes in v7:
time: 113 us; the launch traced here: 112 us
  Pallas kernels  47.8 us (42%)
  waiting for transfers between devices  22.8 us (20%)
  blocking collectives  22 us (19%)
  starting transfers between devices  15.8 us (14%)
  local copies, waits for them, and re-layouts  2.08 us (2%)
    pallas_call x8, Pallas kernels, call(): pl.pallas_call(kernel, out_shape=tuple(outs), grid=grid, in_specs=in_spec...  47.8 us
    all_to_all x1, blocking collectives, exchange(): lax.all_to_all(split, 'tile', split_axis=0, concat_axis=0, tiled=False)  22 us
    all_to_all x3, waiting for transfers between devices, exchange(): lax.all_to_all(split, 'tile', split_axis=0, concat_axis=0, tiled=False)  11.7 us
    ppermute x8, waiting for transfers between devices, swap(): lax.ppermute(values, axis, [(i, i ^ step) for i in range(lax.axis_size(ax...  11.1 us
    all_to_all x3, starting transfers between devices, exchange(): lax.all_to_all(split, 'tile', split_axis=0, concat_axis=0, tiled=False)  10.9 us
    ppermute x8, starting transfers between devices, swap(): lax.ppermute(values, axis, [(i, i ^ step) for i in range(lax.axis_size(ax...  4.96 us
  transfers between devices with their start and end apart: 11, of which 6 were waited for; matrix products, arithmetic and copies ran while one was open for 1% of the time, Pallas kernels for 29%

profile of v7, /device:TPU:0, one launch (start us, length us, event | category | flops | bytes accessed | tf_op | source)
XLA Modules:
  0.0 112.1 jit_solution(17043565697902817844)
XLA Ops:
  0.6 0.0 copy-start.1
  0.6 0.0 copy-start.5
  0.7 0.0 copy-start.7
  0.7 0.0 copy-start.4
  0.7 0.0 copy-start.6
  0.7 3.0 %columns.1 = (bf16[16,128,256]{2,1,0:T(8,128)(2,1)}, bf16[128,2048]{1,0:T(8,128)(2,1)}) custom-call(bf16[256,256]{1,0:T(8,128)(2,1)} %constant.30.order_ref.restore_ref, bf16[128,256]{1,0:T(8,128)(2,1)} %constant.31.table_ref, bf16[2048,256]{1,0:T(8,128)(2,1)} %bitcast.20, bf16[2048,256]{1,0:T(8,128)(2,1)} %bitcast.21, bf16[2048,256]{1,0:T(8,128)(2,1)} %bitcast.22, ...), custom_call_target="tpu_custom_call" | custom-call | tf_op jit(solution)/shard_map/columns/pallas_call | solution.py:444
  3.7 22.0 %all_to_all.20 = bf16[8,16,2048]{2,1,0:T(8,128)(2,1)} all-to-all(bf16[8,16,2048]{2,1,0:T(8,128)(2,1)} %bitcast.31), channel_id=1, replica_groups=mesh['dp'=4,'tile'=8] {'tile'}, dimensions={0} | all-to-all | bytes 1048576 | tf_op jit(solution)/shard_map/all_to_all | solution.py:512
  25.7 9.8 %mix_forward.1 = (bf16[1024,128]{1,0:T(8,128)(2,1)}, bf16[256,1024]{1,0:T(8,128)(2,1)}) custom-call(bf16[128,2048]{1,0:T(8,128)(2,1)} %bitcast.29, bf16[128,128]{1,0:T(8,128)(2,1)} %constant.32.rest_1_.order_ref, bf16[256,128]{1,0:T(8,128)(2,1)} %constant.33.rest_2_.rows_ref, bf16[256,128]{1,0:T(8,128)(2,1)} %constant.34.rest_3_.rest_1_, ...), custom_call_target="tpu_custom_call" | custom-call | tf_op jit(solution)/shard_map/mix_forward/pallas_call | solution.py:444
  35.5 3.6 %all-to-all-start.1 = ((bf16[8,32,1024]{2,1,0:T(8,128)(2,1)}), bf16[8,32,1024]{2,1,0:T(8,128)(2,1)S(1)}, u32[]{:S(2)}, u32[]{:S(2)}) async-start(bf16[8,32,1024]{2,1,0:T(8,128)(2,1)} %bitcast.30), calls=%async_computation.1 | async-start | bytes 1048576 | tf_op jit(solution)/shard_map/all_to_all | solution.py:512
  39.1 1.5 %collective-permute-start.1 = (bf16[1024,128]{1,0:T(8,128)(2,1)}, bf16[1024,128]{1,0:T(8,128)(2,1)S(1)}, u32[]{:S(2)}, u32[]{:S(2)}) collective-permute-start(bf16[1024,128]{1,0:T(8,128)(2,1)} %get-tuple-element.44.refs_0_), channel_id=1, source_target_pairs={{0,16},{8,24},{16,0},{24,8},{1,17},{9,25},{17,1},{25,9},{2,18},{10... | collective-permute-start | bytes 786440 | tf_op jit(solution)/shard_map/ppermute | solution.py:457
  40.7 0.0 collective-permute-start
  40.7 6.1 %collective-permute-done.1.refs_2_ = bf16[1024,128]{1,0:T(8,128)(2,1)S(1)} collective-permute-done((bf16[1024,128]{1,0:T(8,128)(2,1)}, bf16[1024,128]{1,0:T(8,128)(2,1)S(1)}, u32[]{:S(2)}, u32[]{:S(2)}) %collective-permute-start.1) | collective-permute-done | bytes 262176 | tf_op jit(solution)/shard_map/ppermute | solution.py:457
  46.7 0.0 collective-permute-start.2
  46.7 0.8 copy.15
  47.5 2.6 %relayout.1.cot_ref = bf16[16,128,256]{2,1,0:T(8,128)(2,1)} custom-call(bf16[256,256]{1,0:T(8,128)(2,1)} %constant.30.order_ref.restore_ref, bf16[2048,256]{1,0:T(8,128)(2,1)} %bitcast.24, bf16[2048,256]{1,0:T(8,128)(2,1)} %bitcast.25, bf16[2048,256]{1,0:T(8,128)(2,1)} %bitcast.26, bf16[2048,256]{1,0:T(8,128)(2,1)} %bitcast.27), custom_call_target="tpu_custom_call" | custom-call | tf_op jit(solution)/shard_map/relayout/pallas_call | solution.py:444
  50.2 0.1 fusion.4.local_ref
  50.3 3.0 %all-to-all-done.1 = bf16[8,32,1024]{2,1,0:T(8,128)(2,1)S(1)} async-done(((bf16[8,32,1024]{2,1,0:T(8,128)(2,1)}), bf16[8,32,1024]{2,1,0:T(8,128)(2,1)S(1)}, u32[]{:S(2)}, u32[]{:S(2)}) %all-to-all-start.1) | async-done | bytes 524320 | tf_op jit(solution)/shard_map/all_to_all | solution.py:512
  53.3 0.0 copy-start
  53.3 1.2 %copy-done = bf16[16,128,256]{2,1,0:T(8,128)(2,1)S(1)} copy-done((bf16[16,128,256]{2,1,0:T(8,128)(2,1)S(1)}, bf16[16,128,256]{2,1,0:T(8,128)(2,1)}, u32[]{:S(2)}) %copy-start) | copy-done | bytes 1048600
  54.5 3.9 %pixels.1 = (bf16[16,128,256]{2,1,0:T(8,128)(2,1)S(1)}, bf16[128,2048]{1,0:T(8,128)(2,1)}, f32[64,64]{1,0:T(8,128)S(1)}) custom-call(bf16[256,1024]{1,0:T(8,128)(2,1)S(1)} %bitcast.16, bf16[256,256]{1,0:T(8,128)(2,1)S(1)} %copy-done.1, bf16[128,256]{1,0:T(8,128)(2,1)S(1)} %copy-done.6, bf16[128,128]{1,0:T(8,128)(2,1)S(1)} %fusion.4.local_ref, ...), custom_call_target="tpu_custom_call" | custom-call | tf_op jit(solution)/shard_map/pixels/pallas_call | solution.py:444
  58.4 0.0 collective-permute-done.refs_1_
  58.4 0.0 collective-permute-done.2.refs_3_
  58.4 3.6 %all-to-all-start.2 = ((bf16[8,16,2048]{2,1,0:T(8,128)(2,1)}), bf16[8,16,2048]{2,1,0:T(8,128)(2,1)S(1)}, u32[]{:S(2)}, u32[]{:S(2)}) async-start(bf16[8,16,2048]{2,1,0:T(8,128)(2,1)} %bitcast.8), calls=%async_computation.2 | async-start | bytes 1048576 | tf_op jit(solution)/shard_map/all_to_all | solution.py:512
  62.0 0.0 collective-permute-start.3
  62.1 1.2 %collective-permute-done.3 = f32[64,64]{1,0:T(8,128)S(1)} collective-permute-done((f32[64,64]{1,0:T(8,128)S(1)}, f32[64,64]{1,0:T(8,128)S(1)}, u32[]{:S(2)}, u32[]{:S(2)}) %collective-permute-start.3) | collective-permute-done | bytes 16416 | tf_op jit(solution)/shard_map/ppermute | solution.py:457
  63.3 1.5 %collective-permute-start.4 = (f32[64,64]{1,0:T(8,128)S(1)}, f32[64,64]{1,0:T(8,128)S(1)}, u32[]{:S(2)}, u32[]{:S(2)}) collective-permute-start(f32[64,64]{1,0:T(8,128)S(1)} %add.14), channel_id=1, source_target_pairs={{0,16},{8,24},{16,0},{24,8},{1,17},{9,25},{17,1},{25,9},{2,18},{10... | collective-permute-start | bytes 49160 | tf_op jit(solution)/shard_map/ppermute | solution.py:457
  64.8 2.4 %collective-permute-done.4 = f32[64,64]{1,0:T(8,128)S(1)} collective-permute-done((f32[64,64]{1,0:T(8,128)S(1)}, f32[64,64]{1,0:T(8,128)S(1)}, u32[]{:S(2)}, u32[]{:S(2)}) %collective-permute-start.4) | collective-permute-done | bytes 16416 | tf_op jit(solution)/shard_map/ppermute | solution.py:457
  67.2 0.6 add.15.rest_2_
  67.8 8.7 %all-to-all-done.2 = bf16[8,16,2048]{2,1,0:T(8,128)(2,1)S(1)} async-done(((bf16[8,16,2048]{2,1,0:T(8,128)(2,1)}), bf16[8,16,2048]{2,1,0:T(8,128)(2,1)S(1)}, u32[]{:S(2)}, u32[]{:S(2)}) %all-to-all-start.2) | async-done | bytes 524320 | tf_op jit(solution)/shard_map/all_to_all | solution.py:512
  76.5 0.0 copy-done.4
  76.5 0.6 grad_spectra.1.rest_0_.refs_4_
  77.1 0.0 copy-start.2
  77.1 0.1 collective-permute-start.5
  77.2 1.6 %collective-permute-start.6 = (bf16[1024,128]{1,0:T(8,128)(2,1)S(1)}, bf16[1024,128]{1,0:T(8,128)(2,1)S(1)}, u32[]{:S(2)}, u32[]{:S(2)}) collective-permute-start(bf16[1024,128]{1,0:T(8,128)(2,1)S(1)} %grad_spectra.1.rest_0_.refs_4_), channel_id=1, source_target_pairs={{0,16},{8,24},{16,0},{24,8},{1,17},{9,25},{17,1},{25,9},{2,18},{10... | collective-permute-start | bytes 786440 | tf_op jit(solution)/shard_map/ppermute | solution.py:457
  78.8 0.0 copy-done.2
  78.8 9.2 %mix_backward.1 = bf16[256,1152]{1,0:T(8,128)(2,1)} custom-call(bf16[1024,128]{1,0:T(8,128)(2,1)} %copy-done.2, bf16[256,128]{1,0:T(8,128)(2,1)} %constant.34.rest_3_.rest_1_, f32[64,64]{1,0:T(8,128)} %add.15.rest_2_, bf16[32768,128]{1,0:T(8,128)(2,1)} %bitcast.18), custom_call_target="tpu_custom_call" | custom-call | tf_op jit(solution)/shard_map/mix_backward/pallas_call | solution.py:444
  87.9 0.0 collective-permute-done.5.refs_5_
  88.0 0.0 collective-permute-done.6.refs_6_
  88.0 0.2 collective-permute-start.7
  88.2 1.4 %collective-permute-done.7.refs_7_ = bf16[1024,128]{1,0:T(8,128)(2,1)S(1)} collective-permute-done((bf16[1024,128]{1,0:T(8,128)(2,1)S(1)}, bf16[1024,128]{1,0:T(8,128)(2,1)S(1)}, u32[]{:S(2)}, u32[]{:S(2)}) %collective-permute-start.7) | collective-permute-done | bytes 262176 | tf_op jit(solution)/shard_map/ppermute | solution.py:457
  89.6 3.6 %all-to-all-start.3 = ((bf16[8,32,1152]{2,1,0:T(8,128)(2,1)}), bf16[8,32,1152]{2,1,0:T(8,128)(2,1)S(1)}, u32[]{:S(2)}, u32[]{:S(2)}) async-start(bf16[8,32,1152]{2,1,0:T(8,128)(2,1)} %bitcast.28), calls=%async_computation.3 | async-start | bytes 1179648 | tf_op jit(solution)/shard_map/all_to_all | solution.py:512
  93.2 0.0 copy-done.12
  93.2 0.1 fusion.5.local_ref
  93.3 0.0 copy-done.9
  93.3 0.0 copy-done.10
  93.3 16.4 %mode_grad.1 = f32[32768,128]{1,0:T(8,128)} custom-call(bf16[1024,128]{1,0:T(8,128)(2,1)} %get-tuple-element.44.refs_0_, bf16[1024,128]{1,0:T(8,128)(2,1)} %collective-permute-done.refs_1_, bf16[1024,128]{1,0:T(8,128)(2,1)} %copy-done.8, bf16[1024,128]{1,0:T(8,128)(2,1)} %collective-permute-done.2.refs_3_, bf16[1024,128]{1,0:T(8,128)(2,1)} %copy-done.2, ...), custom_call_target="tpu_custom_call" | custom-call | tf_op jit(solution)/shard_map/mode_grad/pallas_call | solution.py:444
  109.7 0.0 all-to-all-done.3
  109.7 2.3 %final.1 = (bf16[2048,256]{1,0:T(8,128)(2,1)}, f32[64,64]{1,0:T(8,128)}) custom-call(bf16[256,1152]{1,0:T(8,128)(2,1)S(1)} %bitcast.14, bf16[256,256]{1,0:T(8,128)(2,1)S(1)} %copy-done.1, bf16[128,256]{1,0:T(8,128)(2,1)S(1)} %copy-done.6, bf16[128,128]{1,0:T(8,128)(2,1)S(1)} %fusion.5.local_ref, bf16[16,128,256]{2,1,0:T(8,128)(2,1)S(1)} %get-tuple-element.53.grad_ref, ...), custom_call_target="tpu_custom_call" | custom-call | tf_op jit(solution)/shard_map/final/pallas_call | solution.py:444
  (14 shorter events, 0.0 us)
Async XLA Ops:
  0.6 52.7 %copy-start.1 = (bf16[256,256]{1,0:T(8,128)(2,1)S(1)}, bf16[256,256]{1,0:T(8,128)(2,1)}, u32[]{:S(2)}) copy-start(bf16[256,256]{1,0:T(8,128)(2,1)} %constant.30.order_ref.restore_ref) | copy-start | bytes 393220
  0.6 52.7 %copy-start.5 = (bf16[128,256]{1,0:T(8,128)(2,1)S(1)}, bf16[128,256]{1,0:T(8,128)(2,1)}, u32[]{:S(2)}) copy-start(bf16[128,256]{1,0:T(8,128)(2,1)} %constant.31.table_ref) | copy-start | bytes 196612
  0.7 75.8 %copy-start.7 = (bf16[128,128]{1,0:T(8,128)(2,1)S(1)}, bf16[128,128]{1,0:T(8,128)(2,1)}, u32[]{:S(2)}) copy-start(bf16[128,128]{1,0:T(8,128)(2,1)} %constant.32.rest_1_.order_ref) | copy-start | bytes 98308
  0.7 75.8 %copy-start.4 = (bf16[256,128]{1,0:T(8,128)(2,1)S(1)}, bf16[256,128]{1,0:T(8,128)(2,1)}, u32[]{:S(2)}) copy-start(bf16[256,128]{1,0:T(8,128)(2,1)} %constant.33.rest_2_.rows_ref) | copy-start | bytes 196612
  0.7 52.6 %copy-start.6 = (bf16[128,256]{1,0:T(8,128)(2,1)S(1)}, bf16[128,256]{1,0:T(8,128)(2,1)}, u32[]{:S(2)}) copy-start(bf16[128,256]{1,0:T(8,128)(2,1)} %constant.35.back_ref) | copy-start | bytes 196612
  3.6 49.7 %copy-start.3 = (bf16[16,128,256]{2,1,0:T(8,128)(2,1)S(1)}, bf16[16,128,256]{2,1,0:T(8,128)(2,1)}, u32[]{:S(2)}) copy-start(bf16[16,128,256]{2,1,0:T(8,128)(2,1)} %get-tuple-element.32.field_ref) | copy-start | bytes 3145732
  3.7 89.6 %copy-start.12 = (bf16[64,64]{1,0:T(8,128)(2,1)S(1)}, bf16[64,64]{1,0:T(8,128)(2,1)}, u32[]{:S(2)}) copy-start(bf16[64,64]{1,0:T(8,128)(2,1)} %param.15) | copy-start | bytes 24580
  35.5 17.8 %all-to-all-start.1 = ((bf16[8,32,1024]{2,1,0:T(8,128)(2,1)}), bf16[8,32,1024]{2,1,0:T(8,128)(2,1)S(1)}, u32[]{:S(2)}, u32[]{:S(2)}) async-start(bf16[8,32,1024]{2,1,0:T(8,128)(2,1)} %bitcast.30), calls=%async_computation.1 | async-start | bytes 1048576 | tf_op jit(solution)/shard_map/all_to_all | solution.py:512
  39.1 7.6 %collective-permute-start.1 = (bf16[1024,128]{1,0:T(8,128)(2,1)}, bf16[1024,128]{1,0:T(8,128)(2,1)S(1)}, u32[]{:S(2)}, u32[]{:S(2)}) collective-permute-start(bf16[1024,128]{1,0:T(8,128)(2,1)} %get-tuple-element.44.refs_0_), channel_id=1, source_target_pairs={{0,16},{8,24},{16,0},{24,8},{1,17},{9,25},{17,1},{25,9},{2,18},{10... | collective-permute-start | bytes 786440 | tf_op jit(solution)/shard_map/ppermute | solution.py:457
  40.7 17.7 %collective-permute-start = (bf16[1024,128]{1,0:T(8,128)(2,1)}, bf16[1024,128]{1,0:T(8,128)(2,1)}, u32[]{:S(2)}, u32[]{:S(2)}) collective-permute-start(bf16[1024,128]{1,0:T(8,128)(2,1)} %get-tuple-element.44.refs_0_), channel_id=1, source_target_pairs={{0,8},{8,0},{16,24},{24,16},{1,9},{9,1},{17,25},{25,17},{2,10},{10... | collective-permute-start | bytes 786440 | tf_op jit(solution)/shard_map/ppermute | solution.py:457
  46.7 46.6 %copy-start.8 = (bf16[1024,128]{1,0:T(8,128)(2,1)}, bf16[1024,128]{1,0:T(8,128)(2,1)S(1)}, u32[]{:S(2)}) copy-start(bf16[1024,128]{1,0:T(8,128)(2,1)S(1)} %collective-permute-done.1.refs_2_) | copy-start | bytes 786436
  46.7 11.7 %collective-permute-start.2 = (bf16[1024,128]{1,0:T(8,128)(2,1)S(1)}, bf16[1024,128]{1,0:T(8,128)(2,1)}, u32[]{:S(2)}, u32[]{:S(2)}) collective-permute-start(bf16[1024,128]{1,0:T(8,128)(2,1)S(1)} %collective-permute-done.1.refs_2_), channel_id=1, source_target_pairs={{0,8},{8,0},{16,24},{24,16},{1,9},{9,1},{17,25},{25,17},{2,10},{10... | collective-permute-start | bytes 786440 | tf_op jit(solution)/shard_map/ppermute | solution.py:457
  53.3 1.2 %copy-start = (bf16[16,128,256]{2,1,0:T(8,128)(2,1)S(1)}, bf16[16,128,256]{2,1,0:T(8,128)(2,1)}, u32[]{:S(2)}) copy-start(bf16[16,128,256]{2,1,0:T(8,128)(2,1)} %relayout.1.cot_ref) | copy-start | bytes 3145732
  58.4 18.1 %all-to-all-start.2 = ((bf16[8,16,2048]{2,1,0:T(8,128)(2,1)}), bf16[8,16,2048]{2,1,0:T(8,128)(2,1)S(1)}, u32[]{:S(2)}, u32[]{:S(2)}) async-start(bf16[8,16,2048]{2,1,0:T(8,128)(2,1)} %bitcast.8), calls=%async_computation.2 | async-start | bytes 1048576 | tf_op jit(solution)/shard_map/all_to_all | solution.py:512
  62.0 1.2 %collective-permute-start.3 = (f32[64,64]{1,0:T(8,128)S(1)}, f32[64,64]{1,0:T(8,128)S(1)}, u32[]{:S(2)}, u32[]{:S(2)}) collective-permute-start(f32[64,64]{1,0:T(8,128)S(1)} %get-tuple-element.36), channel_id=1, source_target_pairs={{0,8},{8,0},{16,24},{24,16},{1,9},{9,1},{17,25},{25,17},{2,10},{10... | collective-permute-start | bytes 49160 | tf_op jit(solution)/shard_map/ppermute | solution.py:457
  63.3 3.9 %collective-permute-start.4 = (f32[64,64]{1,0:T(8,128)S(1)}, f32[64,64]{1,0:T(8,128)S(1)}, u32[]{:S(2)}, u32[]{:S(2)}) collective-permute-start(f32[64,64]{1,0:T(8,128)S(1)} %add.14), channel_id=1, source_target_pairs={{0,16},{8,24},{16,0},{24,8},{1,17},{9,25},{17,1},{25,9},{2,18},{10... | collective-permute-start | bytes 49160 | tf_op jit(solution)/shard_map/ppermute | solution.py:457
  77.1 1.7 %copy-start.2 = (bf16[1024,128]{1,0:T(8,128)(2,1)}, bf16[1024,128]{1,0:T(8,128)(2,1)S(1)}, u32[]{:S(2)}) copy-start(bf16[1024,128]{1,0:T(8,128)(2,1)S(1)} %grad_spectra.1.rest_0_.refs_4_) | copy-start | bytes 786436
  77.1 10.8 %collective-permute-start.5 = (bf16[1024,128]{1,0:T(8,128)(2,1)S(1)}, bf16[1024,128]{1,0:T(8,128)(2,1)S(1)}, u32[]{:S(2)}, u32[]{:S(2)}) collective-permute-start(bf16[1024,128]{1,0:T(8,128)(2,1)S(1)} %grad_spectra.1.rest_0_.refs_4_), channel_id=1, source_target_pairs={{0,8},{8,0},{16,24},{24,16},{1,9},{9,1},{17,25},{25,17},{2,10},{10... | collective-permute-start | bytes 786440 | tf_op jit(solution)/shard_map/ppermute | solution.py:457
  77.2 10.8 %collective-permute-start.6 = (bf16[1024,128]{1,0:T(8,128)(2,1)S(1)}, bf16[1024,128]{1,0:T(8,128)(2,1)S(1)}, u32[]{:S(2)}, u32[]{:S(2)}) collective-permute-start(bf16[1024,128]{1,0:T(8,128)(2,1)S(1)} %grad_spectra.1.rest_0_.refs_4_), channel_id=1, source_target_pairs={{0,16},{8,24},{16,0},{24,8},{1,17},{9,25},{17,1},{25,9},{2,18},{10... | collective-permute-start | bytes 786440 | tf_op jit(solution)/shard_map/ppermute | solution.py:457
  88.0 5.4 %copy-start.9 = (bf16[1024,128]{1,0:T(8,128)(2,1)}, bf16[1024,128]{1,0:T(8,128)(2,1)S(1)}, u32[]{:S(2)}) copy-start(bf16[1024,128]{1,0:T(8,128)(2,1)S(1)} %collective-permute-done.5.refs_5_) | copy-start | bytes 786436
  88.0 5.3 %copy-start.10 = (bf16[1024,128]{1,0:T(8,128)(2,1)}, bf16[1024,128]{1,0:T(8,128)(2,1)S(1)}, u32[]{:S(2)}) copy-start(bf16[1024,128]{1,0:T(8,128)(2,1)S(1)} %collective-permute-done.6.refs_6_) | copy-start | bytes 786436
  88.0 1.6 %collective-permute-start.7 = (bf16[1024,128]{1,0:T(8,128)(2,1)S(1)}, bf16[1024,128]{1,0:T(8,128)(2,1)S(1)}, u32[]{:S(2)}, u32[]{:S(2)}) collective-permute-start(bf16[1024,128]{1,0:T(8,128)(2,1)S(1)} %collective-permute-done.6.refs_6_), channel_id=1, source_target_pairs={{0,8},{8,0},{16,24},{24,16},{1,9},{9,1},{17,25},{25,17},{2,10},{10... | collective-permute-start | bytes 786440 | tf_op jit(solution)/shard_map/ppermute | solution.py:457
  89.6 3.7 %copy-start.11 = (bf16[1024,128]{1,0:T(8,128)(2,1)}, bf16[1024,128]{1,0:T(8,128)(2,1)S(1)}, u32[]{:S(2)}) copy-start(bf16[1024,128]{1,0:T(8,128)(2,1)S(1)} %collective-permute-done.7.refs_7_) | copy-start | bytes 786436
  89.6 20.2 %all-to-all-start.3 = ((bf16[8,32,1152]{2,1,0:T(8,128)(2,1)}), bf16[8,32,1152]{2,1,0:T(8,128)(2,1)S(1)}, u32[]{:S(2)}, u32[]{:S(2)}) async-start(bf16[8,32,1152]{2,1,0:T(8,128)(2,1)} %bitcast.28), calls=%async_computation.3 | async-start | bytes 1179648 | tf_op jit(solution)/shard_map/all_to_all | solution.py:512
